TPU v7x, 256 devices: a whole 4x4x8 slice. The times are simulated.
256 devices in a mesh: depth: 64 (over y, z, core), space: 4 (over x).
Axes of the slice: x: 4, y: 4, z: 8, core: 2. Of those that a mesh axis runs over, the one named last changes fastest.
Arguments:
- coarse_states: float32 [64, 32, 128, 128], P('depth', 'space'), may hold values from -6 to 6
- first_kernels: bfloat16 [256, 9, 128, 128], P('depth'), may hold values from -0.1875 to 0.1875
- second_kernels: bfloat16 [256, 9, 128, 128], P('depth'), may hold values from -0.1875 to 0.1875
- coarse_channel_gain: float32 [64, 128], replicated, may hold values from 0 to 1, as said below
Outputs:
- states: float32 [256, 32, 128, 128], P('depth', 'space')
- relaxed: float32 [64, 32, 128, 128], P('depth', 'space')
Inputs may be any that keep to these rules, and one draw needn't show every extreme that they name: `coarse_channel_gain`: each entry is positive and at most 1.
All inputs are finite; a program needn't handle non-finite values.
Results may differ from a plain program's by a relative error of at most 0.01.
Values may be sent and summed in bfloat16 or wider, within the bound.
No kernel may reach another device: no remote copies, remote signals or barrier semaphores. Data moves between devices by JAX's collectives and lax.ppermute only.
A program may use at most 128 MiB of HBM per device.

v0:
```python
import jax
import jax.numpy as jnp
from jax import lax
from jax.sharding import PartitionSpec as P


def extended(cells, sides, width):
    for axis, dim in sides:
        count = lax.axis_size(axis)
        ends = count - 1
        head = lax.slice_in_dim(cells, 0, width, axis=dim)
        tail = lax.slice_in_dim(cells, cells.shape[dim] - width, cells.shape[dim], axis=dim)
        cells = jnp.concatenate(
            [
                lax.ppermute(tail, axis, [(i, (i + 1) % count) for i in range(ends)]),
                cells,
                lax.ppermute(head, axis, [((i + 1) % count, i) for i in range(ends)]),
            ],
            axis=dim,
        )
    return cells


def from_behind(block, axis, distance):
    devices = range(lax.axis_size(axis))
    route = [(i - distance, i) for i in devices if i - distance in devices]
    return lax.ppermute(block, axis, route)


def prefix(value, axis, join, neutral):
    count, mine = (lax.axis_size(axis), lax.axis_index(axis))
    pieces = jax.tree.map(lambda part: lax.all_gather(part, axis), value)
    running = jax.tree.map(
        lambda part, zero: jnp.full_like(part, 0) + jnp.asarray(zero, part.dtype), value, neutral
    )

    def step(position, running):
        longer = join(running, jax.tree.map(lambda part: part[position], pieces))
        return jax.tree.map(lambda new, old: jnp.where(position < mine, new, old), longer, running)

    return lax.fori_loop(0, count - 1, step, running)


def conv_taps(padded, kernel):
    rows = padded.shape[0] - 2
    cols = padded.shape[1]
    wide = jnp.pad(padded, ((0, 0), (1, 1), (0, 0)))
    parts = [wide[a : a + rows, b : b + cols, :] for a in range(3) for b in range(3)]
    stacked = jnp.concatenate(parts, axis=-1).reshape(rows * cols, -1)
    flat = kernel.reshape(-1, kernel.shape[-1])
    return jnp.dot(stacked, flat, preferred_element_type=jnp.float32).reshape(rows, cols, -1)


def boundary_rows(field):
    return extended(field, (("space", 0),), 1)


def layer_step(state, first, second_half):
    hidden = jnp.tanh(conv_taps(boundary_rows(state.astype(jnp.bfloat16)), first)).astype(
        jnp.bfloat16
    )
    outer = conv_taps(boundary_rows(hidden), second_half)
    return state + 0.5 * jnp.tanh(outer)


def affine_join(earlier, later):
    return (earlier[0] * later[0], later[0] * earlier[1] + later[1])


def shards(coarse_states, first_kernels, second_kernels, coarse_channel_gain):
    layers_here = first_kernels.shape[0]
    start = coarse_states[0]
    position = lax.axis_index("depth")
    count = lax.axis_size("depth")

    def propagate(state):
        for index in range(layers_here):
            state = layer_step(state, first_kernels[index], second_kernels[index])
        return state

    y_first = propagate(start)
    received = from_behind(y_first.astype(jnp.bfloat16), "depth", 1).astype(y_first.dtype)
    c_first = jnp.where(position == 0, start, received)
    y_second = propagate(c_first)
    interval_gain = lax.dynamic_index_in_dim(coarse_channel_gain, position, 0, keepdims=False)
    ones = jnp.ones_like(interval_gain)
    zeros = jnp.zeros_like(c_first)
    next_index = jnp.minimum(position + 1, count - 1)
    next_gain = lax.dynamic_index_in_dim(coarse_channel_gain, next_index, 0, keepdims=False)
    addend = jnp.where(position == 0, y_second, y_second - next_gain * c_first)
    _, carried = prefix((next_gain, addend), "depth", affine_join, (ones, zeros))
    c_second = jnp.where(position == 0, c_first, carried)
    listing = [c_second]
    state = c_second
    for index in range(layers_here - 1):
        state = layer_step(state, first_kernels[index], second_kernels[index])
        listing.append(state)
    return (jnp.stack(listing, axis=0), y_second[None])


def solution(mesh):
    placed = (
        P("depth", "space", None, None),
        P("depth", None, None, None),
        P("depth", None, None, None),
        P(),
    )
    return jax.shard_map(
        shards,
        mesh=mesh,
        in_specs=placed,
        out_specs=(P("depth", "space", None, None), P("depth", "space", None, None)),
        check_vma=False,
    )
```

profile of v0, /device:TPU:2, one launch (start us, length us, event | category | flops | bytes accessed | tf_op | source)
XLA Modules:
  0.0 489.0 jit_solution(1443827606276564113)
XLA Ops:
  8.3 3.4 collective-permute-start
  11.7 2.6 collective-permute-start.1
  15.7 2.0 collective-permute-done.1
  19.4 3.1 collective-permute-start.2
  22.5 2.7 collective-permute-start.3
  25.4 3.0 collective-permute-done.3
  30.0 1.9 collective-permute-start.4
  32.0 3.9 collective-permute-start.5
  39.5 1.9 collective-permute-start.6
  41.4 3.9 collective-permute-start.7
  48.9 1.9 collective-permute-start.8
  50.8 3.9 collective-permute-start.9
  58.4 1.9 collective-permute-start.10
  60.3 3.9 collective-permute-start.11
  67.8 1.9 collective-permute-start.12
  69.7 3.9 collective-permute-start.13
  73.8 1.9 collective-permute-done.13
  77.4 2.0 collective-permute-start.14
  79.4 4.1 collective-permute-start.15
  89.5 1.9 collective-permute-start.17
  91.4 3.9 collective-permute-start.18
  99.1 1.9 collective-permute-start.19
  101.0 3.9 collective-permute-start.20
  108.5 1.9 collective-permute-start.21
  110.4 3.9 collective-permute-start.22
  118.0 1.9 collective-permute-start.23
  119.9 3.9 collective-permute-start.24
  129.3 3.9 collective-permute-start.26
  138.8 3.9 collective-permute-start.28
  148.2 13.7 %collective-permute-start.30 = (bf16[1,128,128]{2,1,0:T(8,128)(2,1)S(1)}, bf16[1,128,128]{2,1,0:T(8,128)(2,1)S(1)}, u32[]{:S(2)}, u32[]{:S(2)}) collective-permute-start(bf16[1,128,128]{2,1,0:T(8,128)(2,1)S(1)} %get-tuple-element.150), channel_id=1, source_target_pairs={{1,0},{2,1},{3,2},{5,4},{6,5},{7,6},{9,8},{10,9},{11,10},{13,12},{... | collective-permute-start | bytes 98312 | tf_op jit(solution)/shard_map/ppermute | solution.py:17
  163.8 1.9 collective-permute-start.31
  165.7 3.9 collective-permute-start.32
  174.2 49.6 %all-gather.1 = f32[64,1,128]{2,1,0:T(1,128)S(1)} all-gather(f32[1,1,128]{2,1,0:T(1,128)S(1)} %get-tuple-element.180), channel_id=1, replica_groups=mesh['depth'=64,'space'=4] {'depth'}, dimensions={0}, use_global_device_ids=true | all-gather | bytes 33280 | tf_op jit(solution)/shard_map/all_gather | solution.py:32
  223.8 101.3 %all-gather.4.cloned.1.call-done = f32[512,128,128]{2,1,0:T(8,128)} async-done(((f32[8,128,128]{2,1,0:T(8,128)}), f32[512,128,128]{2,1,0:T(8,128)}) %all-gather.4.cloned.1.call-update) | async-done | bytes 33554448 | tf_op jit(solution)/shard_map/all_gather | solution.py:32
  325.1 95.6 %while.14 = (s32[]{:T(128)}, f32[8,128,128]{2,1,0:T(8,128)S(1)}, s32[]{:T(128)}, f32[64,128]{1,0:T(8,128)S(1)}, f32[64,8,128,128]{3,2,1,0:T(8,128)}, /*index=5*/s32[]{:T(128)}, s32[]{:T(128)}) while((s32[]{:T(128)}, f32[8,128,128]{2,1,0:T(8,128)S(1)}, s32[]{:T(128)}, f32[64,128]{1,0:T(8,128)S(1)}, f32[64,8,128,128]{3,2,1,0:T(8,128)}, ...), condition=%wide.region_1.2_spmd.clone, body=%wide.region_0.1_spmd.clone.sunk | while | flops 524292 | bytes 1574505 | solution.py:41
  420.8 3.4 collective-permute-start.33
  424.2 2.5 collective-permute-start.34
  426.7 3.3 collective-permute-done.34
  431.9 3.1 collective-permute-start.35
  435.0 2.8 collective-permute-start.36
  437.8 3.0 collective-permute-done.36
  442.5 1.9 collective-permute-start.37
  444.4 3.9 collective-permute-start.38
  452.1 1.9 collective-permute-start.39
  454.1 3.9 collective-permute-start.40
  463.5 3.9 collective-permute-start.42
  471.0 1.9 collective-permute-start.43
  473.0 3.9 collective-permute-start.44
  (463 shorter events, 175.2 us)
Async XLA Ops:
  7.2 318.0 %all-gather.4.cloned.1.call-start = ((), (), s32[]{:S(2)}) async-start(), calls=%async_computation | async-start | bytes 34078720 | tf_op jit(solution)/shard_map/all_gather | solution.py:32
  8.3 7.4 %collective-permute-start = (bf16[1,128,128]{2,1,0:T(8,128)(2,1)S(1)}, bf16[1,128,128]{2,1,0:T(8,128)(2,1)S(1)}, u32[]{:S(2)}, u32[]{:S(2)}) collective-permute-start(bf16[1,128,128]{2,1,0:T(8,128)(2,1)S(1)} %get-tuple-element.177), channel_id=1, source_target_pairs={{0,1},{1,2},{2,3},{4,5},{5,6},{6,7},{8,9},{9,10},{10,11},{12,13},{... | collective-permute-start | bytes 98312 | tf_op jit(solution)/shard_map/ppermute | solution.py:15
  11.7 5.9 %collective-permute-start.1 = (bf16[1,128,128]{2,1,0:T(8,128)(2,1)S(1)}, bf16[1,128,128]{2,1,0:T(8,128)(2,1)S(1)}, u32[]{:S(2)}, u32[]{:S(2)}) collective-permute-start(bf16[1,128,128]{2,1,0:T(8,128)(2,1)S(1)} %get-tuple-element.178), channel_id=1, source_target_pairs={{1,0},{2,1},{3,2},{5,4},{6,5},{7,6},{9,8},{10,9},{11,10},{13,12},{... | collective-permute-start | bytes 98312 | tf_op jit(solution)/shard_map/ppermute | solution.py:17
  15.7 60.9 %copy-start.7 = (bf16[1,9,128,128]{3,2,1,0:T(8,128)(2,1)}, bf16[1,9,128,128]{3,2,1,0:T(8,128)(2,1)S(1)}, u32[]{:S(2)}) copy-start(bf16[1,9,128,128]{3,2,1,0:T(8,128)(2,1)S(1)} %get-tuple-element.131) | copy-start | bytes 884740
  15.7 101.5 %copy-start.2 = (bf16[1,9,128,128]{3,2,1,0:T(8,128)(2,1)}, bf16[1,9,128,128]{3,2,1,0:T(8,128)(2,1)S(1)}, u32[]{:S(2)}) copy-start(bf16[1,9,128,128]{3,2,1,0:T(8,128)(2,1)S(1)} %get-tuple-element.132) | copy-start | bytes 884740
  19.4 6.0 %collective-permute-start.2 = (bf16[1,128,128]{2,1,0:T(8,128)(2,1)S(1)}, bf16[1,128,128]{2,1,0:T(8,128)(2,1)S(1)}, u32[]{:S(2)}, u32[]{:S(2)}) collective-permute-start(bf16[1,128,128]{2,1,0:T(8,128)(2,1)S(1)} %get-tuple-element.175), channel_id=1, source_target_pairs={{0,1},{1,2},{2,3},{4,5},{5,6},{6,7},{8,9},{9,10},{10,11},{12,13},{... | collective-permute-start | bytes 98312 | tf_op jit(solution)/shard_map/ppermute | solution.py:15
  22.5 5.8 %collective-permute-start.3 = (bf16[1,128,128]{2,1,0:T(8,128)(2,1)S(1)}, bf16[1,128,128]{2,1,0:T(8,128)(2,1)S(1)}, u32[]{:S(2)}, u32[]{:S(2)}) collective-permute-start(bf16[1,128,128]{2,1,0:T(8,128)(2,1)S(1)} %get-tuple-element.176), channel_id=1, source_target_pairs={{1,0},{2,1},{3,2},{5,4},{6,5},{7,6},{9,8},{10,9},{11,10},{13,12},{... | collective-permute-start | bytes 98312 | tf_op jit(solution)/shard_map/ppermute | solution.py:17
  30.0 5.9 %collective-permute-start.4 = (bf16[1,128,128]{2,1,0:T(8,128)(2,1)S(1)}, bf16[1,128,128]{2,1,0:T(8,128)(2,1)S(1)}, u32[]{:S(2)}, u32[]{:S(2)}) collective-permute-start(bf16[1,128,128]{2,1,0:T(8,128)(2,1)S(1)} %get-tuple-element.173), channel_id=1, source_target_pairs={{0,1},{1,2},{2,3},{4,5},{5,6},{6,7},{8,9},{9,10},{10,11},{12,13},{... | collective-permute-start | bytes 98312 | tf_op jit(solution)/shard_map/ppermute | solution.py:15
  32.0 5.8 %collective-permute-start.5 = (bf16[1,128,128]{2,1,0:T(8,128)(2,1)S(1)}, bf16[1,128,128]{2,1,0:T(8,128)(2,1)S(1)}, u32[]{:S(2)}, u32[]{:S(2)}) collective-permute-start(bf16[1,128,128]{2,1,0:T(8,128)(2,1)S(1)} %get-tuple-element.174), channel_id=1, source_target_pairs={{1,0},{2,1},{3,2},{5,4},{6,5},{7,6},{9,8},{10,9},{11,10},{13,12},{... | collective-permute-start | bytes 98312 | tf_op jit(solution)/shard_map/ppermute | solution.py:17
  39.5 5.9 %collective-permute-start.6 = (bf16[1,128,128]{2,1,0:T(8,128)(2,1)S(1)}, bf16[1,128,128]{2,1,0:T(8,128)(2,1)S(1)}, u32[]{:S(2)}, u32[]{:S(2)}) collective-permute-start(bf16[1,128,128]{2,1,0:T(8,128)(2,1)S(1)} %get-tuple-element.171), channel_id=1, source_target_pairs={{0,1},{1,2},{2,3},{4,5},{5,6},{6,7},{8,9},{9,10},{10,11},{12,13},{... | collective-permute-start | bytes 98312 | tf_op jit(solution)/shard_map/ppermute | solution.py:15
  41.4 5.8 %collective-permute-start.7 = (bf16[1,128,128]{2,1,0:T(8,128)(2,1)S(1)}, bf16[1,128,128]{2,1,0:T(8,128)(2,1)S(1)}, u32[]{:S(2)}, u32[]{:S(2)}) collective-permute-start(bf16[1,128,128]{2,1,0:T(8,128)(2,1)S(1)} %get-tuple-element.172), channel_id=1, source_target_pairs={{1,0},{2,1},{3,2},{5,4},{6,5},{7,6},{9,8},{10,9},{11,10},{13,12},{... | collective-permute-start | bytes 98312 | tf_op jit(solution)/shard_map/ppermute | solution.py:17
  48.9 5.9 %collective-permute-start.8 = (bf16[1,128,128]{2,1,0:T(8,128)(2,1)S(1)}, bf16[1,128,128]{2,1,0:T(8,128)(2,1)S(1)}, u32[]{:S(2)}, u32[]{:S(2)}) collective-permute-start(bf16[1,128,128]{2,1,0:T(8,128)(2,1)S(1)} %get-tuple-element.169), channel_id=1, source_target_pairs={{0,1},{1,2},{2,3},{4,5},{5,6},{6,7},{8,9},{9,10},{10,11},{12,13},{... | collective-permute-start | bytes 98312 | tf_op jit(solution)/shard_map/ppermute | solution.py:15
  50.8 5.8 %collective-permute-start.9 = (bf16[1,128,128]{2,1,0:T(8,128)(2,1)S(1)}, bf16[1,128,128]{2,1,0:T(8,128)(2,1)S(1)}, u32[]{:S(2)}, u32[]{:S(2)}) collective-permute-start(bf16[1,128,128]{2,1,0:T(8,128)(2,1)S(1)} %get-tuple-element.170), channel_id=1, source_target_pairs={{1,0},{2,1},{3,2},{5,4},{6,5},{7,6},{9,8},{10,9},{11,10},{13,12},{... | collective-permute-start | bytes 98312 | tf_op jit(solution)/shard_map/ppermute | solution.py:17
  58.4 5.9 %collective-permute-start.10 = (bf16[1,128,128]{2,1,0:T(8,128)(2,1)S(1)}, bf16[1,128,128]{2,1,0:T(8,128)(2,1)S(1)}, u32[]{:S(2)}, u32[]{:S(2)}) collective-permute-start(bf16[1,128,128]{2,1,0:T(8,128)(2,1)S(1)} %get-tuple-element.167), channel_id=1, source_target_pairs={{0,1},{1,2},{2,3},{4,5},{5,6},{6,7},{8,9},{9,10},{10,11},{12,13},{... | collective-permute-start | bytes 98312 | tf_op jit(solution)/shard_map/ppermute | solution.py:15
  60.3 5.8 %collective-permute-start.11 = (bf16[1,128,128]{2,1,0:T(8,128)(2,1)S(1)}, bf16[1,128,128]{2,1,0:T(8,128)(2,1)S(1)}, u32[]{:S(2)}, u32[]{:S(2)}) collective-permute-start(bf16[1,128,128]{2,1,0:T(8,128)(2,1)S(1)} %get-tuple-element.168), channel_id=1, source_target_pairs={{1,0},{2,1},{3,2},{5,4},{6,5},{7,6},{9,8},{10,9},{11,10},{13,12},{... | collective-permute-start | bytes 98312 | tf_op jit(solution)/shard_map/ppermute | solution.py:17
  67.8 6.0 %collective-permute-start.12 = (bf16[1,128,128]{2,1,0:T(8,128)(2,1)S(1)}, bf16[1,128,128]{2,1,0:T(8,128)(2,1)S(1)}, u32[]{:S(2)}, u32[]{:S(2)}) collective-permute-start(bf16[1,128,128]{2,1,0:T(8,128)(2,1)S(1)} %get-tuple-element.165), channel_id=1, source_target_pairs={{0,1},{1,2},{2,3},{4,5},{5,6},{6,7},{8,9},{9,10},{10,11},{12,13},{... | collective-permute-start | bytes 98312 | tf_op jit(solution)/shard_map/ppermute | solution.py:15
  69.7 6.0 %collective-permute-start.13 = (bf16[1,128,128]{2,1,0:T(8,128)(2,1)S(1)}, bf16[1,128,128]{2,1,0:T(8,128)(2,1)S(1)}, u32[]{:S(2)}, u32[]{:S(2)}) collective-permute-start(bf16[1,128,128]{2,1,0:T(8,128)(2,1)S(1)} %get-tuple-element.166), channel_id=1, source_target_pairs={{1,0},{2,1},{3,2},{5,4},{6,5},{7,6},{9,8},{10,9},{11,10},{13,12},{... | collective-permute-start | bytes 98312 | tf_op jit(solution)/shard_map/ppermute | solution.py:17
  77.4 6.1 %collective-permute-start.14 = (bf16[1,128,128]{2,1,0:T(8,128)(2,1)S(1)}, bf16[1,128,128]{2,1,0:T(8,128)(2,1)S(1)}, u32[]{:S(2)}, u32[]{:S(2)}) collective-permute-start(bf16[1,128,128]{2,1,0:T(8,128)(2,1)S(1)} %get-tuple-element.163), channel_id=1, source_target_pairs={{0,1},{1,2},{2,3},{4,5},{5,6},{6,7},{8,9},{9,10},{10,11},{12,13},{... | collective-permute-start | bytes 98312 | tf_op jit(solution)/shard_map/ppermute | solution.py:15
  79.4 5.8 %collective-permute-start.15 = (bf16[1,128,128]{2,1,0:T(8,128)(2,1)S(1)}, bf16[1,128,128]{2,1,0:T(8,128)(2,1)S(1)}, u32[]{:S(2)}, u32[]{:S(2)}) collective-permute-start(bf16[1,128,128]{2,1,0:T(8,128)(2,1)S(1)} %get-tuple-element.164), channel_id=1, source_target_pairs={{1,0},{2,1},{3,2},{5,4},{6,5},{7,6},{9,8},{10,9},{11,10},{13,12},{... | collective-permute-start | bytes 98312 | tf_op jit(solution)/shard_map/ppermute | solution.py:17
  86.9 2.4 collective-permute-start.16
  89.5 5.9 %collective-permute-start.17 = (bf16[1,128,128]{2,1,0:T(8,128)(2,1)S(1)}, bf16[1,128,128]{2,1,0:T(8,128)(2,1)S(1)}, u32[]{:S(2)}, u32[]{:S(2)}) collective-permute-start(bf16[1,128,128]{2,1,0:T(8,128)(2,1)S(1)} %get-tuple-element.161), channel_id=1, source_target_pairs={{0,1},{1,2},{2,3},{4,5},{5,6},{6,7},{8,9},{9,10},{10,11},{12,13},{... | collective-permute-start | bytes 98312 | tf_op jit(solution)/shard_map/ppermute | solution.py:15
  91.4 5.8 %collective-permute-start.18 = (bf16[1,128,128]{2,1,0:T(8,128)(2,1)S(1)}, bf16[1,128,128]{2,1,0:T(8,128)(2,1)S(1)}, u32[]{:S(2)}, u32[]{:S(2)}) collective-permute-start(bf16[1,128,128]{2,1,0:T(8,128)(2,1)S(1)} %get-tuple-element.162), channel_id=1, source_target_pairs={{1,0},{2,1},{3,2},{5,4},{6,5},{7,6},{9,8},{10,9},{11,10},{13,12},{... | collective-permute-start | bytes 98312 | tf_op jit(solution)/shard_map/ppermute | solution.py:17
  99.1 5.9 %collective-permute-start.19 = (bf16[1,128,128]{2,1,0:T(8,128)(2,1)S(1)}, bf16[1,128,128]{2,1,0:T(8,128)(2,1)S(1)}, u32[]{:S(2)}, u32[]{:S(2)}) collective-permute-start(bf16[1,128,128]{2,1,0:T(8,128)(2,1)S(1)} %get-tuple-element.159), channel_id=1, source_target_pairs={{0,1},{1,2},{2,3},{4,5},{5,6},{6,7},{8,9},{9,10},{10,11},{12,13},{... | collective-permute-start | bytes 98312 | tf_op jit(solution)/shard_map/ppermute | solution.py:15
  101.0 5.8 %collective-permute-start.20 = (bf16[1,128,128]{2,1,0:T(8,128)(2,1)S(1)}, bf16[1,128,128]{2,1,0:T(8,128)(2,1)S(1)}, u32[]{:S(2)}, u32[]{:S(2)}) collective-permute-start(bf16[1,128,128]{2,1,0:T(8,128)(2,1)S(1)} %get-tuple-element.160), channel_id=1, source_target_pairs={{1,0},{2,1},{3,2},{5,4},{6,5},{7,6},{9,8},{10,9},{11,10},{13,12},{... | collective-permute-start | bytes 98312 | tf_op jit(solution)/shard_map/ppermute | solution.py:17
  108.5 5.9 %collective-permute-start.21 = (bf16[1,128,128]{2,1,0:T(8,128)(2,1)S(1)}, bf16[1,128,128]{2,1,0:T(8,128)(2,1)S(1)}, u32[]{:S(2)}, u32[]{:S(2)}) collective-permute-start(bf16[1,128,128]{2,1,0:T(8,128)(2,1)S(1)} %get-tuple-element.157), channel_id=1, source_target_pairs={{0,1},{1,2},{2,3},{4,5},{5,6},{6,7},{8,9},{9,10},{10,11},{12,13},{... | collective-permute-start | bytes 98312 | tf_op jit(solution)/shard_map/ppermute | solution.py:15
  110.4 5.8 %collective-permute-start.22 = (bf16[1,128,128]{2,1,0:T(8,128)(2,1)S(1)}, bf16[1,128,128]{2,1,0:T(8,128)(2,1)S(1)}, u32[]{:S(2)}, u32[]{:S(2)}) collective-permute-start(bf16[1,128,128]{2,1,0:T(8,128)(2,1)S(1)} %get-tuple-element.158), channel_id=1, source_target_pairs={{1,0},{2,1},{3,2},{5,4},{6,5},{7,6},{9,8},{10,9},{11,10},{13,12},{... | collective-permute-start | bytes 98312 | tf_op jit(solution)/shard_map/ppermute | solution.py:17
  118.0 5.9 %collective-permute-start.23 = (bf16[1,128,128]{2,1,0:T(8,128)(2,1)S(1)}, bf16[1,128,128]{2,1,0:T(8,128)(2,1)S(1)}, u32[]{:S(2)}, u32[]{:S(2)}) collective-permute-start(bf16[1,128,128]{2,1,0:T(8,128)(2,1)S(1)} %get-tuple-element.155), channel_id=1, source_target_pairs={{0,1},{1,2},{2,3},{4,5},{5,6},{6,7},{8,9},{9,10},{10,11},{12,13},{... | collective-permute-start | bytes 98312 | tf_op jit(solution)/shard_map/ppermute | solution.py:15
  119.9 5.8 %collective-permute-start.24 = (bf16[1,128,128]{2,1,0:T(8,128)(2,1)S(1)}, bf16[1,128,128]{2,1,0:T(8,128)(2,1)S(1)}, u32[]{:S(2)}, u32[]{:S(2)}) collective-permute-start(bf16[1,128,128]{2,1,0:T(8,128)(2,1)S(1)} %get-tuple-element.156), channel_id=1, source_target_pairs={{1,0},{2,1},{3,2},{5,4},{6,5},{7,6},{9,8},{10,9},{11,10},{13,12},{... | collective-permute-start | bytes 98312 | tf_op jit(solution)/shard_map/ppermute | solution.py:17
  127.4 5.9 %collective-permute-start.25 = (bf16[1,128,128]{2,1,0:T(8,128)(2,1)S(1)}, bf16[1,128,128]{2,1,0:T(8,128)(2,1)S(1)}, u32[]{:S(2)}, u32[]{:S(2)}) collective-permute-start(bf16[1,128,128]{2,1,0:T(8,128)(2,1)S(1)} %get-tuple-element.153), channel_id=1, source_target_pairs={{0,1},{1,2},{2,3},{4,5},{5,6},{6,7},{8,9},{9,10},{10,11},{12,13},{... | collective-permute-start | bytes 98312 | tf_op jit(solution)/shard_map/ppermute | solution.py:15
  129.3 5.8 %collective-permute-start.26 = (bf16[1,128,128]{2,1,0:T(8,128)(2,1)S(1)}, bf16[1,128,128]{2,1,0:T(8,128)(2,1)S(1)}, u32[]{:S(2)}, u32[]{:S(2)}) collective-permute-start(bf16[1,128,128]{2,1,0:T(8,128)(2,1)S(1)} %get-tuple-element.154), channel_id=1, source_target_pairs={{1,0},{2,1},{3,2},{5,4},{6,5},{7,6},{9,8},{10,9},{11,10},{13,12},{... | collective-permute-start | bytes 98312 | tf_op jit(solution)/shard_map/ppermute | solution.py:17
  136.8 5.9 %collective-permute-start.27 = (bf16[1,128,128]{2,1,0:T(8,128)(2,1)S(1)}, bf16[1,128,128]{2,1,0:T(8,128)(2,1)S(1)}, u32[]{:S(2)}, u32[]{:S(2)}) collective-permute-start(bf16[1,128,128]{2,1,0:T(8,128)(2,1)S(1)} %get-tuple-element.151), channel_id=1, source_target_pairs={{0,1},{1,2},{2,3},{4,5},{5,6},{6,7},{8,9},{9,10},{10,11},{12,13},{... | collective-permute-start | bytes 98312 | tf_op jit(solution)/shard_map/ppermute | solution.py:15
  138.8 5.8 %collective-permute-start.28 = (bf16[1,128,128]{2,1,0:T(8,128)(2,1)S(1)}, bf16[1,128,128]{2,1,0:T(8,128)(2,1)S(1)}, u32[]{:S(2)}, u32[]{:S(2)}) collective-permute-start(bf16[1,128,128]{2,1,0:T(8,128)(2,1)S(1)} %get-tuple-element.152), channel_id=1, source_target_pairs={{1,0},{2,1},{3,2},{5,4},{6,5},{7,6},{9,8},{10,9},{11,10},{13,12},{... | collective-permute-start | bytes 98312 | tf_op jit(solution)/shard_map/ppermute | solution.py:17
  146.3 15.6 %collective-permute-start.29 = (bf16[1,128,128]{2,1,0:T(8,128)(2,1)S(1)}, bf16[1,128,128]{2,1,0:T(8,128)(2,1)S(1)}, u32[]{:S(2)}, u32[]{:S(2)}) collective-permute-start(bf16[1,128,128]{2,1,0:T(8,128)(2,1)S(1)} %get-tuple-element.149), channel_id=1, source_target_pairs={{0,1},{1,2},{2,3},{4,5},{5,6},{6,7},{8,9},{9,10},{10,11},{12,13},{... | collective-permute-start | bytes 98312 | tf_op jit(solution)/shard_map/ppermute | solution.py:15
  148.2 13.7 %collective-permute-start.30 = (bf16[1,128,128]{2,1,0:T(8,128)(2,1)S(1)}, bf16[1,128,128]{2,1,0:T(8,128)(2,1)S(1)}, u32[]{:S(2)}, u32[]{:S(2)}) collective-permute-start(bf16[1,128,128]{2,1,0:T(8,128)(2,1)S(1)} %get-tuple-element.150), channel_id=1, source_target_pairs={{1,0},{2,1},{3,2},{5,4},{6,5},{7,6},{9,8},{10,9},{11,10},{13,12},{... | collective-permute-start | bytes 98312 | tf_op jit(solution)/shard_map/ppermute | solution.py:17
  163.8 6.6 %collective-permute-start.31 = (bf16[1,128,128]{2,1,0:T(8,128)(2,1)S(1)}, bf16[1,128,128]{2,1,0:T(8,128)(2,1)S(1)}, u32[]{:S(2)}, u32[]{:S(2)}) collective-permute-start(bf16[1,128,128]{2,1,0:T(8,128)(2,1)S(1)} %get-tuple-element.147), channel_id=1, source_target_pairs={{0,1},{1,2},{2,3},{4,5},{5,6},{6,7},{8,9},{9,10},{10,11},{12,13},{... | collective-permute-start | bytes 98312 | tf_op jit(solution)/shard_map/ppermute | solution.py:15
  165.7 5.8 %collective-permute-start.32 = (bf16[1,128,128]{2,1,0:T(8,128)(2,1)S(1)}, bf16[1,128,128]{2,1,0:T(8,128)(2,1)S(1)}, u32[]{:S(2)}, u32[]{:S(2)}) collective-permute-start(bf16[1,128,128]{2,1,0:T(8,128)(2,1)S(1)} %get-tuple-element.148), channel_id=1, source_target_pairs={{1,0},{2,1},{3,2},{5,4},{6,5},{7,6},{9,8},{10,9},{11,10},{13,12},{... | collective-permute-start | bytes 98312 | tf_op jit(solution)/shard_map/ppermute | solution.py:17
  420.8 5.9 %collective-permute-start.33 = (bf16[1,128,128]{2,1,0:T(8,128)(2,1)S(1)}, bf16[1,128,128]{2,1,0:T(8,128)(2,1)S(1)}, u32[]{:S(2)}, u32[]{:S(2)}) collective-permute-start(bf16[1,128,128]{2,1,0:T(8,128)(2,1)S(1)} %get-tuple-element.145), channel_id=1, source_target_pairs={{0,1},{1,2},{2,3},{4,5},{5,6},{6,7},{8,9},{9,10},{10,11},{12,13},{... | collective-permute-start | bytes 98312 | tf_op jit(solution)/shard_map/ppermute | solution.py:15
  424.2 5.8 %collective-permute-start.34 = (bf16[1,128,128]{2,1,0:T(8,128)(2,1)S(1)}, bf16[1,128,128]{2,1,0:T(8,128)(2,1)S(1)}, u32[]{:S(2)}, u32[]{:S(2)}) collective-permute-start(bf16[1,128,128]{2,1,0:T(8,128)(2,1)S(1)} %get-tuple-element.146), channel_id=1, source_target_pairs={{1,0},{2,1},{3,2},{5,4},{6,5},{7,6},{9,8},{10,9},{11,10},{13,12},{... | collective-permute-start | bytes 98312 | tf_op jit(solution)/shard_map/ppermute | solution.py:17
  431.9 5.9 %collective-permute-start.35 = (bf16[1,128,128]{2,1,0:T(8,128)(2,1)S(1)}, bf16[1,128,128]{2,1,0:T(8,128)(2,1)S(1)}, u32[]{:S(2)}, u32[]{:S(2)}) collective-permute-start(bf16[1,128,128]{2,1,0:T(8,128)(2,1)S(1)} %get-tuple-element.143), channel_id=1, source_target_pairs={{0,1},{1,2},{2,3},{4,5},{5,6},{6,7},{8,9},{9,10},{10,11},{12,13},{... | collective-permute-start | bytes 98312 | tf_op jit(solution)/shard_map/ppermute | solution.py:15
  435.0 5.8 %collective-permute-start.36 = (bf16[1,128,128]{2,1,0:T(8,128)(2,1)S(1)}, bf16[1,128,128]{2,1,0:T(8,128)(2,1)S(1)}, u32[]{:S(2)}, u32[]{:S(2)}) collective-permute-start(bf16[1,128,128]{2,1,0:T(8,128)(2,1)S(1)} %get-tuple-element.144), channel_id=1, source_target_pairs={{1,0},{2,1},{3,2},{5,4},{6,5},{7,6},{9,8},{10,9},{11,10},{13,12},{... | collective-permute-start | bytes 98312 | tf_op jit(solution)/shard_map/ppermute | solution.py:17
  442.5 5.9 %collective-permute-start.37 = (bf16[1,128,128]{2,1,0:T(8,128)(2,1)S(1)}, bf16[1,128,128]{2,1,0:T(8,128)(2,1)S(1)}, u32[]{:S(2)}, u32[]{:S(2)}) collective-permute-start(bf16[1,128,128]{2,1,0:T(8,128)(2,1)S(1)} %get-tuple-element.141), channel_id=1, source_target_pairs={{0,1},{1,2},{2,3},{4,5},{5,6},{6,7},{8,9},{9,10},{10,11},{12,13},{... | collective-permute-start | bytes 98312 | tf_op jit(solution)/shard_map/ppermute | solution.py:15
  444.4 5.8 %collective-permute-start.38 = (bf16[1,128,128]{2,1,0:T(8,128)(2,1)S(1)}, bf16[1,128,128]{2,1,0:T(8,128)(2,1)S(1)}, u32[]{:S(2)}, u32[]{:S(2)}) collective-permute-start(bf16[1,128,128]{2,1,0:T(8,128)(2,1)S(1)} %get-tuple-element.142), channel_id=1, source_target_pairs={{1,0},{2,1},{3,2},{5,4},{6,5},{7,6},{9,8},{10,9},{11,10},{13,12},{... | collective-permute-start | bytes 98312 | tf_op jit(solution)/shard_map/ppermute | solution.py:17
  452.1 5.9 %collective-permute-start.39 = (bf16[1,128,128]{2,1,0:T(8,128)(2,1)S(1)}, bf16[1,128,128]{2,1,0:T(8,128)(2,1)S(1)}, u32[]{:S(2)}, u32[]{:S(2)}) collective-permute-start(bf16[1,128,128]{2,1,0:T(8,128)(2,1)S(1)} %get-tuple-element.139), channel_id=1, source_target_pairs={{0,1},{1,2},{2,3},{4,5},{5,6},{6,7},{8,9},{9,10},{10,11},{12,13},{... | collective-permute-start | bytes 98312 | tf_op jit(solution)/shard_map/ppermute | solution.py:15
  454.1 5.8 %collective-permute-start.40 = (bf16[1,128,128]{2,1,0:T(8,128)(2,1)S(1)}, bf16[1,128,128]{2,1,0:T(8,128)(2,1)S(1)}, u32[]{:S(2)}, u32[]{:S(2)}) collective-permute-start(bf16[1,128,128]{2,1,0:T(8,128)(2,1)S(1)} %get-tuple-element.140), channel_id=1, source_target_pairs={{1,0},{2,1},{3,2},{5,4},{6,5},{7,6},{9,8},{10,9},{11,10},{13,12},{... | collective-permute-start | bytes 98312 | tf_op jit(solution)/shard_map/ppermute | solution.py:17
  461.6 5.9 %collective-permute-start.41 = (bf16[1,128,128]{2,1,0:T(8,128)(2,1)S(1)}, bf16[1,128,128]{2,1,0:T(8,128)(2,1)S(1)}, u32[]{:S(2)}, u32[]{:S(2)}) collective-permute-start(bf16[1,128,128]{2,1,0:T(8,128)(2,1)S(1)} %get-tuple-element.137), channel_id=1, source_target_pairs={{0,1},{1,2},{2,3},{4,5},{5,6},{6,7},{8,9},{9,10},{10,11},{12,13},{... | collective-permute-start | bytes 98312 | tf_op jit(solution)/shard_map/ppermute | solution.py:15
  463.5 5.8 %collective-permute-start.42 = (bf16[1,128,128]{2,1,0:T(8,128)(2,1)S(1)}, bf16[1,128,128]{2,1,0:T(8,128)(2,1)S(1)}, u32[]{:S(2)}, u32[]{:S(2)}) collective-permute-start(bf16[1,128,128]{2,1,0:T(8,128)(2,1)S(1)} %get-tuple-element.138), channel_id=1, source_target_pairs={{1,0},{2,1},{3,2},{5,4},{6,5},{7,6},{9,8},{10,9},{11,10},{13,12},{... | collective-permute-start | bytes 98312 | tf_op jit(solution)/shard_map/ppermute | solution.py:17
  471.0 5.9 %collective-permute-start.43 = (bf16[1,128,128]{2,1,0:T(8,128)(2,1)S(1)}, bf16[1,128,128]{2,1,0:T(8,128)(2,1)S(1)}, u32[]{:S(2)}, u32[]{:S(2)}) collective-permute-start(bf16[1,128,128]{2,1,0:T(8,128)(2,1)S(1)} %get-tuple-element.135), channel_id=1, source_target_pairs={{0,1},{1,2},{2,3},{4,5},{5,6},{6,7},{8,9},{9,10},{10,11},{12,13},{... | collective-permute-start | bytes 98312 | tf_op jit(solution)/shard_map/ppermute | solution.py:15
  473.0 5.8 %collective-permute-start.44 = (bf16[1,128,128]{2,1,0:T(8,128)(2,1)S(1)}, bf16[1,128,128]{2,1,0:T(8,128)(2,1)S(1)}, u32[]{:S(2)}, u32[]{:S(2)}) collective-permute-start(bf16[1,128,128]{2,1,0:T(8,128)(2,1)S(1)} %get-tuple-element.136), channel_id=1, source_target_pairs={{1,0},{2,1},{3,2},{5,4},{6,5},{7,6},{9,8},{10,9},{11,10},{13,12},{... | collective-permute-start | bytes 98312 | tf_op jit(solution)/shard_map/ppermute | solution.py:17
  (7 other events, 20.1 us)
Sparse Core Ops, SparseCore 0:
  174.3 150.7 all-gather.3
where the time goes:
time: 498 us; the launch traced here: 489 us
  waiting for transfers between devices  145 us (29%)
  starting transfers between devices  140 us (28%)
  other arithmetic  101 us (20%)
  blocking collectives  49.6 us (10%)
  matrix products  18.3 us (4%)
  between operations  16.9 us (3%)
  local copies, waits for them, and re-layouts  16.4 us (3%)
    all_gather x1, waiting for transfers between devices, prefix(): pieces = jax.tree.map(lambda part: lax.all_gather(part, axis), value)  101 us
    select_n x63, other arithmetic, step(): jnp.where(position < mine, new, old)  93.2 us
    ppermute x22, starting transfers between devices, extended(): lax.ppermute(head, axis, [((i + 1) % count, i) for i in range(ends)])  91 us
    all_gather x1, blocking collectives, prefix(): pieces = jax.tree.map(lambda part: lax.all_gather(part, axis), value)  49.6 us
    ppermute x22, starting transfers between devices, extended(): lax.ppermute(tail, axis, [(i, (i + 1) % count) for i in range(ends)])  47.6 us
    ppermute x22, waiting for transfers between devices, extended(): lax.ppermute(head, axis, [((i + 1) % count, i) for i in range(ends)])  42.3 us
    dot_general x22, matrix products, conv_taps(): jnp.dot(stacked, flat, preferred_element_type=jnp.float32)  18.3 us
    unnamed x149, local copies, waits for them, and re-layouts  11.1 us
  transfers between devices with their start and end apart: 46, of which 24 were waited for; matrix products, arithmetic and copies ran while one was open for 0% of the time, Pallas kernels for 0%

commit v1 on v0

v1 whole, which is shorter than its diff:
```python
import functools

import jax
import jax.numpy as jnp
from jax import lax
from jax.experimental import pallas as pl
from jax.experimental.pallas import tpu as pltpu
from jax.sharding import PartitionSpec as P

GROUP = 4
W = 128
C = 128


def widen_taps(taps, wide, slot):
    wide[slot, pl.ds(0, 9 * C), pl.ds(0, C)] = taps
    wide[slot, pl.ds(3 * C, 9 * C), pl.ds(C, C)] = taps


def spread(dst, pair, half, row):
    column = lax.broadcasted_iota(jnp.int32, (W, C), 0)
    before = jnp.where(column == 0, 0.0, pltpu.roll(row, 1, 0))
    after = jnp.where(column == W - 1, 0.0, pltpu.roll(row, W - 1, 0))
    for tap, part in enumerate((before, row, after)):
        dst[pair, :, pl.ds((half * 3 + tap) * C, C)] = part.astype(jnp.bfloat16)


def conv_pairs(src, wide, slot, pairs, emit):
    for first in range(0, pairs, GROUP):
        count = min(GROUP, pairs - first)
        low = src[pl.ds(first, count)].reshape(count * W, 6 * C)
        high = src[pl.ds(first + 1, count)].reshape(count * W, 6 * C)
        total = jnp.dot(
            low, wide[slot, pl.ds(0, 6 * C), :], preferred_element_type=jnp.float32
        ) + jnp.dot(high, wide[slot, pl.ds(6 * C, 6 * C), :], preferred_element_type=jnp.float32)
        for index in range(count):
            for half in range(2):
                emit(
                    first + index,
                    half,
                    total[index * W : (index + 1) * W, half * C : (half + 1) * C],
                )


def layers(count, halo, own, flags, state, fields, wide, firsts, seconds, after_layer):
    def keep(row, value):
        if row < halo:
            return value * flags[0]
        if row >= halo + own:
            return value * flags[1]
        return value

    rows = own + 2 * halo
    wide[:, pl.ds(9 * C, 3 * C), pl.ds(0, C)] = jnp.zeros((2, 3 * C, C), jnp.bfloat16)
    wide[:, pl.ds(0, 3 * C), pl.ds(C, C)] = jnp.zeros((2, 3 * C, C), jnp.bfloat16)
    for layer in range(count):
        widen_taps(firsts[layer], wide, 0)
        offset = 2 * layer + 1

        def hidden(pair, half, value, offset=offset):
            row = offset + 2 * pair + half
            spread(fields[1], pair, half, keep(row, jnp.tanh(value)))

        conv_pairs(fields[0], wide, 0, (rows - 2 * offset) // 2, hidden)
        widen_taps(seconds[layer], wide, 1)
        offset = 2 * layer + 2

        def outer(pair, half, value, offset=offset, last=layer == count - 1):
            row = offset + 2 * pair + half
            new = state[row] + 0.5 * keep(row, jnp.tanh(value))
            if not last:
                state[row] = new
                spread(fields[0], pair, half, new)
            after_layer(offset // 2, row, new)

        conv_pairs(fields[1], wide, 1, (rows - 2 * offset) // 2, outer)


def first_kernel(flags_ref, own_ref, top_ref, bottom_ref, firsts, seconds, y_ref, state, fa, fb, wide):
    own = own_ref.shape[0]
    halo = top_ref.shape[0]
    for row in range(own + 2 * halo):
        if row < halo:
            value = top_ref[row].astype(jnp.float32)
        elif row < halo + own:
            value = own_ref[row - halo]
        else:
            value = bottom_ref[row - halo - own].astype(jnp.float32)
        state[row] = value
        spread(fa, row // 2, row % 2, value)

    def after_layer(done, row, new):
        if done == firsts.shape[0]:
            y_ref[row - halo] = new.astype(jnp.bfloat16)

    flags = (flags_ref[0], flags_ref[1])
    layers(firsts.shape[0], halo, own, flags, state, (fa, fb), wide, firsts, seconds, after_layer)


def second_kernel(
    flags_ref, own_ref, top_ref, bottom_ref, got_ref, got_top_ref, got_bottom_ref, y_ref,
    firsts, seconds, relaxed_ref, resid_ref, state, fa, fb, wide,
):
    own = own_ref.shape[0]
    halo = top_ref.shape[0]
    start = flags_ref[2] > 0.5
    for row in range(own + 2 * halo):
        if row < halo:
            value = jnp.where(start, top_ref[row], got_top_ref[row]).astype(jnp.float32)
        elif row < halo + own:
            at = row - halo
            value = jnp.where(start, own_ref[at], got_ref[at].astype(jnp.float32))
        else:
            at = row - halo - own
            value = jnp.where(start, bottom_ref[at], got_bottom_ref[at]).astype(jnp.float32)
        state[row] = value
        spread(fa, row // 2, row % 2, value)

    def after_layer(done, row, new):
        if done == firsts.shape[0]:
            at = row - halo
            relaxed_ref[at] = new
            resid_ref[at] = (new - y_ref[at].astype(jnp.float32)).astype(jnp.bfloat16)

    flags = (flags_ref[0], flags_ref[1])
    layers(firsts.shape[0], halo, own, flags, state, (fa, fb), wide, firsts, seconds, after_layer)


def third_kernel(
    flags_ref, own_ref, top_ref, bottom_ref, got_ref, got_top_ref, got_bottom_ref,
    error_ref, error_top_ref, error_bottom_ref, firsts, seconds, states_ref, state, fa, fb, wide,
):
    own = own_ref.shape[0]
    halo = error_top_ref.shape[0]
    skip = top_ref.shape[0] - halo
    start = flags_ref[2] > 0.5
    for row in range(own + 2 * halo):
        if row < halo:
            value = jnp.where(start, top_ref[row + skip], got_top_ref[row + skip]).astype(jnp.float32)
            value = value + error_top_ref[row].astype(jnp.float32)
        elif row < halo + own:
            at = row - halo
            value = jnp.where(start, own_ref[at], got_ref[at].astype(jnp.float32))
            value = value + error_ref[at].astype(jnp.float32)
            states_ref[0, at] = value
        else:
            at = row - halo - own
            value = jnp.where(start, bottom_ref[at], got_bottom_ref[at]).astype(jnp.float32)
            value = value + error_bottom_ref[at].astype(jnp.float32)
        state[row] = value
        spread(fa, row // 2, row % 2, value)

    def after_layer(done, row, new):
        if halo <= row < halo + own:
            states_ref[done, row - halo] = new

    flags = (flags_ref[0], flags_ref[1])
    count = firsts.shape[0] - 1
    layers(count, halo, own, flags, state, (fa, fb), wide, firsts, seconds, after_layer)


def scan_kernel(gain_ref, resid_ref, error_ref):
    count = error_ref.shape[0]
    error_ref[0] = jnp.zeros(error_ref.shape[1:], error_ref.dtype)
    carry = jnp.zeros(error_ref.shape[1:], jnp.float32)
    for j in range(1, count):
        carry = gain_ref[pl.ds(j, 1), :] * carry + resid_ref[j - 1].astype(jnp.float32)
        error_ref[j] = carry.astype(error_ref.dtype)


def call(kernel, halo, own, outs, args):
    rows = own + 2 * halo
    in_specs = [pl.BlockSpec(memory_space=pltpu.SMEM)]
    in_specs += [pl.BlockSpec(memory_space=pltpu.VMEM)] * (len(args) - 1)
    return pl.pallas_call(
        kernel,
        out_shape=outs,
        in_specs=in_specs,
        out_specs=jax.tree.map(lambda _: pl.BlockSpec(memory_space=pltpu.VMEM), outs),
        scratch_shapes=[
            pltpu.VMEM((rows, W, C), jnp.float32),
            pltpu.VMEM((rows // 2, W, 6 * C), jnp.bfloat16),
            pltpu.VMEM((rows // 2, W, 6 * C), jnp.bfloat16),
            pltpu.VMEM((2, 12 * C, 2 * C), jnp.bfloat16),
        ],
        compiler_params=pltpu.CompilerParams(vmem_limit_bytes=40 * 2**20),
    )(*args)


def neighbour(block, up):
    count = lax.axis_size("space")
    route = [(i, i + 1) if up else (i + 1, i) for i in range(count - 1)]
    return lax.ppermute(block, "space", route)


def from_previous(block, shift):
    depth, space = lax.axis_size("depth"), lax.axis_size("space")
    route = [
        (d * space + s + shift, (d + 1) * space + s)
        for d in range(depth - 1)
        for s in range(space)
        if 0 <= s + shift < space
    ]
    return lax.ppermute(block, ("depth", "space"), route)


def shards(coarse_states, first_kernels, second_kernels, coarse_channel_gain):
    own_rows = coarse_states.shape[1]
    here = first_kernels.shape[0]
    bf16 = jnp.bfloat16
    start = coarse_states[0]
    depth = lax.axis_size("depth")
    slab = lax.axis_index("space")
    flags = jnp.stack(
        [slab > 0, slab < lax.axis_size("space") - 1, lax.axis_index("depth") == 0]
    ).astype(jnp.float32)
    firsts = first_kernels.reshape(here, 9 * C, C)
    seconds = second_kernels.reshape(here, 9 * C, C)

    halo = 2 * here
    rounded = start.astype(bf16)
    top = neighbour(rounded[own_rows - halo :], True)
    bottom = neighbour(rounded[:halo], False)
    field = jax.ShapeDtypeStruct(start.shape, bf16)
    y_first = call(
        first_kernel, halo, own_rows, field, (flags, start, top, bottom, firsts, seconds)
    )
    got_top = from_previous(y_first[own_rows - halo :], -1)
    got = from_previous(y_first, 0)
    got_bottom = from_previous(y_first[:halo], 1)
    relaxed, resid = call(
        second_kernel, halo, own_rows,
        (jax.ShapeDtypeStruct(start.shape, jnp.float32), field),
        (flags, start, top, bottom, got, got_top, got_bottom, y_first, firsts, seconds),
    )
    pixels = own_rows * W // depth
    columns = lax.all_to_all(resid.reshape(depth, pixels, C), "depth", 0, 0)
    errors = pl.pallas_call(
        scan_kernel, out_shape=jax.ShapeDtypeStruct(columns.shape, bf16)
    )(coarse_channel_gain, columns)
    error = lax.all_to_all(errors, "depth", 0, 0).reshape(start.shape)
    near = halo - 2
    error_top = neighbour(error[own_rows - near :], True)
    error_bottom = neighbour(error[:near], False)
    states = call(
        third_kernel, near, own_rows,
        jax.ShapeDtypeStruct((here,) + start.shape, jnp.float32),
        (flags, start, top, bottom, got, got_top, got_bottom, error, error_top, error_bottom,
         firsts, seconds),
    )
    return states, relaxed[None]


def solution(mesh):
    placed = (
        P("depth", "space", None, None),
        P("depth", None, None, None),
        P("depth", None, None, None),
        P(),
    )
    return jax.shard_map(
        shards,
        mesh=mesh,
        in_specs=placed,
        out_specs=(P("depth", "space", None, None), P("depth", "space", None, None)),
        check_vma=False,
    )
```

time: 498 us -> 120 us (0.24); the launches traced: 489 us -> 119 us
  waiting for transfers between devices: 145 us -> 16.7 us
  starting transfers between devices: 140 us -> 20.7 us
  other arithmetic: 101 us -> 1.16 us
  Pallas kernels: 0 us -> 30 us
  matrix products: 18.3 us -> 0 us
  between operations: 16.9 us -> 0.78 us
  local copies, waits for them, and re-layouts: 16.4 us -> 6.49 us
  blocking collectives: 49.6 us -> 43.5 us
    ppermute x45 -> x7, starting transfers between devices: 140 us -> 20.7 us  [the longest x4 12.2 us: neighbour(): return lax.ppermute(block, 'space', route)]
    all_gather x1 -> x0, waiting for transfers between devices: 101 us -> none  [prefix(): pieces = jax.tree.map(lambda part: lax.all_gather(part, axis), value)]
    select_n x63 -> x0, other arithmetic: 93.2 us -> none  [step(): jnp.where(position < mine, new, old)]
    all_gather x1 -> x0, blocking collectives: 49.6 us -> none  [prefix(): pieces = jax.tree.map(lambda part: lax.all_gather(part, axis), value)]
    all_to_all x0 -> x2, blocking collectives: none -> 43.5 us  [the longest x1 25.5 us: shards(): columns = lax.all_to_all(resid.reshape(depth, pixels, C), 'depth', 0, 0)]
    pallas_call x0 -> x4, Pallas kernels: none -> 30 us  [the longest x3 28.2 us: call(): pl.pallas_call(kernel, out_shape=outs, in_specs=in_specs, out_specs=jax.t...]
    ppermute x45 -> x7, waiting for transfers between devices: 43.6 us -> 16.7 us  [the longest x4 12.1 us: neighbour(): return lax.ppermute(block, 'space', route)]
    dot_general x22 -> x0, matrix products: 18.3 us -> none  [conv_taps(): jnp.dot(stacked, flat, preferred_element_type=jnp.float32)]
  transfers between devices with their start and end apart: 46 -> 7, of which waited for: 24 -> 5; matrix products, arithmetic and copies ran while one was open for 0% -> 0% of each run, Pallas kernels for 0% -> 0%
where the time goes in v1:
time: 120 us; the launch traced here: 119 us
  blocking collectives  43.5 us (36%)
  Pallas kernels  30 us (25%)
  starting transfers between devices  20.7 us (17%)
  waiting for transfers between devices  16.7 us (14%)
  local copies, waits for them, and re-layouts  6.49 us (5%)
    pallas_call x3, Pallas kernels, call(): pl.pallas_call(kernel, out_shape=outs, in_specs=in_specs, out_specs=jax.t...  28.2 us
    all_to_all x1, blocking collectives, shards(): columns = lax.all_to_all(resid.reshape(depth, pixels, C), 'depth', 0, 0)  25.5 us
    all_to_all x1, blocking collectives, shards(): error = lax.all_to_all(errors, 'depth', 0, 0).reshape(start.shape)  18 us
    ppermute x4, starting transfers between devices, neighbour(): return lax.ppermute(block, 'space', route)  12.2 us
    ppermute x4, waiting for transfers between devices, neighbour(): return lax.ppermute(block, 'space', route)  12.1 us
    ppermute x3, starting transfers between devices, from_previous(): return lax.ppermute(block, ('depth', 'space'), route)  8.55 us
    unnamed x24, local copies, waits for them, and re-layouts  6.45 us
    ppermute x3, waiting for transfers between devices, from_previous(): return lax.ppermute(block, ('depth', 'space'), route)  4.68 us
  transfers between devices with their start and end apart: 7, of which 5 were waited for; matrix products, arithmetic and copies ran while one was open for 0% of the time, Pallas kernels for 0%

profile of v1, /device:TPU:2, one launch (start us, length us, event | category | flops | bytes accessed | tf_op | source)
XLA Modules:
  0.0 119.4 jit_solution(11651410214696393895)
XLA Ops:
  0.6 1.1 bitcast_convert_fusion
  1.7 4.2 %collective-permute-start.1 = (bf16[8,128,128]{2,1,0:T(8,128)(2,1)S(1)}, bf16[8,128,128]{2,1,0:T(8,128)(2,1)S(1)}, u32[]{:S(2)}, u32[]{:S(2)}) collective-permute-start(bf16[8,128,128]{2,1,0:T(8,128)(2,1)S(1)} %bitcast_convert_fusion), channel_id=1, source_target_pairs={{1,0},{2,1},{3,2},{5,4},{6,5},{7,6},{9,8},{10,9},{11,10},{13,12},{... | collective-permute-start | bytes 786440 | tf_op jit(solution)/shard_map/ppermute | solution.py:193
  5.9 1.9 %collective-permute-start = (bf16[8,128,128]{2,1,0:T(8,128)(2,1)S(1)}, bf16[8,128,128]{2,1,0:T(8,128)(2,1)S(1)}, u32[]{:S(2)}, u32[]{:S(2)}) collective-permute-start(bf16[8,128,128]{2,1,0:T(8,128)(2,1)S(1)} %bitcast_convert_fusion), channel_id=1, source_target_pairs={{0,1},{1,2},{2,3},{4,5},{5,6},{6,7},{8,9},{9,10},{10,11},{12,13},{... | collective-permute-start | bytes 786440 | tf_op jit(solution)/shard_map/ppermute | solution.py:193
  7.8 0.1 add_convert_fusion.flags_ref
  7.9 3.7 %collective-permute-done.1.bottom_ref = bf16[8,128,128]{2,1,0:T(8,128)(2,1)S(1)} collective-permute-done((bf16[8,128,128]{2,1,0:T(8,128)(2,1)S(1)}, bf16[8,128,128]{2,1,0:T(8,128)(2,1)S(1)}, u32[]{:S(2)}, u32[]{:S(2)}) %collective-permute-start.1) | collective-permute-done | bytes 262176 | tf_op jit(solution)/shard_map/ppermute | solution.py:193
  11.7 2.5 %collective-permute-done.top_ref = bf16[8,128,128]{2,1,0:T(8,128)(2,1)S(1)} collective-permute-done((bf16[8,128,128]{2,1,0:T(8,128)(2,1)S(1)}, bf16[8,128,128]{2,1,0:T(8,128)(2,1)S(1)}, u32[]{:S(2)}, u32[]{:S(2)}) %collective-permute-start) | collective-permute-done | bytes 262176 | tf_op jit(solution)/shard_map/ppermute | solution.py:193
  14.2 0.0 copy-start
  14.2 1.3 %copy-done = bf16[4,9,128,128]{3,2,1,0:T(8,128)(2,1)S(1)} copy-done((bf16[4,9,128,128]{3,2,1,0:T(8,128)(2,1)S(1)}, bf16[4,9,128,128]{3,2,1,0:T(8,128)(2,1)}, u32[]{:S(2)}) %copy-start) | copy-done | bytes 1179672
  15.4 0.0 copy-start.2
  15.4 1.3 %copy-done.2 = bf16[4,9,128,128]{3,2,1,0:T(8,128)(2,1)S(1)} copy-done((bf16[4,9,128,128]{3,2,1,0:T(8,128)(2,1)S(1)}, bf16[4,9,128,128]{3,2,1,0:T(8,128)(2,1)}, u32[]{:S(2)}) %copy-start.2) | copy-done | bytes 1179672
  16.7 0.0 copy-start.4
  16.7 1.0 copy-done.4
  17.8 9.5 %shard_map.59.y_ref = bf16[8,128,128]{2,1,0:T(8,128)(2,1)S(1)} custom-call(f32[3]{0:T(128)S(1)} %add_convert_fusion.flags_ref, f32[8,128,128]{2,1,0:T(8,128)S(1)} %bitcast.18, bf16[8,128,128]{2,1,0:T(8,128)(2,1)S(1)} %collective-permute-done.top_ref, bf16[8,128,128]{2,1,0:T(8,128)(2,1)S(1)} %collective-permute-done.1.bottom_ref, ...), custom_call_target="tpu_custom_call" | custom-call | tf_op jit(solution)/shard_map/pallas_call | solution.py:175
  27.3 1.3 %collective-permute-start.4 = (bf16[8,128,128]{2,1,0:T(8,128)(2,1)S(1)}, bf16[8,128,128]{2,1,0:T(8,128)(2,1)S(1)}, u32[]{:S(2)}, u32[]{:S(2)}) collective-permute-start(bf16[8,128,128]{2,1,0:T(8,128)(2,1)S(1)} %shard_map.59.y_ref), channel_id=1, source_target_pairs={{1,4},{2,5},{3,6},{5,8},{6,9},{7,10},{9,12},{10,13},{11,14},{13,16... | collective-permute-start | bytes 786440 | tf_op jit(solution)/shard_map/ppermute | solution.py:204
  28.6 5.3 %collective-permute-start.3 = (bf16[8,128,128]{2,1,0:T(8,128)(2,1)S(1)}, bf16[8,128,128]{2,1,0:T(8,128)(2,1)S(1)}, u32[]{:S(2)}, u32[]{:S(2)}) collective-permute-start(bf16[8,128,128]{2,1,0:T(8,128)(2,1)S(1)} %shard_map.59.y_ref), channel_id=1, source_target_pairs={{0,5},{1,6},{2,7},{4,9},{5,10},{6,11},{8,13},{9,14},{10,15},{12,17... | collective-permute-start | bytes 786440 | tf_op jit(solution)/shard_map/ppermute | solution.py:204
  33.9 2.0 %collective-permute-start.2 = (bf16[8,128,128]{2,1,0:T(8,128)(2,1)S(1)}, bf16[8,128,128]{2,1,0:T(8,128)(2,1)S(1)}, u32[]{:S(2)}, u32[]{:S(2)}) collective-permute-start(bf16[8,128,128]{2,1,0:T(8,128)(2,1)S(1)} %shard_map.59.y_ref), channel_id=1, source_target_pairs={{0,4},{1,5},{2,6},{3,7},{4,8},{5,9},{6,10},{7,11},{8,12},{9,13},{1... | collective-permute-start | bytes 786440 | tf_op jit(solution)/shard_map/ppermute | solution.py:204
  35.8 0.0 collective-permute-done.4.got_bottom_ref
  35.8 0.0 copy-start.6
  35.9 4.7 %collective-permute-done.3.got_top_ref = bf16[8,128,128]{2,1,0:T(8,128)(2,1)S(1)} collective-permute-done((bf16[8,128,128]{2,1,0:T(8,128)(2,1)S(1)}, bf16[8,128,128]{2,1,0:T(8,128)(2,1)S(1)}, u32[]{:S(2)}, u32[]{:S(2)}) %collective-permute-start.3) | collective-permute-done | bytes 262176 | tf_op jit(solution)/shard_map/ppermute | solution.py:204
  40.5 0.0 copy-start.8
  40.5 0.0 collective-permute-done.2.got_ref
  40.5 0.0 copy-start.10
  40.5 0.0 copy-start.5
  40.5 10.4 %shard_map.60 = (f32[8,128,128]{2,1,0:T(8,128)}, bf16[8,128,128]{2,1,0:T(8,128)(2,1)S(1)}) custom-call(f32[3]{0:T(128)S(1)} %add_convert_fusion.flags_ref, f32[8,128,128]{2,1,0:T(8,128)S(1)} %bitcast.19, bf16[8,128,128]{2,1,0:T(8,128)(2,1)S(1)} %collective-permute-done.top_ref, bf16[8,128,128]{2,1,0:T(8,128)(2,1)S(1)} %collective-permute-done.1.bottom_ref, ...), custom_call_target="tpu_custom_call" | custom-call | tf_op jit(solution)/shard_map/pallas_call | solution.py:175
  50.9 0.0 copy-done.6
  50.9 0.0 copy-done.8
  50.9 0.0 copy-done.10
  50.9 0.0 copy-start.1
  50.9 0.0 copy-start.3
  50.9 25.5 %all_to_all.10.resid_ref = bf16[64,16,128]{2,1,0:T(8,128)(2,1)} all-to-all(bf16[64,16,128]{2,1,0:T(8,128)(2,1)S(1)} %bitcast.22), channel_id=1, replica_groups=mesh['depth'=64,'space'=4] {'depth'}, dimensions={0} | all-to-all | bytes 524288 | tf_op jit(solution)/shard_map/all_to_all | solution.py:237
  76.4 1.8 %shard_map.61 = bf16[64,16,128]{2,1,0:T(8,128)(2,1)} custom-call(f32[64,128]{1,0:T(8,128)} %gain_ref.1, bf16[64,16,128]{2,1,0:T(8,128)(2,1)} %all_to_all.10.resid_ref), custom_call_target="tpu_custom_call" | custom-call | tf_op jit(solution)/shard_map/pallas_call | solution.py:238
  78.2 18.0 %all_to_all.11 = bf16[64,16,128]{2,1,0:T(8,128)(2,1)S(1)} all-to-all(bf16[64,16,128]{2,1,0:T(8,128)(2,1)} %shard_map.61), channel_id=1, replica_groups=mesh['depth'=64,'space'=4] {'depth'}, dimensions={0} | all-to-all | bytes 524288 | tf_op jit(solution)/shard_map/all_to_all | solution.py:241
  96.3 3.4 %collective-permute-start.5 = (bf16[6,128,128]{2,1,0:T(8,128)(2,1)S(1)}, bf16[6,128,128]{2,1,0:T(8,128)(2,1)S(1)}, u32[]{:S(2)}, u32[]{:S(2)}) collective-permute-start(bf16[6,128,128]{2,1,0:T(8,128)(2,1)S(1)} %bitcast.24), channel_id=1, source_target_pairs={{0,1},{1,2},{2,3},{4,5},{5,6},{6,7},{8,9},{9,10},{10,11},{12,13},{... | collective-permute-start | bytes 589832 | tf_op jit(solution)/shard_map/ppermute | solution.py:193
  99.7 2.7 %collective-permute-start.6 = (bf16[6,128,128]{2,1,0:T(8,128)(2,1)S(1)}, bf16[6,128,128]{2,1,0:T(8,128)(2,1)S(1)}, u32[]{:S(2)}, u32[]{:S(2)}) collective-permute-start(bf16[6,128,128]{2,1,0:T(8,128)(2,1)S(1)} %bitcast.23), channel_id=1, source_target_pairs={{1,0},{2,1},{3,2},{5,4},{6,5},{7,6},{9,8},{10,9},{11,10},{13,12},{... | collective-permute-start | bytes 589832 | tf_op jit(solution)/shard_map/ppermute | solution.py:193
  102.3 2.7 %collective-permute-done.5.error_top_ref = bf16[6,128,128]{2,1,0:T(8,128)(2,1)S(1)} collective-permute-done((bf16[6,128,128]{2,1,0:T(8,128)(2,1)S(1)}, bf16[6,128,128]{2,1,0:T(8,128)(2,1)S(1)}, u32[]{:S(2)}, u32[]{:S(2)}) %collective-permute-start.5) | collective-permute-done | bytes 196640 | tf_op jit(solution)/shard_map/ppermute | solution.py:193
  105.0 3.1 %collective-permute-done.6.error_bottom_ref = bf16[6,128,128]{2,1,0:T(8,128)(2,1)S(1)} collective-permute-done((bf16[6,128,128]{2,1,0:T(8,128)(2,1)S(1)}, bf16[6,128,128]{2,1,0:T(8,128)(2,1)S(1)}, u32[]{:S(2)}, u32[]{:S(2)}) %collective-permute-start.6) | collective-permute-done | bytes 196640 | tf_op jit(solution)/shard_map/ppermute | solution.py:193
  108.2 0.0 copy-done.5
  108.2 0.0 copy-done.1
  108.2 0.0 copy-done.3
  108.2 0.0 copy-start.7
  108.2 0.9 copy-done.7
  109.1 0.0 copy-start.9
  109.1 0.9 copy-done.9
  110.1 0.0 copy-start.11
  110.1 0.9 copy-done.11
  111.0 8.4 %shard_map.62 = f32[4,8,128,128]{3,2,1,0:T(8,128)} custom-call(f32[3]{0:T(128)S(1)} %add_convert_fusion.flags_ref, f32[8,128,128]{2,1,0:T(8,128)S(1)} %bitcast.20, bf16[8,128,128]{2,1,0:T(8,128)(2,1)S(1)} %collective-permute-done.top_ref, bf16[8,128,128]{2,1,0:T(8,128)(2,1)S(1)} %collective-permute-done.1.bottom_ref, bf16[8,128,128]{2,1,0:T(8,128)(2,1)S(1)} %copy-done.11, ...), custom_call_target="tpu_custom_call" | custom-call | tf_op jit(solution)/shard_map/pallas_call | solution.py:175
  (1 shorter events, 0.0 us)
Async XLA Ops:
  1.7 9.9 %collective-permute-start.1 = (bf16[8,128,128]{2,1,0:T(8,128)(2,1)S(1)}, bf16[8,128,128]{2,1,0:T(8,128)(2,1)S(1)}, u32[]{:S(2)}, u32[]{:S(2)}) collective-permute-start(bf16[8,128,128]{2,1,0:T(8,128)(2,1)S(1)} %bitcast_convert_fusion), channel_id=1, source_target_pairs={{1,0},{2,1},{3,2},{5,4},{6,5},{7,6},{9,8},{10,9},{11,10},{13,12},{... | collective-permute-start | bytes 786440 | tf_op jit(solution)/shard_map/ppermute | solution.py:193
  5.9 8.3 %collective-permute-start = (bf16[8,128,128]{2,1,0:T(8,128)(2,1)S(1)}, bf16[8,128,128]{2,1,0:T(8,128)(2,1)S(1)}, u32[]{:S(2)}, u32[]{:S(2)}) collective-permute-start(bf16[8,128,128]{2,1,0:T(8,128)(2,1)S(1)} %bitcast_convert_fusion), channel_id=1, source_target_pairs={{0,1},{1,2},{2,3},{4,5},{5,6},{6,7},{8,9},{9,10},{10,11},{12,13},{... | collective-permute-start | bytes 786440 | tf_op jit(solution)/shard_map/ppermute | solution.py:193
  14.2 1.3 %copy-start = (bf16[4,9,128,128]{3,2,1,0:T(8,128)(2,1)S(1)}, bf16[4,9,128,128]{3,2,1,0:T(8,128)(2,1)}, u32[]{:S(2)}) copy-start(bf16[4,9,128,128]{3,2,1,0:T(8,128)(2,1)} %param.5) | copy-start | bytes 3538948
  15.4 1.3 %copy-start.2 = (bf16[4,9,128,128]{3,2,1,0:T(8,128)(2,1)S(1)}, bf16[4,9,128,128]{3,2,1,0:T(8,128)(2,1)}, u32[]{:S(2)}) copy-start(bf16[4,9,128,128]{3,2,1,0:T(8,128)(2,1)} %param.6) | copy-start | bytes 3538948
  16.7 1.0 copy-start.4
  27.3 8.6 %collective-permute-start.4 = (bf16[8,128,128]{2,1,0:T(8,128)(2,1)S(1)}, bf16[8,128,128]{2,1,0:T(8,128)(2,1)S(1)}, u32[]{:S(2)}, u32[]{:S(2)}) collective-permute-start(bf16[8,128,128]{2,1,0:T(8,128)(2,1)S(1)} %shard_map.59.y_ref), channel_id=1, source_target_pairs={{1,4},{2,5},{3,6},{5,8},{6,9},{7,10},{9,12},{10,13},{11,14},{13,16... | collective-permute-start | bytes 786440 | tf_op jit(solution)/shard_map/ppermute | solution.py:204
  28.6 12.0 %collective-permute-start.3 = (bf16[8,128,128]{2,1,0:T(8,128)(2,1)S(1)}, bf16[8,128,128]{2,1,0:T(8,128)(2,1)S(1)}, u32[]{:S(2)}, u32[]{:S(2)}) collective-permute-start(bf16[8,128,128]{2,1,0:T(8,128)(2,1)S(1)} %shard_map.59.y_ref), channel_id=1, source_target_pairs={{0,5},{1,6},{2,7},{4,9},{5,10},{6,11},{8,13},{9,14},{10,15},{12,17... | collective-permute-start | bytes 786440 | tf_op jit(solution)/shard_map/ppermute | solution.py:204
  33.9 6.7 %collective-permute-start.2 = (bf16[8,128,128]{2,1,0:T(8,128)(2,1)S(1)}, bf16[8,128,128]{2,1,0:T(8,128)(2,1)S(1)}, u32[]{:S(2)}, u32[]{:S(2)}) collective-permute-start(bf16[8,128,128]{2,1,0:T(8,128)(2,1)S(1)} %shard_map.59.y_ref), channel_id=1, source_target_pairs={{0,4},{1,5},{2,6},{3,7},{4,8},{5,9},{6,10},{7,11},{8,12},{9,13},{1... | collective-permute-start | bytes 786440 | tf_op jit(solution)/shard_map/ppermute | solution.py:204
  35.8 15.1 %copy-start.6 = (bf16[8,128,128]{2,1,0:T(8,128)(2,1)}, bf16[8,128,128]{2,1,0:T(8,128)(2,1)S(1)}, u32[]{:S(2)}) copy-start(bf16[8,128,128]{2,1,0:T(8,128)(2,1)S(1)} %collective-permute-done.4.got_bottom_ref) | copy-start | bytes 786436
  40.5 10.4 %copy-start.8 = (bf16[8,128,128]{2,1,0:T(8,128)(2,1)}, bf16[8,128,128]{2,1,0:T(8,128)(2,1)S(1)}, u32[]{:S(2)}) copy-start(bf16[8,128,128]{2,1,0:T(8,128)(2,1)S(1)} %collective-permute-done.3.got_top_ref) | copy-start | bytes 786436
  40.5 10.4 %copy-start.10 = (bf16[8,128,128]{2,1,0:T(8,128)(2,1)}, bf16[8,128,128]{2,1,0:T(8,128)(2,1)S(1)}, u32[]{:S(2)}) copy-start(bf16[8,128,128]{2,1,0:T(8,128)(2,1)S(1)} %collective-permute-done.2.got_ref) | copy-start | bytes 786436
  40.5 67.6 %copy-start.5 = (f32[1,8,128,128]{3,2,1,0:T(8,128)S(1)}, f32[1,8,128,128]{3,2,1,0:T(8,128)}, u32[]{:S(2)}) copy-start(f32[1,8,128,128]{3,2,1,0:T(8,128)} %param.4) | copy-start | bytes 1572868
  50.9 57.3 %copy-start.1 = (bf16[4,9,128,128]{3,2,1,0:T(8,128)(2,1)S(1)}, bf16[4,9,128,128]{3,2,1,0:T(8,128)(2,1)}, u32[]{:S(2)}) copy-start(bf16[4,9,128,128]{3,2,1,0:T(8,128)(2,1)} %param.5) | copy-start | bytes 3538948
  50.9 57.2 %copy-start.3 = (bf16[4,9,128,128]{3,2,1,0:T(8,128)(2,1)S(1)}, bf16[4,9,128,128]{3,2,1,0:T(8,128)(2,1)}, u32[]{:S(2)}) copy-start(bf16[4,9,128,128]{3,2,1,0:T(8,128)(2,1)} %param.6) | copy-start | bytes 3538948
  96.3 8.8 %collective-permute-start.5 = (bf16[6,128,128]{2,1,0:T(8,128)(2,1)S(1)}, bf16[6,128,128]{2,1,0:T(8,128)(2,1)S(1)}, u32[]{:S(2)}, u32[]{:S(2)}) collective-permute-start(bf16[6,128,128]{2,1,0:T(8,128)(2,1)S(1)} %bitcast.24), channel_id=1, source_target_pairs={{0,1},{1,2},{2,3},{4,5},{5,6},{6,7},{8,9},{9,10},{10,11},{12,13},{... | collective-permute-start | bytes 589832 | tf_op jit(solution)/shard_map/ppermute | solution.py:193
  99.7 8.5 %collective-permute-start.6 = (bf16[6,128,128]{2,1,0:T(8,128)(2,1)S(1)}, bf16[6,128,128]{2,1,0:T(8,128)(2,1)S(1)}, u32[]{:S(2)}, u32[]{:S(2)}) collective-permute-start(bf16[6,128,128]{2,1,0:T(8,128)(2,1)S(1)} %bitcast.23), channel_id=1, source_target_pairs={{1,0},{2,1},{3,2},{5,4},{6,5},{7,6},{9,8},{10,9},{11,10},{13,12},{... | collective-permute-start | bytes 589832 | tf_op jit(solution)/shard_map/ppermute | solution.py:193
  108.2 1.0 copy-start.7
  109.1 0.9 copy-start.9
  110.1 0.9 copy-start.11

commit v2 on v1

v2 whole, which is shorter than its diff:
```python
import functools

import jax
import jax.numpy as jnp
from jax import lax
from jax.experimental import pallas as pl
from jax.experimental.pallas import tpu as pltpu
from jax.sharding import PartitionSpec as P

GROUP = 1
W = 128
C = 128
VMEM_LIMIT = 32 * 2**20
CODE_SCALE = 86.0 / 18.0


def round_kernel(start_ref, rounded_ref, own_ref, sems):
    copies = [
        pltpu.make_async_copy(start_ref.at[row], own_ref.at[row], sems.at[row])
        for row in range(own_ref.shape[0])
    ]
    for copy in copies:
        copy.start()
    for row, copy in enumerate(copies):
        copy.wait()
        rounded_ref[row] = own_ref[row].astype(jnp.bfloat16)


def taps_kernel(firsts, seconds, wide, sems):
    copies = []
    for at in range(wide.shape[0]):
        source = (firsts, seconds)[at % 2].at[at // 2]
        for half in range(2):
            copies.append(
                pltpu.make_async_copy(
                    source,
                    wide.at[at, pl.ds(half * 3 * C, 9 * C), pl.ds(half * C, C)],
                    sems.at[at, half],
                )
            )
    for copy in copies:
        copy.start()
    blank = jnp.zeros((3 * C, C), jnp.bfloat16)
    for at in range(wide.shape[0]):
        wide[at, pl.ds(9 * C, 3 * C), pl.ds(0, C)] = blank
        wide[at, pl.ds(0, 3 * C), pl.ds(C, C)] = blank
    for copy in copies:
        copy.wait()


def spread(dst, pair, half, row):
    column = lax.broadcasted_iota(jnp.int32, (W, C), 0)
    before = jnp.where(column == 0, 0.0, pltpu.roll(row, 1, 0))
    after = jnp.where(column == W - 1, 0.0, pltpu.roll(row, W - 1, 0))
    for tap, part in enumerate((before, row, after)):
        dst[pair, :, pl.ds((half * 3 + tap) * C, C)] = part.astype(jnp.bfloat16)


def conv_pairs(src, wide, slot, pairs, emit):
    for first in range(0, pairs, GROUP):
        count = min(GROUP, pairs - first)
        low = src[pl.ds(first, count)].reshape(count * W, 6 * C)
        high = src[pl.ds(first + 1, count)].reshape(count * W, 6 * C)
        total = jnp.dot(
            low, wide[slot, pl.ds(0, 6 * C), :], preferred_element_type=jnp.float32
        ) + jnp.dot(high, wide[slot, pl.ds(6 * C, 6 * C), :], preferred_element_type=jnp.float32)
        for index in range(count):
            for half in range(2):
                emit(
                    first + index,
                    half,
                    total[index * W : (index + 1) * W, half * C : (half + 1) * C],
                )


def layers(count, halo, own, state, fields, wide, after_layer):
    slab = lax.axis_index("space")
    above = (slab > 0).astype(jnp.float32)
    below = (slab < lax.axis_size("space") - 1).astype(jnp.float32)

    def keep(row, value):
        if row < halo:
            return value * above
        if row >= halo + own:
            return value * below
        return value

    rows = own + 2 * halo
    for layer in range(count):
        offset = 2 * layer + 1

        def hidden(pair, half, value, offset=offset):
            row = offset + 2 * pair + half
            spread(fields[1], pair, half, keep(row, jnp.tanh(value)))

        conv_pairs(fields[0], wide, 2 * layer, (rows - 2 * offset) // 2, hidden)
        offset = 2 * layer + 2

        def outer(pair, half, value, offset=offset, last=layer == count - 1):
            row = offset + 2 * pair + half
            new = state[row] + 0.5 * keep(row, jnp.tanh(value))
            if not last:
                state[row] = new
                spread(fields[0], pair, half, new)
            if halo <= row < halo + own:
                after_layer(offset // 2, row - halo, new)

        conv_pairs(fields[1], wide, 2 * layer + 1, (rows - 2 * offset) // 2, outer)


def load_rows(halo, own, value_of, state, field):
    for row in range(own + 2 * halo):
        value = value_of(row)
        state[row] = value
        spread(field, row // 2, row % 2, value)


def first_kernel(own_ref, wide, top_ref, bottom_ref, y_ref, state, fa, fb):
    own = own_ref.shape[0]
    halo = top_ref.shape[0]

    def value_of(row):
        if row < halo:
            return top_ref[row].astype(jnp.float32)
        if row >= halo + own:
            return bottom_ref[row - halo - own].astype(jnp.float32)
        return own_ref[row - halo]

    load_rows(halo, own, value_of, state, fa)

    def after_layer(done, row, new):
        if 2 * done == halo:
            y_ref[row] = new.astype(jnp.bfloat16)

    layers(halo // 2, halo, own, state, (fa, fb), wide, after_layer)


def second_kernel(own_ref, wide, top_ref, bottom_ref, got_ref, got_top_ref, got_bottom_ref, y_ref,
                  relaxed_ref, code_ref, state, fa, fb, kept, out_sems):
    own = own_ref.shape[0]
    halo = top_ref.shape[0]
    begin = lax.axis_index("depth") == 0

    def value_of(row):
        if row < halo:
            return jnp.where(begin, top_ref[row], got_top_ref[row]).astype(jnp.float32)
        if row >= halo + own:
            at = row - halo - own
            return jnp.where(begin, bottom_ref[at], got_bottom_ref[at]).astype(jnp.float32)
        return jnp.where(begin, own_ref[row - halo], got_ref[row - halo].astype(jnp.float32))

    load_rows(halo, own, value_of, state, fa)
    outs = []

    def after_layer(done, row, new):
        if 2 * done == halo:
            kept[row] = new
            outs.append(pltpu.make_async_copy(kept.at[row], relaxed_ref.at[row], out_sems.at[row]))
            outs[-1].start()
            resid = new - y_ref[row].astype(jnp.float32)
            code_ref[row] = jnp.exp(resid * CODE_SCALE).astype(jnp.bfloat16)

    layers(halo // 2, halo, own, state, (fa, fb), wide, after_layer)
    for out in outs:
        out.wait()


def third_kernel(own_ref, wide, top_ref, bottom_ref, got_ref, got_top_ref, got_bottom_ref,
                 error_ref, error_top_ref, error_bottom_ref, states_ref,
                 state, fa, fb, kept, out_sems):
    own = own_ref.shape[0]
    halo = error_top_ref.shape[0]
    skip = top_ref.shape[0] - halo
    begin = lax.axis_index("depth") == 0
    outs = []

    def put(done, row, value):
        kept[done, row] = value
        outs.append(
            pltpu.make_async_copy(
                kept.at[done, row], states_ref.at[done, row], out_sems.at[done, row]
            )
        )
        outs[-1].start()

    def value_of(row):
        if row < halo:
            value = jnp.where(begin, top_ref[row + skip], got_top_ref[row + skip])
            return value.astype(jnp.float32) + error_top_ref[row].astype(jnp.float32)
        if row >= halo + own:
            at = row - halo - own
            value = jnp.where(begin, bottom_ref[at], got_bottom_ref[at])
            return value.astype(jnp.float32) + error_bottom_ref[at].astype(jnp.float32)
        at = row - halo
        value = jnp.where(begin, own_ref[at], got_ref[at].astype(jnp.float32))
        value = value + error_ref[at].astype(jnp.float32)
        put(0, at, value)
        return value

    load_rows(halo, own, value_of, state, fa)
    layers(halo // 2, halo, own, state, (fa, fb), wide, put)
    for out in outs:
        out.wait()


def scan_kernel(gain_ref, code_ref, error_ref):
    count = error_ref.shape[0]
    error_ref[0] = jnp.zeros(error_ref.shape[1:], error_ref.dtype)
    carry = jnp.zeros(error_ref.shape[1:], jnp.float32)
    for j in range(1, count):
        resid = jnp.log(code_ref[j - 1].astype(jnp.float32)) * (1 / CODE_SCALE)
        carry = gain_ref[pl.ds(j, 1), :] * carry + resid
        error_ref[j] = carry.astype(error_ref.dtype)


def on_chip(count):
    return [pl.BlockSpec(memory_space=pltpu.VMEM)] * count


def sweep(kernel, halo, own, outs, args, kept=None):
    rows = own + 2 * halo
    scratch = [
        pltpu.VMEM((rows, W, C), jnp.float32),
        pltpu.VMEM((rows // 2, W, 6 * C), jnp.bfloat16),
        pltpu.VMEM((rows // 2, W, 6 * C), jnp.bfloat16),
    ]
    out_specs = on_chip(len(outs))
    if kept is not None:
        scratch += [pltpu.VMEM(outs[0].shape, jnp.float32), pltpu.SemaphoreType.DMA(kept)]
        out_specs[0] = pl.BlockSpec(memory_space=pltpu.HBM)
    flops = 2 * 9 * C * C * W * sum(rows - 2 * k for k in range(1, halo + 1))
    return pl.pallas_call(
        kernel,
        out_shape=outs,
        in_specs=on_chip(len(args)),
        out_specs=tuple(out_specs),
        scratch_shapes=scratch,
        compiler_params=pltpu.CompilerParams(vmem_limit_bytes=VMEM_LIMIT),
        cost_estimate=pl.CostEstimate(flops=flops, bytes_accessed=2**22, transcendentals=0),
    )(*args)


def neighbour(block, up):
    count = lax.axis_size("space")
    route = [(i, i + 1) if up else (i + 1, i) for i in range(count - 1)]
    return lax.ppermute(block, "space", route)


def from_previous(block, shift):
    depth, space = lax.axis_size("depth"), lax.axis_size("space")
    route = [
        (d * space + s + shift, (d + 1) * space + s)
        for d in range(depth - 1)
        for s in range(space)
        if 0 <= s + shift < space
    ]
    return lax.ppermute(block, ("depth", "space"), route)


def shards(coarse_states, first_kernels, second_kernels, coarse_channel_gain):
    here = first_kernels.shape[0]
    start = coarse_states[0]
    own = start.shape[0]
    depth = lax.axis_size("depth")
    wide_field = jax.ShapeDtypeStruct(start.shape, jnp.float32)
    field = jax.ShapeDtypeStruct(start.shape, jnp.bfloat16)
    hbm = pl.BlockSpec(memory_space=pltpu.HBM)

    halo = 2 * here
    rounded, start = pl.pallas_call(
        round_kernel,
        out_shape=(field, wide_field),
        in_specs=[hbm],
        out_specs=tuple(on_chip(2)),
        scratch_shapes=[pltpu.SemaphoreType.DMA((own,))],
        compiler_params=pltpu.CompilerParams(vmem_limit_bytes=VMEM_LIMIT),
    )(start)
    top = neighbour(rounded[own - halo :], True)
    bottom = neighbour(rounded[:halo], False)
    wide = pl.pallas_call(
        taps_kernel,
        out_shape=jax.ShapeDtypeStruct((2 * here, 12 * C, 2 * C), jnp.bfloat16),
        in_specs=[hbm, hbm],
        out_specs=pl.BlockSpec(memory_space=pltpu.VMEM),
        scratch_shapes=[pltpu.SemaphoreType.DMA((2 * here, 2))],
        compiler_params=pltpu.CompilerParams(vmem_limit_bytes=VMEM_LIMIT),
        cost_estimate=pl.CostEstimate(flops=0, bytes_accessed=2**24, transcendentals=0),
    )(first_kernels.reshape(here, 9 * C, C), second_kernels.reshape(here, 9 * C, C))

    (y_first,) = sweep(first_kernel, halo, own, (field,), (start, wide, top, bottom))
    got_top = from_previous(y_first[own - halo :], -1)
    got = from_previous(y_first, 0)
    got_bottom = from_previous(y_first[:halo], 1)
    before = (start, wide, top, bottom, got, got_top, got_bottom)
    relaxed, code = sweep(
        second_kernel, halo, own, (wide_field, field), before + (y_first,), kept=(own,)
    )
    pixels = own * W // depth
    columns = lax.all_to_all(code.reshape(depth, pixels, C), "depth", 0, 0)
    errors = pl.pallas_call(
        scan_kernel,
        out_shape=jax.ShapeDtypeStruct(columns.shape, jnp.bfloat16),
        in_specs=on_chip(2),
        out_specs=on_chip(1)[0],
        compiler_params=pltpu.CompilerParams(vmem_limit_bytes=VMEM_LIMIT),
    )(coarse_channel_gain, columns)
    error = lax.all_to_all(errors, "depth", 0, 0).reshape(start.shape)
    near = halo - 2
    error_top = neighbour(error[own - near :], True)
    error_bottom = neighbour(error[:near], False)
    (states,) = sweep(
        third_kernel, near, own, (jax.ShapeDtypeStruct((here,) + start.shape, jnp.float32),),
        before + (error, error_top, error_bottom), kept=(here, own),
    )
    return states, relaxed[None]


def solution(mesh):
    placed = (
        P("depth", "space", None, None),
        P("depth", None, None, None),
        P("depth", None, None, None),
        P(),
    )
    return jax.shard_map(
        shards,
        mesh=mesh,
        in_specs=placed,
        out_specs=(P("depth", "space", None, None), P("depth", "space", None, None)),
        check_vma=False,
    )
```

time: 120 us -> 104 us (0.87)
  Pallas kernels: 30 us -> 22.3 us
  waiting for transfers between devices: 16.7 us -> 13.1 us
  local copies, waits for them, and re-layouts: 6.49 us -> 3.62 us
    pallas_call x3 -> x5, Pallas kernels: 28.2 us -> 22.1 us  [the longest x3 20.2 us: sweep(): pl.pallas_call(kernel, out_shape=outs, in_specs=on_chip(len(args)), out_s...]
    ppermute x4, waiting for transfers between devices: 12.1 us -> 8.41 us  [neighbour(): return lax.ppermute(block, 'space', route)]
    unnamed x24 -> x8, local copies, waits for them, and re-layouts: 6.45 us -> 3.58 us
    pallas_call x1, Pallas kernels: 1.8 us -> 0.14 us  [shards(): pl.pallas_call(scan_kernel, out_shape=jax.ShapeDtypeStruct(columns.shape,...]
  transfers between devices with their start and end apart: 7 -> 7, of which waited for: 5 -> 5; matrix products, arithmetic and copies ran while one was open for 0% -> 0% of each run, Pallas kernels for 0% -> 1%
where the time goes in v2:
time: 104 us
  blocking collectives  43 us (41%)
  Pallas kernels  22.3 us (21%)
  starting transfers between devices  20.7 us (20%)
  waiting for transfers between devices  13.1 us (13%)
  local copies, waits for them, and re-layouts  3.62 us (3%)
    all_to_all x1, blocking collectives, shards(): columns = lax.all_to_all(code.reshape(depth, pixels, C), 'depth', 0, 0)  25.2 us
    pallas_call x3, Pallas kernels, sweep(): pl.pallas_call(kernel, out_shape=outs, in_specs=on_chip(len(args)), out_s...  20.2 us
    all_to_all x1, blocking collectives, shards(): error = lax.all_to_all(errors, 'depth', 0, 0).reshape(start.shape)  17.8 us
    ppermute x4, starting transfers between devices, neighbour(): return lax.ppermute(block, 'space', route)  12.2 us
    ppermute x3, starting transfers between devices, from_previous(): return lax.ppermute(block, ('depth', 'space'), route)  8.55 us
    ppermute x4, waiting for transfers between devices, neighbour(): return lax.ppermute(block, 'space', route)  8.41 us
    ppermute x3, waiting for transfers between devices, from_previous(): return lax.ppermute(block, ('depth', 'space'), route)  4.69 us
    unnamed x8, local copies, waits for them, and re-layouts  3.58 us
  transfers between devices with their start and end apart: 7, of which 5 were waited for; matrix products, arithmetic and copies ran while one was open for 0% of the time, Pallas kernels for 1%

profile of v2, /device:TPU:2, one launch (start us, length us, event | category | flops | bytes accessed | tf_op | source)
XLA Modules:
  0.0 103.7 jit_solution(17971752410323303587)
XLA Ops:
  0.6 0.0 copy-start.2
  0.6 1.0 copy-done.2
  1.7 0.8 shard_map.59
  2.4 4.2 %collective-permute-start.1 = (bf16[8,128,128]{2,1,0:T(8,128)(2,1)S(1)}, bf16[8,128,128]{2,1,0:T(8,128)(2,1)S(1)}, u32[]{:S(2)}, u32[]{:S(2)}) collective-permute-start(bf16[8,128,128]{2,1,0:T(8,128)(2,1)S(1)} %get-tuple-element.7), channel_id=1, source_target_pairs={{1,0},{2,1},{3,2},{5,4},{6,5},{7,6},{9,8},{10,9},{11,10},{13,12},{... | collective-permute-start | bytes 786440 | tf_op jit(solution)/shard_map/ppermute | solution.py:246
  6.6 1.9 %collective-permute-start = (bf16[8,128,128]{2,1,0:T(8,128)(2,1)S(1)}, bf16[8,128,128]{2,1,0:T(8,128)(2,1)S(1)}, u32[]{:S(2)}, u32[]{:S(2)}) collective-permute-start(bf16[8,128,128]{2,1,0:T(8,128)(2,1)S(1)} %get-tuple-element.7), channel_id=1, source_target_pairs={{0,1},{1,2},{2,3},{4,5},{5,6},{6,7},{8,9},{9,10},{10,11},{12,13},{... | collective-permute-start | bytes 786440 | tf_op jit(solution)/shard_map/ppermute | solution.py:246
  8.6 0.0 copy-start
  8.6 1.3 %copy-done = bf16[4,9,128,128]{3,2,1,0:T(8,128)(2,1)S(1)} copy-done((bf16[4,9,128,128]{3,2,1,0:T(8,128)(2,1)S(1)}, bf16[4,9,128,128]{3,2,1,0:T(8,128)(2,1)}, u32[]{:S(2)}) %copy-start) | copy-done | bytes 1179672
  9.8 0.0 copy-start.1
  9.8 1.3 %copy-done.1 = bf16[4,9,128,128]{3,2,1,0:T(8,128)(2,1)S(1)} copy-done((bf16[4,9,128,128]{3,2,1,0:T(8,128)(2,1)S(1)}, bf16[4,9,128,128]{3,2,1,0:T(8,128)(2,1)}, u32[]{:S(2)}) %copy-start.1) | copy-done | bytes 1179672
  11.1 1.2 %shard_map.60.wide = bf16[8,1536,256]{2,1,0:T(8,128)(2,1)S(1)} custom-call(bf16[4,1152,128]{2,1,0:T(8,128)(2,1)S(1)} %bitcast.9, bf16[4,1152,128]{2,1,0:T(8,128)(2,1)S(1)} %bitcast.10), custom_call_target="tpu_custom_call" | custom-call | bytes 16777216 | tf_op jit(solution)/shard_map/pallas_call | solution.py:280
  12.3 0.1 collective-permute-done.1.bottom_ref
  12.4 2.5 %collective-permute-done.top_ref = bf16[8,128,128]{2,1,0:T(8,128)(2,1)S(1)} collective-permute-done((bf16[8,128,128]{2,1,0:T(8,128)(2,1)S(1)}, bf16[8,128,128]{2,1,0:T(8,128)(2,1)S(1)}, u32[]{:S(2)}, u32[]{:S(2)}) %collective-permute-start) | collective-permute-done | bytes 262176 | tf_op jit(solution)/shard_map/ppermute | solution.py:246
  14.9 6.9 %shard_map.61.y_ref = bf16[8,128,128]{2,1,0:T(8,128)(2,1)S(1)} custom-call(f32[8,128,128]{2,1,0:T(8,128)S(1)} %get-tuple-element.6.own_ref, bf16[8,1536,256]{2,1,0:T(8,128)(2,1)S(1)} %shard_map.60.wide, bf16[8,128,128]{2,1,0:T(8,128)(2,1)S(1)} %collective-permute-done.top_ref, bf16[8,128,128]{2,1,0:T(8,128)(2,1)S(1)} %collective-permute-done.1.bottom_ref), custom_call_target="tpu_custom_call" | custom-call | flops 4529848320 | bytes 4194304 | tf_op jit(solution)/shard_map/pallas_call | solution.py:232
  21.8 0.0 copy-start.3
  21.8 1.3 %collective-permute-start.4 = (bf16[8,128,128]{2,1,0:T(8,128)(2,1)S(1)}, bf16[8,128,128]{2,1,0:T(8,128)(2,1)S(1)}, u32[]{:S(2)}, u32[]{:S(2)}) collective-permute-start(bf16[8,128,128]{2,1,0:T(8,128)(2,1)S(1)} %shard_map.61.y_ref), channel_id=1, source_target_pairs={{1,4},{2,5},{3,6},{5,8},{6,9},{7,10},{9,12},{10,13},{11,14},{13,16... | collective-permute-start | bytes 786440 | tf_op jit(solution)/shard_map/ppermute | solution.py:257
  23.1 5.3 %collective-permute-start.3 = (bf16[8,128,128]{2,1,0:T(8,128)(2,1)S(1)}, bf16[8,128,128]{2,1,0:T(8,128)(2,1)S(1)}, u32[]{:S(2)}, u32[]{:S(2)}) collective-permute-start(bf16[8,128,128]{2,1,0:T(8,128)(2,1)S(1)} %shard_map.61.y_ref), channel_id=1, source_target_pairs={{0,5},{1,6},{2,7},{4,9},{5,10},{6,11},{8,13},{9,14},{10,15},{12,17... | collective-permute-start | bytes 786440 | tf_op jit(solution)/shard_map/ppermute | solution.py:257
  28.4 2.0 %collective-permute-start.2 = (bf16[8,128,128]{2,1,0:T(8,128)(2,1)S(1)}, bf16[8,128,128]{2,1,0:T(8,128)(2,1)S(1)}, u32[]{:S(2)}, u32[]{:S(2)}) collective-permute-start(bf16[8,128,128]{2,1,0:T(8,128)(2,1)S(1)} %shard_map.61.y_ref), channel_id=1, source_target_pairs={{0,4},{1,5},{2,6},{3,7},{4,8},{5,9},{6,10},{7,11},{8,12},{9,13},{1... | collective-permute-start | bytes 786440 | tf_op jit(solution)/shard_map/ppermute | solution.py:257
  30.3 0.0 collective-permute-done.4.got_bottom_ref
  30.4 4.7 %collective-permute-done.3.got_top_ref = bf16[8,128,128]{2,1,0:T(8,128)(2,1)S(1)} collective-permute-done((bf16[8,128,128]{2,1,0:T(8,128)(2,1)S(1)}, bf16[8,128,128]{2,1,0:T(8,128)(2,1)S(1)}, u32[]{:S(2)}, u32[]{:S(2)}) %collective-permute-start.3) | collective-permute-done | bytes 262176 | tf_op jit(solution)/shard_map/ppermute | solution.py:257
  35.0 0.0 collective-permute-done.2.got_ref
  35.0 7.7 %shard_map.62 = (f32[8,128,128]{2,1,0:T(8,128)}, bf16[8,128,128]{2,1,0:T(8,128)(2,1)S(1)}) custom-call(f32[8,128,128]{2,1,0:T(8,128)S(1)} %get-tuple-element.6.own_ref, bf16[8,1536,256]{2,1,0:T(8,128)(2,1)S(1)} %shard_map.60.wide, bf16[8,128,128]{2,1,0:T(8,128)(2,1)S(1)} %collective-permute-done.top_ref, ...), custom_call_target="tpu_custom_call" | custom-call | flops 4529848320 | bytes 4194304 | tf_op jit(solution)/shard_map/pallas_call | solution.py:232
  42.8 25.2 %all_to_all.10.code_ref = bf16[64,16,128]{2,1,0:T(8,128)(2,1)S(1)} all-to-all(bf16[64,16,128]{2,1,0:T(8,128)(2,1)S(1)} %bitcast.12), channel_id=1, replica_groups=mesh['depth'=64,'space'=4] {'depth'}, dimensions={0} | all-to-all | bytes 524288 | tf_op jit(solution)/shard_map/all_to_all | solution.py:299
  68.0 0.0 copy-done.3
  68.0 0.1 shard_map.63
  68.1 17.8 %all_to_all.11 = bf16[64,16,128]{2,1,0:T(8,128)(2,1)S(1)} all-to-all(bf16[64,16,128]{2,1,0:T(8,128)(2,1)S(1)} %shard_map.63), channel_id=1, replica_groups=mesh['depth'=64,'space'=4] {'depth'}, dimensions={0} | all-to-all | bytes 524288 | tf_op jit(solution)/shard_map/all_to_all | solution.py:307
  86.0 3.4 %collective-permute-start.5 = (bf16[6,128,128]{2,1,0:T(8,128)(2,1)S(1)}, bf16[6,128,128]{2,1,0:T(8,128)(2,1)S(1)}, u32[]{:S(2)}, u32[]{:S(2)}) collective-permute-start(bf16[6,128,128]{2,1,0:T(8,128)(2,1)S(1)} %bitcast.14), channel_id=1, source_target_pairs={{0,1},{1,2},{2,3},{4,5},{5,6},{6,7},{8,9},{9,10},{10,11},{12,13},{... | collective-permute-start | bytes 589832 | tf_op jit(solution)/shard_map/ppermute | solution.py:246
  89.4 2.7 %collective-permute-start.6 = (bf16[6,128,128]{2,1,0:T(8,128)(2,1)S(1)}, bf16[6,128,128]{2,1,0:T(8,128)(2,1)S(1)}, u32[]{:S(2)}, u32[]{:S(2)}) collective-permute-start(bf16[6,128,128]{2,1,0:T(8,128)(2,1)S(1)} %bitcast.13), channel_id=1, source_target_pairs={{1,0},{2,1},{3,2},{5,4},{6,5},{7,6},{9,8},{10,9},{11,10},{13,12},{... | collective-permute-start | bytes 589832 | tf_op jit(solution)/shard_map/ppermute | solution.py:246
  92.1 2.7 %collective-permute-done.5.error_top_ref = bf16[6,128,128]{2,1,0:T(8,128)(2,1)S(1)} collective-permute-done((bf16[6,128,128]{2,1,0:T(8,128)(2,1)S(1)}, bf16[6,128,128]{2,1,0:T(8,128)(2,1)S(1)}, u32[]{:S(2)}, u32[]{:S(2)}) %collective-permute-start.5) | collective-permute-done | bytes 196640 | tf_op jit(solution)/shard_map/ppermute | solution.py:246
  94.8 3.1 %collective-permute-done.6.error_bottom_ref = bf16[6,128,128]{2,1,0:T(8,128)(2,1)S(1)} collective-permute-done((bf16[6,128,128]{2,1,0:T(8,128)(2,1)S(1)}, bf16[6,128,128]{2,1,0:T(8,128)(2,1)S(1)}, u32[]{:S(2)}, u32[]{:S(2)}) %collective-permute-start.6) | collective-permute-done | bytes 196640 | tf_op jit(solution)/shard_map/ppermute | solution.py:246
  97.9 5.6 %shard_map.64 = f32[4,8,128,128]{3,2,1,0:T(8,128)} custom-call(f32[8,128,128]{2,1,0:T(8,128)S(1)} %get-tuple-element.6.own_ref, bf16[8,1536,256]{2,1,0:T(8,128)(2,1)S(1)} %shard_map.60.wide, bf16[8,128,128]{2,1,0:T(8,128)(2,1)S(1)} %collective-permute-done.top_ref, bf16[8,128,128]{2,1,0:T(8,128)(2,1)S(1)} %collective-permute-done.1.bottom_ref, ...), custom_call_target="tpu_custom_call" | custom-call | flops 2944401408 | bytes 4194304 | tf_op jit(solution)/shard_map/pallas_call | solution.py:232
  (1 shorter events, 0.0 us)
Async XLA Ops:
  0.6 1.0 %copy-start.2 = (f32[1,8,128,128]{3,2,1,0:T(8,128)S(1)}, f32[1,8,128,128]{3,2,1,0:T(8,128)}, u32[]{:S(2)}) copy-start(f32[1,8,128,128]{3,2,1,0:T(8,128)} %param.4) | copy-start | bytes 1572868
  2.4 9.9 %collective-permute-start.1 = (bf16[8,128,128]{2,1,0:T(8,128)(2,1)S(1)}, bf16[8,128,128]{2,1,0:T(8,128)(2,1)S(1)}, u32[]{:S(2)}, u32[]{:S(2)}) collective-permute-start(bf16[8,128,128]{2,1,0:T(8,128)(2,1)S(1)} %get-tuple-element.7), channel_id=1, source_target_pairs={{1,0},{2,1},{3,2},{5,4},{6,5},{7,6},{9,8},{10,9},{11,10},{13,12},{... | collective-permute-start | bytes 786440 | tf_op jit(solution)/shard_map/ppermute | solution.py:246
  6.6 8.3 %collective-permute-start = (bf16[8,128,128]{2,1,0:T(8,128)(2,1)S(1)}, bf16[8,128,128]{2,1,0:T(8,128)(2,1)S(1)}, u32[]{:S(2)}, u32[]{:S(2)}) collective-permute-start(bf16[8,128,128]{2,1,0:T(8,128)(2,1)S(1)} %get-tuple-element.7), channel_id=1, source_target_pairs={{0,1},{1,2},{2,3},{4,5},{5,6},{6,7},{8,9},{9,10},{10,11},{12,13},{... | collective-permute-start | bytes 786440 | tf_op jit(solution)/shard_map/ppermute | solution.py:246
  8.6 1.3 %copy-start = (bf16[4,9,128,128]{3,2,1,0:T(8,128)(2,1)S(1)}, bf16[4,9,128,128]{3,2,1,0:T(8,128)(2,1)}, u32[]{:S(2)}) copy-start(bf16[4,9,128,128]{3,2,1,0:T(8,128)(2,1)} %param.5) | copy-start | bytes 3538948
  9.8 1.3 %copy-start.1 = (bf16[4,9,128,128]{3,2,1,0:T(8,128)(2,1)S(1)}, bf16[4,9,128,128]{3,2,1,0:T(8,128)(2,1)}, u32[]{:S(2)}) copy-start(bf16[4,9,128,128]{3,2,1,0:T(8,128)(2,1)} %param.6) | copy-start | bytes 3538948
  21.8 46.2 %copy-start.3 = (f32[64,128]{1,0:T(8,128)S(1)}, f32[64,128]{1,0:T(8,128)}, u32[]{:S(2)}) copy-start(f32[64,128]{1,0:T(8,128)} %gain_ref.1) | copy-start | bytes 98308
  21.8 8.6 %collective-permute-start.4 = (bf16[8,128,128]{2,1,0:T(8,128)(2,1)S(1)}, bf16[8,128,128]{2,1,0:T(8,128)(2,1)S(1)}, u32[]{:S(2)}, u32[]{:S(2)}) collective-permute-start(bf16[8,128,128]{2,1,0:T(8,128)(2,1)S(1)} %shard_map.61.y_ref), channel_id=1, source_target_pairs={{1,4},{2,5},{3,6},{5,8},{6,9},{7,10},{9,12},{10,13},{11,14},{13,16... | collective-permute-start | bytes 786440 | tf_op jit(solution)/shard_map/ppermute | solution.py:257
  23.1 12.0 %collective-permute-start.3 = (bf16[8,128,128]{2,1,0:T(8,128)(2,1)S(1)}, bf16[8,128,128]{2,1,0:T(8,128)(2,1)S(1)}, u32[]{:S(2)}, u32[]{:S(2)}) collective-permute-start(bf16[8,128,128]{2,1,0:T(8,128)(2,1)S(1)} %shard_map.61.y_ref), channel_id=1, source_target_pairs={{0,5},{1,6},{2,7},{4,9},{5,10},{6,11},{8,13},{9,14},{10,15},{12,17... | collective-permute-start | bytes 786440 | tf_op jit(solution)/shard_map/ppermute | solution.py:257
  28.4 6.7 %collective-permute-start.2 = (bf16[8,128,128]{2,1,0:T(8,128)(2,1)S(1)}, bf16[8,128,128]{2,1,0:T(8,128)(2,1)S(1)}, u32[]{:S(2)}, u32[]{:S(2)}) collective-permute-start(bf16[8,128,128]{2,1,0:T(8,128)(2,1)S(1)} %shard_map.61.y_ref), channel_id=1, source_target_pairs={{0,4},{1,5},{2,6},{3,7},{4,8},{5,9},{6,10},{7,11},{8,12},{9,13},{1... | collective-permute-start | bytes 786440 | tf_op jit(solution)/shard_map/ppermute | solution.py:257
  86.0 8.8 %collective-permute-start.5 = (bf16[6,128,128]{2,1,0:T(8,128)(2,1)S(1)}, bf16[6,128,128]{2,1,0:T(8,128)(2,1)S(1)}, u32[]{:S(2)}, u32[]{:S(2)}) collective-permute-start(bf16[6,128,128]{2,1,0:T(8,128)(2,1)S(1)} %bitcast.14), channel_id=1, source_target_pairs={{0,1},{1,2},{2,3},{4,5},{5,6},{6,7},{8,9},{9,10},{10,11},{12,13},{... | collective-permute-start | bytes 589832 | tf_op jit(solution)/shard_map/ppermute | solution.py:246
  89.4 8.5 %collective-permute-start.6 = (bf16[6,128,128]{2,1,0:T(8,128)(2,1)S(1)}, bf16[6,128,128]{2,1,0:T(8,128)(2,1)S(1)}, u32[]{:S(2)}, u32[]{:S(2)}) collective-permute-start(bf16[6,128,128]{2,1,0:T(8,128)(2,1)S(1)} %bitcast.13), channel_id=1, source_target_pairs={{1,0},{2,1},{3,2},{5,4},{6,5},{7,6},{9,8},{10,9},{11,10},{13,12},{... | collective-permute-start | bytes 589832 | tf_op jit(solution)/shard_map/ppermute | solution.py:246

commit v3 on v2

--- a/solution.py
+++ b/solution.py
@@ -11,23 +11,20 @@
 W = 128
 C = 128
 VMEM_LIMIT = 32 * 2**20
-CODE_SCALE = 86.0 / 18.0
-
-
-def round_kernel(start_ref, rounded_ref, own_ref, sems):
-    copies = [
-        pltpu.make_async_copy(start_ref.at[row], own_ref.at[row], sems.at[row])
-        for row in range(own_ref.shape[0])
-    ]
-    for copy in copies:
-        copy.start()
-    for row, copy in enumerate(copies):
-        copy.wait()
-        rounded_ref[row] = own_ref[row].astype(jnp.bfloat16)
-
-
-def taps_kernel(firsts, seconds, wide, sems):
-    copies = []
+RESID_SCALE = 86.0 / 18.0
+JOINED_SCALE = 86.0 / 36.0
+
+
+def encode(value, scale):
+    return jnp.exp(value * scale).astype(jnp.bfloat16)
+
+
+def decode(code, scale):
+    return jnp.log(code.astype(jnp.float32)) * (1 / scale)
+
+
+def taps_kernel(start_ref, firsts, seconds, own_ref, wide, sems, own_sem):
+    copies = [pltpu.make_async_copy(start_ref, own_ref, own_sem)]
     for at in range(wide.shape[0]):
         source = (firsts, seconds)[at % 2].at[at // 2]
         for half in range(2):
@@ -136,7 +133,7 @@
 
 
 def second_kernel(own_ref, wide, top_ref, bottom_ref, got_ref, got_top_ref, got_bottom_ref, y_ref,
-                  relaxed_ref, code_ref, state, fa, fb, kept, out_sems):
+                  relaxed_ref, code_ref, state, fa, fb):
     own = own_ref.shape[0]
     halo = top_ref.shape[0]
     begin = lax.axis_index("depth") == 0
@@ -150,29 +147,25 @@
         return jnp.where(begin, own_ref[row - halo], got_ref[row - halo].astype(jnp.float32))
 
     load_rows(halo, own, value_of, state, fa)
-    outs = []
 
     def after_layer(done, row, new):
         if 2 * done == halo:
-            kept[row] = new
-            outs.append(pltpu.make_async_copy(kept.at[row], relaxed_ref.at[row], out_sems.at[row]))
-            outs[-1].start()
+            relaxed_ref[row] = new
             resid = new - y_ref[row].astype(jnp.float32)
-            code_ref[row] = jnp.exp(resid * CODE_SCALE).astype(jnp.bfloat16)
+            code_ref[row] = encode(resid, RESID_SCALE)
 
     layers(halo // 2, halo, own, state, (fa, fb), wide, after_layer)
-    for out in outs:
-        out.wait()
 
 
 def third_kernel(own_ref, wide, top_ref, bottom_ref, got_ref, got_top_ref, got_bottom_ref,
-                 error_ref, error_top_ref, error_bottom_ref, states_ref,
-                 state, fa, fb, kept, out_sems):
+                 error_ref, error_top_ref, error_bottom_ref, y_ref, states_ref, relaxed_ref,
+                 state, fa, fb, kept, out_sems, relaxed_sem):
     own = own_ref.shape[0]
     halo = error_top_ref.shape[0]
     skip = top_ref.shape[0] - halo
     begin = lax.axis_index("depth") == 0
-    outs = []
+    outs = [pltpu.make_async_copy(y_ref, relaxed_ref, relaxed_sem)]
+    outs[0].start()
 
     def put(done, row, value):
         kept[done, row] = value
@@ -203,18 +196,57 @@
         out.wait()
 
 
-def scan_kernel(gain_ref, code_ref, error_ref):
+def join_kernel(gain_ref, codes_ref, joined_ref):
+    depth = lax.axis_index("depth")
+    rows = joined_ref.shape[0]
+    first = lax.rem(depth, 2) * rows
+    later = lax.min(depth - lax.rem(depth, 2) + 2, gain_ref.shape[0] - 1)
+    gain = gain_ref[pl.ds(later, 1), :]
+    for row in range(rows):
+        early = decode(codes_ref[0, first + row], RESID_SCALE)
+        late = decode(codes_ref[1, first + row], RESID_SCALE)
+        joined_ref[row] = encode(gain * early + late, JOINED_SCALE)
+
+
+def scan_kernel(gain_ref, joined_ref, error_ref):
     count = error_ref.shape[0]
-    error_ref[0] = jnp.zeros(error_ref.shape[1:], error_ref.dtype)
     carry = jnp.zeros(error_ref.shape[1:], jnp.float32)
-    for j in range(1, count):
-        resid = jnp.log(code_ref[j - 1].astype(jnp.float32)) * (1 / CODE_SCALE)
-        carry = gain_ref[pl.ds(j, 1), :] * carry + resid
-        error_ref[j] = carry.astype(error_ref.dtype)
+    error_ref[0] = carry.astype(error_ref.dtype)
+    for k in range(count - 1):
+        gain = gain_ref[pl.ds(2 * k + 1, 1), :] * gain_ref[pl.ds(2 * k + 2, 1), :]
+        carry = gain * carry + decode(joined_ref[k], JOINED_SCALE)
+        error_ref[k + 1] = carry.astype(error_ref.dtype)
+
+
+def split_kernel(gain_ref, codes_ref, pair_ref, error_ref, upper_ref, lower_ref):
+    depth = lax.axis_index("depth")
+    rows = error_ref.shape[0]
+    near = upper_ref.shape[0]
+    odd = lax.rem(depth, 2) == 1
+    gain = gain_ref[pl.ds(depth, 1), :]
+    for row in range(rows):
+        error = pair_ref[row].astype(jnp.float32)
+        own = gain * error + decode(codes_ref[0, row], RESID_SCALE)
+        value = jnp.where(odd, own, error).astype(jnp.bfloat16)
+        error_ref[row] = value
+        if row < near:
+            upper_ref[row] = value
+        if row >= rows - near:
+            lower_ref[row - rows + near] = value
 
 
 def on_chip(count):
     return [pl.BlockSpec(memory_space=pltpu.VMEM)] * count
+
+
+def small(kernel, outs, *args):
+    return pl.pallas_call(
+        kernel,
+        out_shape=outs,
+        in_specs=on_chip(len(args)),
+        out_specs=jax.tree.map(lambda _: on_chip(1)[0], outs),
+        compiler_params=pltpu.CompilerParams(vmem_limit_bytes=VMEM_LIMIT),
+    )(*args)
 
 
 def sweep(kernel, halo, own, outs, args, kept=None):
@@ -226,8 +258,12 @@
     ]
     out_specs = on_chip(len(outs))
     if kept is not None:
-        scratch += [pltpu.VMEM(outs[0].shape, jnp.float32), pltpu.SemaphoreType.DMA(kept)]
-        out_specs[0] = pl.BlockSpec(memory_space=pltpu.HBM)
+        scratch += [
+            pltpu.VMEM(outs[0].shape, jnp.float32),
+            pltpu.SemaphoreType.DMA(kept),
+            pltpu.SemaphoreType.DMA,
+        ]
+        out_specs = [pl.BlockSpec(memory_space=pltpu.HBM)] * len(outs)
     flops = 2 * 9 * C * C * W * sum(rows - 2 * k for k in range(1, halo + 1))
     return pl.pallas_call(
         kernel,
@@ -267,50 +303,53 @@
     hbm = pl.BlockSpec(memory_space=pltpu.HBM)
 
     halo = 2 * here
-    rounded, start = pl.pallas_call(
-        round_kernel,
-        out_shape=(field, wide_field),
-        in_specs=[hbm],
-        out_specs=tuple(on_chip(2)),
-        scratch_shapes=[pltpu.SemaphoreType.DMA((own,))],
-        compiler_params=pltpu.CompilerParams(vmem_limit_bytes=VMEM_LIMIT),
-    )(start)
+    rounded = start.astype(jnp.bfloat16)
     top = neighbour(rounded[own - halo :], True)
     bottom = neighbour(rounded[:halo], False)
-    wide = pl.pallas_call(
+    start, wide = pl.pallas_call(
         taps_kernel,
-        out_shape=jax.ShapeDtypeStruct((2 * here, 12 * C, 2 * C), jnp.bfloat16),
-        in_specs=[hbm, hbm],
-        out_specs=pl.BlockSpec(memory_space=pltpu.VMEM),
-        scratch_shapes=[pltpu.SemaphoreType.DMA((2 * here, 2))],
+        out_shape=(
+            wide_field,
+            jax.ShapeDtypeStruct((2 * here, 12 * C, 2 * C), jnp.bfloat16),
+        ),
+        in_specs=[hbm, hbm, hbm],
+        out_specs=tuple(on_chip(2)),
+        scratch_shapes=[pltpu.SemaphoreType.DMA((2 * here, 2)), pltpu.SemaphoreType.DMA],
         compiler_params=pltpu.CompilerParams(vmem_limit_bytes=VMEM_LIMIT),
         cost_estimate=pl.CostEstimate(flops=0, bytes_accessed=2**24, transcendentals=0),
-    )(first_kernels.reshape(here, 9 * C, C), second_kernels.reshape(here, 9 * C, C))
+    )(start, first_kernels.reshape(here, 9 * C, C), second_kernels.reshape(here, 9 * C, C))
 
     (y_first,) = sweep(first_kernel, halo, own, (field,), (start, wide, top, bottom))
     got_top = from_previous(y_first[own - halo :], -1)
     got = from_previous(y_first, 0)
     got_bottom = from_previous(y_first[:halo], 1)
     before = (start, wide, top, bottom, got, got_top, got_bottom)
-    relaxed, code = sweep(
-        second_kernel, halo, own, (wide_field, field), before + (y_first,), kept=(own,)
-    )
-    pixels = own * W // depth
-    columns = lax.all_to_all(code.reshape(depth, pixels, C), "depth", 0, 0)
-    errors = pl.pallas_call(
-        scan_kernel,
-        out_shape=jax.ShapeDtypeStruct(columns.shape, jnp.bfloat16),
-        in_specs=on_chip(2),
-        out_specs=on_chip(1)[0],
-        compiler_params=pltpu.CompilerParams(vmem_limit_bytes=VMEM_LIMIT),
-    )(coarse_channel_gain, columns)
-    error = lax.all_to_all(errors, "depth", 0, 0).reshape(start.shape)
+    y_second, code = sweep(
+        second_kernel, halo, own, (wide_field, field), before + (y_first,)
+    )
+    pairs = [[at, at + 1] for at in range(0, depth, 2)]
+    alike = [list(range(core, depth, 2)) for core in range(2)]
+    codes = lax.all_gather(code, "depth", axis_index_groups=pairs)
+    half = jax.ShapeDtypeStruct((own // 2,) + field.shape[1:], jnp.bfloat16)
+    joined = small(join_kernel, half, coarse_channel_gain, codes)
+    joined = joined.reshape(depth // 2, own * W // depth, C)
+    joined = lax.all_to_all(joined, "depth", 0, 0, axis_index_groups=alike)
+    errors = small(
+        scan_kernel, jax.ShapeDtypeStruct(joined.shape, jnp.bfloat16), coarse_channel_gain, joined
+    )
+    errors = lax.all_to_all(errors, "depth", 0, 0, axis_index_groups=alike)
+    pair = lax.all_gather(errors.reshape(half.shape), "depth", axis_index_groups=pairs)
     near = halo - 2
-    error_top = neighbour(error[own - near :], True)
-    error_bottom = neighbour(error[:near], False)
-    (states,) = sweep(
-        third_kernel, near, own, (jax.ShapeDtypeStruct((here,) + start.shape, jnp.float32),),
-        before + (error, error_top, error_bottom), kept=(here, own),
+    part = jax.ShapeDtypeStruct((near,) + field.shape[1:], jnp.bfloat16)
+    error, upper, lower = small(
+        split_kernel, (field, part, part), coarse_channel_gain, codes, pair.reshape(field.shape)
+    )
+    error_top = neighbour(lower, True)
+    error_bottom = neighbour(upper, False)
+    states, relaxed = sweep(
+        third_kernel, near, own,
+        (jax.ShapeDtypeStruct((here,) + start.shape, jnp.float32), wide_field),
+        before + (error, error_top, error_bottom, y_second), kept=(here, own),
     )
     return states, relaxed[None]
 

time: 104 us -> 101 us (0.971)
  blocking collectives: 43 us -> 41.3 us
  Pallas kernels: 22.3 us -> 21 us
  other arithmetic: 0 us -> 1.08 us
    all_to_all x2, blocking collectives: 43 us -> 37 us  [the longest x1 23 us: shards(): joined = lax.all_to_all(joined, 'depth', 0, 0, axis_index_groups=alike)]
    all_gather x0 -> x2, blocking collectives: none -> 4.35 us  [the longest x1 2.37 us: shards(): codes = lax.all_gather(code, 'depth', axis_index_groups=pairs)]
    convert_element_type x0 -> x1, other arithmetic: none -> 1.08 us  [shards(): rounded = start.astype(jnp.bfloat16)]
    pallas_call x3 -> x4, Pallas kernels: 2.09 us -> 1.6 us  [the longest x1 1.23 us: shards(): pl.pallas_call(taps_kernel, out_shape=(wide_field, jax.ShapeDtypeStruct((...]
  transfers between devices with their start and end apart: 7 -> 7, of which waited for: 5 -> 4; matrix products, arithmetic and copies ran while one was open for 0% -> 0% of each run, Pallas kernels for 1% -> 1%
where the time goes in v3:
time: 101 us
  blocking collectives  41.3 us (41%)
  Pallas kernels  21 us (21%)
  starting transfers between devices  20.7 us (20%)
  waiting for transfers between devices  12.1 us (12%)
  local copies, waits for them, and re-layouts  3.58 us (4%)
  other arithmetic  1.08 us (1%)
    all_to_all x1, blocking collectives, shards(): joined = lax.all_to_all(joined, 'depth', 0, 0, axis_index_groups=alike)  23 us
    pallas_call x3, Pallas kernels, sweep(): pl.pallas_call(kernel, out_shape=outs, in_specs=on_chip(len(args)), out_s...  19.4 us
    all_to_all x1, blocking collectives, shards(): errors = lax.all_to_all(errors, 'depth', 0, 0, axis_index_groups=alike)  13.9 us
    ppermute x4, starting transfers between devices, neighbour(): return lax.ppermute(block, 'space', route)  12.2 us
    ppermute x3, starting transfers between devices, from_previous(): return lax.ppermute(block, ('depth', 'space'), route)  8.55 us
    ppermute x4, waiting for transfers between devices, neighbour(): return lax.ppermute(block, 'space', route)  7.4 us
    ppermute x3, waiting for transfers between devices, from_previous(): return lax.ppermute(block, ('depth', 'space'), route)  4.69 us
    unnamed x8, local copies, waits for them, and re-layouts  3.58 us
  transfers between devices with their start and end apart: 7, of which 4 were waited for; matrix products, arithmetic and copies ran while one was open for 0% of the time, Pallas kernels for 1%

profile of v3, /device:TPU:2, one launch (start us, length us, event | category | flops | bytes accessed | tf_op | source)
XLA Modules:
  0.0 100.8 jit_solution(13026128291029307042)
XLA Ops:
  0.6 1.1 %bitcast_convert_fusion = bf16[8,128,128]{2,1,0:T(8,128)(2,1)S(1)} fusion(f32[1,8,128,128]{3,2,1,0:T(8,128)} %param.4), kind=kLoop, calls=%fused_computation | loop fusion | flops 131072 | bytes 786432 | tf_op jit(solution)/shard_map/convert_element_type | solution.py:306
  1.7 4.2 %collective-permute-start.1 = (bf16[8,128,128]{2,1,0:T(8,128)(2,1)S(1)}, bf16[8,128,128]{2,1,0:T(8,128)(2,1)S(1)}, u32[]{:S(2)}, u32[]{:S(2)}) collective-permute-start(bf16[8,128,128]{2,1,0:T(8,128)(2,1)S(1)} %bitcast_convert_fusion), channel_id=1, source_target_pairs={{1,0},{2,1},{3,2},{5,4},{6,5},{7,6},{9,8},{10,9},{11,10},{13,12},{... | collective-permute-start | bytes 786440 | tf_op jit(solution)/shard_map/ppermute | solution.py:282
  5.9 1.9 %collective-permute-start = (bf16[8,128,128]{2,1,0:T(8,128)(2,1)S(1)}, bf16[8,128,128]{2,1,0:T(8,128)(2,1)S(1)}, u32[]{:S(2)}, u32[]{:S(2)}) collective-permute-start(bf16[8,128,128]{2,1,0:T(8,128)(2,1)S(1)} %bitcast_convert_fusion), channel_id=1, source_target_pairs={{0,1},{1,2},{2,3},{4,5},{5,6},{6,7},{8,9},{9,10},{10,11},{12,13},{... | collective-permute-start | bytes 786440 | tf_op jit(solution)/shard_map/ppermute | solution.py:282
  7.8 0.0 copy-start
  7.8 1.0 %copy-done = f32[1,8,128,128]{3,2,1,0:T(8,128)S(1)} copy-done((f32[1,8,128,128]{3,2,1,0:T(8,128)S(1)}, f32[1,8,128,128]{3,2,1,0:T(8,128)}, u32[]{:S(2)}) %copy-start) | copy-done | bytes 524312
  8.9 0.0 copy-start.1
  8.9 1.3 %copy-done.1 = bf16[4,9,128,128]{3,2,1,0:T(8,128)(2,1)S(1)} copy-done((bf16[4,9,128,128]{3,2,1,0:T(8,128)(2,1)S(1)}, bf16[4,9,128,128]{3,2,1,0:T(8,128)(2,1)}, u32[]{:S(2)}) %copy-start.1) | copy-done | bytes 1179672
  10.1 0.0 copy-start.2
  10.2 1.3 %copy-done.2 = bf16[4,9,128,128]{3,2,1,0:T(8,128)(2,1)S(1)} copy-done((bf16[4,9,128,128]{3,2,1,0:T(8,128)(2,1)S(1)}, bf16[4,9,128,128]{3,2,1,0:T(8,128)(2,1)}, u32[]{:S(2)}) %copy-start.2) | copy-done | bytes 1179672
  11.4 1.2 %shard_map.59 = (f32[8,128,128]{2,1,0:T(8,128)S(1)}, bf16[8,1536,256]{2,1,0:T(8,128)(2,1)S(1)}) custom-call(f32[8,128,128]{2,1,0:T(8,128)S(1)} %bitcast.11, bf16[4,1152,128]{2,1,0:T(8,128)(2,1)S(1)} %bitcast.12, bf16[4,1152,128]{2,1,0:T(8,128)(2,1)S(1)} %bitcast.13), custom_call_target="tpu_custom_call" | custom-call | bytes 16777216 | tf_op jit(solution)/shard_map/pallas_call | solution.py:309
  12.7 0.0 collective-permute-done.1.bottom_ref
  12.7 1.5 %collective-permute-done.top_ref = bf16[8,128,128]{2,1,0:T(8,128)(2,1)S(1)} collective-permute-done((bf16[8,128,128]{2,1,0:T(8,128)(2,1)S(1)}, bf16[8,128,128]{2,1,0:T(8,128)(2,1)S(1)}, u32[]{:S(2)}, u32[]{:S(2)}) %collective-permute-start) | collective-permute-done | bytes 262176 | tf_op jit(solution)/shard_map/ppermute | solution.py:282
  14.2 6.9 %shard_map.60.y_ref = bf16[8,128,128]{2,1,0:T(8,128)(2,1)S(1)} custom-call(f32[8,128,128]{2,1,0:T(8,128)S(1)} %get-tuple-element.11.own_ref, bf16[8,1536,256]{2,1,0:T(8,128)(2,1)S(1)} %get-tuple-element.12.wide, bf16[8,128,128]{2,1,0:T(8,128)(2,1)S(1)} %collective-permute-done.top_ref, bf16[8,128,128]{2,1,0:T(8,128)(2,1)S(1)} %collective-permute-done.1.bottom_ref), custom_call_target="tpu_custom_call" | custom-call | flops 4529848320 | bytes 4194304 | tf_op jit(solution)/shard_map/pallas_call | solution.py:268
  21.0 0.0 copy-start.3
  21.0 1.3 %collective-permute-start.4 = (bf16[8,128,128]{2,1,0:T(8,128)(2,1)S(1)}, bf16[8,128,128]{2,1,0:T(8,128)(2,1)S(1)}, u32[]{:S(2)}, u32[]{:S(2)}) collective-permute-start(bf16[8,128,128]{2,1,0:T(8,128)(2,1)S(1)} %shard_map.60.y_ref), channel_id=1, source_target_pairs={{1,4},{2,5},{3,6},{5,8},{6,9},{7,10},{9,12},{10,13},{11,14},{13,16... | collective-permute-start | bytes 786440 | tf_op jit(solution)/shard_map/ppermute | solution.py:293
  22.4 5.3 %collective-permute-start.3 = (bf16[8,128,128]{2,1,0:T(8,128)(2,1)S(1)}, bf16[8,128,128]{2,1,0:T(8,128)(2,1)S(1)}, u32[]{:S(2)}, u32[]{:S(2)}) collective-permute-start(bf16[8,128,128]{2,1,0:T(8,128)(2,1)S(1)} %shard_map.60.y_ref), channel_id=1, source_target_pairs={{0,5},{1,6},{2,7},{4,9},{5,10},{6,11},{8,13},{9,14},{10,15},{12,17... | collective-permute-start | bytes 786440 | tf_op jit(solution)/shard_map/ppermute | solution.py:293
  27.6 2.0 %collective-permute-start.2 = (bf16[8,128,128]{2,1,0:T(8,128)(2,1)S(1)}, bf16[8,128,128]{2,1,0:T(8,128)(2,1)S(1)}, u32[]{:S(2)}, u32[]{:S(2)}) collective-permute-start(bf16[8,128,128]{2,1,0:T(8,128)(2,1)S(1)} %shard_map.60.y_ref), channel_id=1, source_target_pairs={{0,4},{1,5},{2,6},{3,7},{4,8},{5,9},{6,10},{7,11},{8,12},{9,13},{1... | collective-permute-start | bytes 786440 | tf_op jit(solution)/shard_map/ppermute | solution.py:293
  29.6 0.0 collective-permute-done.4.got_bottom_ref
  29.6 4.7 %collective-permute-done.3.got_top_ref = bf16[8,128,128]{2,1,0:T(8,128)(2,1)S(1)} collective-permute-done((bf16[8,128,128]{2,1,0:T(8,128)(2,1)S(1)}, bf16[8,128,128]{2,1,0:T(8,128)(2,1)S(1)}, u32[]{:S(2)}, u32[]{:S(2)}) %collective-permute-start.3) | collective-permute-done | bytes 262176 | tf_op jit(solution)/shard_map/ppermute | solution.py:293
  34.3 0.0 collective-permute-done.2.got_ref
  34.3 6.9 %shard_map.61 = (f32[8,128,128]{2,1,0:T(8,128)S(1)}, bf16[8,128,128]{2,1,0:T(8,128)(2,1)S(1)}) custom-call(f32[8,128,128]{2,1,0:T(8,128)S(1)} %get-tuple-element.11.own_ref, bf16[8,1536,256]{2,1,0:T(8,128)(2,1)S(1)} %get-tuple-element.12.wide, bf16[8,128,128]{2,1,0:T(8,128)(2,1)S(1)} %collective-permute-done.top_ref, ...), custom_call_target="tpu_custom_call" | custom-call | flops 4529848320 | bytes 4194304 | tf_op jit(solution)/shard_map/pallas_call | solution.py:268
  41.3 2.4 %all-gather = bf16[16,128,128]{2,1,0:T(8,128)(2,1)S(1)} all-gather(bf16[8,128,128]{2,1,0:T(8,128)(2,1)S(1)} %get-tuple-element.13), channel_id=2, replica_groups={{0,4},{8,12},{16,20},{24,28},{32,36},{40,44},{48,52},{56,60},{64,68},{7..., dimensions={0}, use_global_device_ids=true | all-gather | bytes 786432 | tf_op jit(solution)/shard_map/all_gather | solution.py:332
  43.6 0.0 copy-done.3
  43.6 0.1 shard_map.62
  43.8 23.0 %all_to_all.10.joined_ref = bf16[32,16,128]{2,1,0:T(8,128)(2,1)S(1)} all-to-all(bf16[32,16,128]{2,1,0:T(8,128)(2,1)S(1)} %bitcast.15), channel_id=1, replica_groups={{0,8,16,24,32,40,48,56,64,72,80,88,96,104,112,120,128,136,144,152,160,1..., dimensions={0} | all-to-all | bytes 262144 | tf_op jit(solution)/shard_map/all_to_all | solution.py:336
  66.8 0.1 shard_map.63
  66.9 13.9 %all_to_all.11 = bf16[32,16,128]{2,1,0:T(8,128)(2,1)S(1)} all-to-all(bf16[32,16,128]{2,1,0:T(8,128)(2,1)S(1)} %shard_map.63), channel_id=1, replica_groups={{0,8,16,24,32,40,48,56,64,72,80,88,96,104,112,120,128,136,144,152,160,1..., dimensions={0} | all-to-all | bytes 262144 | tf_op jit(solution)/shard_map/all_to_all | solution.py:340
  80.8 2.0 %all_gather.11 = bf16[2,4,128,128]{3,2,1,0:T(8,128)(2,1)S(1)} all-gather(bf16[1,4,128,128]{3,2,1,0:T(8,128)(2,1)S(1)} %bitcast.16), channel_id=1, replica_groups={{0,4},{8,12},{16,20},{24,28},{32,36},{40,44},{48,52},{56,60},{64,68},{7..., dimensions={0}, use_global_device_ids=true | all-gather | bytes 393216 | tf_op jit(solution)/shard_map/all_gather | solution.py:341
  82.8 0.2 shard_map.64
  83.0 3.4 %collective-permute-start.5 = (bf16[6,128,128]{2,1,0:T(8,128)(2,1)S(1)}, bf16[6,128,128]{2,1,0:T(8,128)(2,1)S(1)}, u32[]{:S(2)}, u32[]{:S(2)}) collective-permute-start(bf16[6,128,128]{2,1,0:T(8,128)(2,1)S(1)} %get-tuple-element.15), channel_id=1, source_target_pairs={{0,1},{1,2},{2,3},{4,5},{5,6},{6,7},{8,9},{9,10},{10,11},{12,13},{... | collective-permute-start | bytes 589832 | tf_op jit(solution)/shard_map/ppermute | solution.py:282
  86.4 2.7 %collective-permute-start.6 = (bf16[6,128,128]{2,1,0:T(8,128)(2,1)S(1)}, bf16[6,128,128]{2,1,0:T(8,128)(2,1)S(1)}, u32[]{:S(2)}, u32[]{:S(2)}) collective-permute-start(bf16[6,128,128]{2,1,0:T(8,128)(2,1)S(1)} %get-tuple-element.16), channel_id=1, source_target_pairs={{1,0},{2,1},{3,2},{5,4},{6,5},{7,6},{9,8},{10,9},{11,10},{13,12},{... | collective-permute-start | bytes 589832 | tf_op jit(solution)/shard_map/ppermute | solution.py:282
  89.1 2.8 %collective-permute-done.5.error_top_ref = bf16[6,128,128]{2,1,0:T(8,128)(2,1)S(1)} collective-permute-done((bf16[6,128,128]{2,1,0:T(8,128)(2,1)S(1)}, bf16[6,128,128]{2,1,0:T(8,128)(2,1)S(1)}, u32[]{:S(2)}, u32[]{:S(2)}) %collective-permute-start.5) | collective-permute-done | bytes 196640 | tf_op jit(solution)/shard_map/ppermute | solution.py:282
  91.8 3.1 %collective-permute-done.6.error_bottom_ref = bf16[6,128,128]{2,1,0:T(8,128)(2,1)S(1)} collective-permute-done((bf16[6,128,128]{2,1,0:T(8,128)(2,1)S(1)}, bf16[6,128,128]{2,1,0:T(8,128)(2,1)S(1)}, u32[]{:S(2)}, u32[]{:S(2)}) %collective-permute-start.6) | collective-permute-done | bytes 196640 | tf_op jit(solution)/shard_map/ppermute | solution.py:282
  95.0 5.6 %shard_map.65 = (f32[4,8,128,128]{3,2,1,0:T(8,128)}, f32[8,128,128]{2,1,0:T(8,128)}) custom-call(f32[8,128,128]{2,1,0:T(8,128)S(1)} %get-tuple-element.11.own_ref, bf16[8,1536,256]{2,1,0:T(8,128)(2,1)S(1)} %get-tuple-element.12.wide, bf16[8,128,128]{2,1,0:T(8,128)(2,1)S(1)} %collective-permute-done.top_ref, ...), custom_call_target="tpu_custom_call" | custom-call | flops 2944401408 | bytes 4194304 | tf_op jit(solution)/shard_map/pallas_call | solution.py:268
Async XLA Ops:
  1.7 10.9 %collective-permute-start.1 = (bf16[8,128,128]{2,1,0:T(8,128)(2,1)S(1)}, bf16[8,128,128]{2,1,0:T(8,128)(2,1)S(1)}, u32[]{:S(2)}, u32[]{:S(2)}) collective-permute-start(bf16[8,128,128]{2,1,0:T(8,128)(2,1)S(1)} %bitcast_convert_fusion), channel_id=1, source_target_pairs={{1,0},{2,1},{3,2},{5,4},{6,5},{7,6},{9,8},{10,9},{11,10},{13,12},{... | collective-permute-start | bytes 786440 | tf_op jit(solution)/shard_map/ppermute | solution.py:282
  5.9 8.3 %collective-permute-start = (bf16[8,128,128]{2,1,0:T(8,128)(2,1)S(1)}, bf16[8,128,128]{2,1,0:T(8,128)(2,1)S(1)}, u32[]{:S(2)}, u32[]{:S(2)}) collective-permute-start(bf16[8,128,128]{2,1,0:T(8,128)(2,1)S(1)} %bitcast_convert_fusion), channel_id=1, source_target_pairs={{0,1},{1,2},{2,3},{4,5},{5,6},{6,7},{8,9},{9,10},{10,11},{12,13},{... | collective-permute-start | bytes 786440 | tf_op jit(solution)/shard_map/ppermute | solution.py:282
  7.8 1.0 %copy-start = (f32[1,8,128,128]{3,2,1,0:T(8,128)S(1)}, f32[1,8,128,128]{3,2,1,0:T(8,128)}, u32[]{:S(2)}) copy-start(f32[1,8,128,128]{3,2,1,0:T(8,128)} %param.4) | copy-start | bytes 1572868
  8.9 1.3 %copy-start.1 = (bf16[4,9,128,128]{3,2,1,0:T(8,128)(2,1)S(1)}, bf16[4,9,128,128]{3,2,1,0:T(8,128)(2,1)}, u32[]{:S(2)}) copy-start(bf16[4,9,128,128]{3,2,1,0:T(8,128)(2,1)} %param.5) | copy-start | bytes 3538948
  10.1 1.3 %copy-start.2 = (bf16[4,9,128,128]{3,2,1,0:T(8,128)(2,1)S(1)}, bf16[4,9,128,128]{3,2,1,0:T(8,128)(2,1)}, u32[]{:S(2)}) copy-start(bf16[4,9,128,128]{3,2,1,0:T(8,128)(2,1)} %param.6) | copy-start | bytes 3538948
  21.0 22.6 %copy-start.3 = (f32[64,128]{1,0:T(8,128)S(1)}, f32[64,128]{1,0:T(8,128)}, u32[]{:S(2)}) copy-start(f32[64,128]{1,0:T(8,128)} %gain_ref.5) | copy-start | bytes 98308
  21.0 8.6 %collective-permute-start.4 = (bf16[8,128,128]{2,1,0:T(8,128)(2,1)S(1)}, bf16[8,128,128]{2,1,0:T(8,128)(2,1)S(1)}, u32[]{:S(2)}, u32[]{:S(2)}) collective-permute-start(bf16[8,128,128]{2,1,0:T(8,128)(2,1)S(1)} %shard_map.60.y_ref), channel_id=1, source_target_pairs={{1,4},{2,5},{3,6},{5,8},{6,9},{7,10},{9,12},{10,13},{11,14},{13,16... | collective-permute-start | bytes 786440 | tf_op jit(solution)/shard_map/ppermute | solution.py:293
  22.4 12.0 %collective-permute-start.3 = (bf16[8,128,128]{2,1,0:T(8,128)(2,1)S(1)}, bf16[8,128,128]{2,1,0:T(8,128)(2,1)S(1)}, u32[]{:S(2)}, u32[]{:S(2)}) collective-permute-start(bf16[8,128,128]{2,1,0:T(8,128)(2,1)S(1)} %shard_map.60.y_ref), channel_id=1, source_target_pairs={{0,5},{1,6},{2,7},{4,9},{5,10},{6,11},{8,13},{9,14},{10,15},{12,17... | collective-permute-start | bytes 786440 | tf_op jit(solution)/shard_map/ppermute | solution.py:293
  27.6 6.7 %collective-permute-start.2 = (bf16[8,128,128]{2,1,0:T(8,128)(2,1)S(1)}, bf16[8,128,128]{2,1,0:T(8,128)(2,1)S(1)}, u32[]{:S(2)}, u32[]{:S(2)}) collective-permute-start(bf16[8,128,128]{2,1,0:T(8,128)(2,1)S(1)} %shard_map.60.y_ref), channel_id=1, source_target_pairs={{0,4},{1,5},{2,6},{3,7},{4,8},{5,9},{6,10},{7,11},{8,12},{9,13},{1... | collective-permute-start | bytes 786440 | tf_op jit(solution)/shard_map/ppermute | solution.py:293
  83.0 8.8 %collective-permute-start.5 = (bf16[6,128,128]{2,1,0:T(8,128)(2,1)S(1)}, bf16[6,128,128]{2,1,0:T(8,128)(2,1)S(1)}, u32[]{:S(2)}, u32[]{:S(2)}) collective-permute-start(bf16[6,128,128]{2,1,0:T(8,128)(2,1)S(1)} %get-tuple-element.15), channel_id=1, source_target_pairs={{0,1},{1,2},{2,3},{4,5},{5,6},{6,7},{8,9},{9,10},{10,11},{12,13},{... | collective-permute-start | bytes 589832 | tf_op jit(solution)/shard_map/ppermute | solution.py:282
  86.4 8.6 %collective-permute-start.6 = (bf16[6,128,128]{2,1,0:T(8,128)(2,1)S(1)}, bf16[6,128,128]{2,1,0:T(8,128)(2,1)S(1)}, u32[]{:S(2)}, u32[]{:S(2)}) collective-permute-start(bf16[6,128,128]{2,1,0:T(8,128)(2,1)S(1)} %get-tuple-element.16), channel_id=1, source_target_pairs={{1,0},{2,1},{3,2},{5,4},{6,5},{7,6},{9,8},{10,9},{11,10},{13,12},{... | collective-permute-start | bytes 589832 | tf_op jit(solution)/shard_map/ppermute | solution.py:282

commit v4 on v3

--- a/solution.py
+++ b/solution.py
@@ -7,7 +7,6 @@
 from jax.experimental.pallas import tpu as pltpu
 from jax.sharding import PartitionSpec as P
 
-GROUP = 1
 W = 128
 C = 128
 VMEM_LIMIT = 32 * 2**20
@@ -53,24 +52,46 @@
         dst[pair, :, pl.ds((half * 3 + tap) * C, C)] = part.astype(jnp.bfloat16)
 
 
-def conv_pairs(src, wide, slot, pairs, emit):
-    for first in range(0, pairs, GROUP):
-        count = min(GROUP, pairs - first)
-        low = src[pl.ds(first, count)].reshape(count * W, 6 * C)
-        high = src[pl.ds(first + 1, count)].reshape(count * W, 6 * C)
-        total = jnp.dot(
-            low, wide[slot, pl.ds(0, 6 * C), :], preferred_element_type=jnp.float32
-        ) + jnp.dot(high, wide[slot, pl.ds(6 * C, 6 * C), :], preferred_element_type=jnp.float32)
-        for index in range(count):
-            for half in range(2):
-                emit(
-                    first + index,
-                    half,
-                    total[index * W : (index + 1) * W, half * C : (half + 1) * C],
-                )
-
-
-def layers(count, halo, own, state, fields, wide, after_layer):
+def conv_pair(src, wide, slot, pair, emit):
+    total = jnp.dot(
+        src[pair], wide[slot, pl.ds(0, 6 * C), :], preferred_element_type=jnp.float32
+    ) + jnp.dot(src[pair + 1], wide[slot, pl.ds(6 * C, 6 * C), :], preferred_element_type=jnp.float32)
+    for half in range(2):
+        emit(pair, half, total[:, half * C : (half + 1) * C])
+
+
+def inner_steps(own, value_of, wide, mid, parts):
+    values = {}
+    for row in range(own):
+        values[row] = value_of(row)
+        spread(parts[0], row // 2, row % 2, values[row])
+    for step in range(1, len(parts)):
+
+        def hidden(pair, half, value, step=step):
+            spread(parts[step], pair, half, jnp.tanh(value))
+
+        def outer(pair, half, value, step=step):
+            new = value_of(step + 2 * pair + half) + 0.5 * jnp.tanh(value)
+            mid[2 * pair + half] = new
+            spread(parts[step], pair, half, new)
+
+        for pair in range(inner_pairs(own, step)):
+            conv_pair(parts[step - 1], wide, step - 1, pair, outer if step % 2 == 0 else hidden)
+
+
+def first_inner(own_ref, wide, mid, *parts):
+    inner_steps(own_ref.shape[0], lambda row: own_ref[row], wide, mid, parts)
+
+
+def third_inner(own_ref, wide, got_ref, error_ref, begin_ref, mid, *parts):
+    begin = lax.axis_index("depth") == 0
+    for row in range(own_ref.shape[0]):
+        value = jnp.where(begin, own_ref[row], got_ref[row].astype(jnp.float32))
+        begin_ref[row] = value + error_ref[row].astype(jnp.float32)
+    inner_steps(own_ref.shape[0], lambda row: begin_ref[row], wide, mid, parts)
+
+
+def layers(count, halo, own, state, fields, wide, after_layer, mid, parts):
     slab = lax.axis_index("space")
     above = (slab > 0).astype(jnp.float32)
     below = (slab < lax.axis_size("space") - 1).astype(jnp.float32)
@@ -83,36 +104,53 @@
         return value
 
     rows = own + 2 * halo
-    for layer in range(count):
-        offset = 2 * layer + 1
-
-        def hidden(pair, half, value, offset=offset):
-            row = offset + 2 * pair + half
-            spread(fields[1], pair, half, keep(row, jnp.tanh(value)))
-
-        conv_pairs(fields[0], wide, 2 * layer, (rows - 2 * offset) // 2, hidden)
-        offset = 2 * layer + 2
-
-        def outer(pair, half, value, offset=offset, last=layer == count - 1):
-            row = offset + 2 * pair + half
+    for step in range(1, 2 * count + 1):
+        src, dst = fields[(step - 1) % 2], fields[step % 2]
+        inside = range(halo // 2, halo // 2 + inner_pairs(own, step)) if parts else ()
+
+        def hidden(pair, half, value, step=step, dst=dst):
+            row = step + 2 * pair + half
+            spread(dst, pair, half, keep(row, jnp.tanh(value)))
+
+        def outer(pair, half, value, step=step, dst=dst):
+            row = step + 2 * pair + half
             new = state[row] + 0.5 * keep(row, jnp.tanh(value))
-            if not last:
+            if step < 2 * count:
                 state[row] = new
-                spread(fields[0], pair, half, new)
+                spread(dst, pair, half, new)
             if halo <= row < halo + own:
-                after_layer(offset // 2, row - halo, new)
-
-        conv_pairs(fields[1], wide, 2 * layer + 1, (rows - 2 * offset) // 2, outer)
-
-
-def load_rows(halo, own, value_of, state, field):
+                after_layer(step // 2, row - halo, new)
+
+        for pair in range((rows - 2 * step) // 2):
+            if pair not in inside:
+                conv_pair(src, wide, step - 1, pair, outer if step % 2 == 0 else hidden)
+                continue
+            dst[pair] = parts[step][pair - halo // 2]
+            if step % 2 == 0:
+                for half in range(2):
+                    row = step + 2 * pair + half
+                    new = mid[2 * (pair - halo // 2) + half]
+                    state[row] = new
+                    after_layer(step // 2, row - halo, new)
+
+
+def inner_pairs(own, step):
+    return max(own // 2 - step, 0)
+
+
+def load_rows(halo, own, value_of, state, field, part):
     for row in range(own + 2 * halo):
         value = value_of(row)
         state[row] = value
-        spread(field, row // 2, row % 2, value)
-
-
-def first_kernel(own_ref, wide, top_ref, bottom_ref, y_ref, state, fa, fb):
+        if part is None or not halo <= row < halo + own:
+            spread(field, row // 2, row % 2, value)
+    if part is not None:
+        for pair in range(own // 2):
+            field[halo // 2 + pair] = part[pair]
+
+
+def first_kernel(own_ref, wide, top_ref, bottom_ref, mid, *refs):
+    parts, (y_ref, state, fa, fb) = refs[:-4], refs[-4:]
     own = own_ref.shape[0]
     halo = top_ref.shape[0]
 
@@ -123,13 +161,13 @@
             return bottom_ref[row - halo - own].astype(jnp.float32)
         return own_ref[row - halo]
 
-    load_rows(halo, own, value_of, state, fa)
+    load_rows(halo, own, value_of, state, fa, parts[0])
 
     def after_layer(done, row, new):
         if 2 * done == halo:
             y_ref[row] = new.astype(jnp.bfloat16)
 
-    layers(halo // 2, halo, own, state, (fa, fb), wide, after_layer)
+    layers(halo // 2, halo, own, state, (fa, fb), wide, after_layer, mid, parts)
 
 
 def second_kernel(own_ref, wide, top_ref, bottom_ref, got_ref, got_top_ref, got_bottom_ref, y_ref,
@@ -146,7 +184,7 @@
             return jnp.where(begin, bottom_ref[at], got_bottom_ref[at]).astype(jnp.float32)
         return jnp.where(begin, own_ref[row - halo], got_ref[row - halo].astype(jnp.float32))
 
-    load_rows(halo, own, value_of, state, fa)
+    load_rows(halo, own, value_of, state, fa, None)
 
     def after_layer(done, row, new):
         if 2 * done == halo:
@@ -154,18 +192,22 @@
             resid = new - y_ref[row].astype(jnp.float32)
             code_ref[row] = encode(resid, RESID_SCALE)
 
-    layers(halo // 2, halo, own, state, (fa, fb), wide, after_layer)
-
-
-def third_kernel(own_ref, wide, top_ref, bottom_ref, got_ref, got_top_ref, got_bottom_ref,
-                 error_ref, error_top_ref, error_bottom_ref, y_ref, states_ref, relaxed_ref,
-                 state, fa, fb, kept, out_sems, relaxed_sem):
+    layers(halo // 2, halo, own, state, (fa, fb), wide, after_layer, None, ())
+
+
+def third_kernel(own_ref, wide, top_ref, bottom_ref, got_top_ref, got_bottom_ref,
+                 error_top_ref, error_bottom_ref, y_ref, mid, *refs):
+    parts, (states_ref, relaxed_ref, state, fa, fb, kept, out_sems, relaxed_sem) = refs[:-8], refs[-8:]
     own = own_ref.shape[0]
     halo = error_top_ref.shape[0]
     skip = top_ref.shape[0] - halo
     begin = lax.axis_index("depth") == 0
-    outs = [pltpu.make_async_copy(y_ref, relaxed_ref, relaxed_sem)]
-    outs[0].start()
+    outs = [
+        pltpu.make_async_copy(y_ref, relaxed_ref, relaxed_sem),
+        pltpu.make_async_copy(own_ref, states_ref.at[0], out_sems.at[0, 0]),
+    ]
+    for out in outs:
+        out.start()
 
     def put(done, row, value):
         kept[done, row] = value
@@ -184,14 +226,10 @@
             at = row - halo - own
             value = jnp.where(begin, bottom_ref[at], got_bottom_ref[at])
             return value.astype(jnp.float32) + error_bottom_ref[at].astype(jnp.float32)
-        at = row - halo
-        value = jnp.where(begin, own_ref[at], got_ref[at].astype(jnp.float32))
-        value = value + error_ref[at].astype(jnp.float32)
-        put(0, at, value)
-        return value
-
-    load_rows(halo, own, value_of, state, fa)
-    layers(halo // 2, halo, own, state, (fa, fb), wide, put)
+        return own_ref[row - halo]
+
+    load_rows(halo, own, value_of, state, fa, parts[0])
+    layers(halo // 2, halo, own, state, (fa, fb), wide, put, mid, parts)
     for out in outs:
         out.wait()
 
@@ -239,13 +277,16 @@
     return [pl.BlockSpec(memory_space=pltpu.VMEM)] * count
 
 
-def small(kernel, outs, *args):
+def small(kernel, outs, *args, flops=1):
     return pl.pallas_call(
         kernel,
         out_shape=outs,
         in_specs=on_chip(len(args)),
         out_specs=jax.tree.map(lambda _: on_chip(1)[0], outs),
         compiler_params=pltpu.CompilerParams(vmem_limit_bytes=VMEM_LIMIT),
+        cost_estimate=pl.CostEstimate(
+            flops=flops * 36 * C * C * W, bytes_accessed=2**19, transcendentals=0
+        ),
     )(*args)
 
 
@@ -319,7 +360,13 @@
         cost_estimate=pl.CostEstimate(flops=0, bytes_accessed=2**24, transcendentals=0),
     )(start, first_kernels.reshape(here, 9 * C, C), second_kernels.reshape(here, 9 * C, C))
 
-    (y_first,) = sweep(first_kernel, halo, own, (field,), (start, wide, top, bottom))
+    inner = [jax.ShapeDtypeStruct((own - 4,) + field.shape[1:], jnp.float32)] + [
+        jax.ShapeDtypeStruct((inner_pairs(own, step), W, 6 * C), jnp.bfloat16)
+        for step in range(own // 2)
+    ]
+    pairs_inside = sum(inner_pairs(own, step) for step in range(1, own // 2))
+    known = small(first_inner, inner, start, wide, flops=pairs_inside)
+    (y_first,) = sweep(first_kernel, halo, own, (field,), (start, wide, top, bottom, *known))
     got_top = from_previous(y_first[own - halo :], -1)
     got = from_previous(y_first, 0)
     got_bottom = from_previous(y_first[:halo], 1)
@@ -346,10 +393,14 @@
     )
     error_top = neighbour(lower, True)
     error_bottom = neighbour(upper, False)
+    begin, *known = small(
+        third_inner, [wide_field] + inner, start, wide, got, error, flops=pairs_inside
+    )
     states, relaxed = sweep(
         third_kernel, near, own,
         (jax.ShapeDtypeStruct((here,) + start.shape, jnp.float32), wide_field),
-        before + (error, error_top, error_bottom, y_second), kept=(here, own),
+        (begin, wide, top, bottom, got_top, got_bottom, error_top, error_bottom, y_second, *known),
+        kept=(here, own),
     )
     return states, relaxed[None]
 

time: 101 us -> 100 us (0.990)
  waiting for transfers between devices: 12.1 us -> 9.48 us
  Pallas kernels: 21 us -> 22.4 us
    ppermute x4, waiting for transfers between devices: 7.4 us -> 4.79 us  [neighbour(): return lax.ppermute(block, 'space', route)]
    pallas_call x3 -> x5, Pallas kernels: 0.37 us -> 2.97 us  [small(): pl.pallas_call(kernel, out_shape=outs, in_specs=on_chip(len(args)), out_s...]
    pallas_call x3, Pallas kernels: 19.4 us -> 18.2 us  [sweep(): pl.pallas_call(kernel, out_shape=outs, in_specs=on_chip(len(args)), out_s...]
  transfers between devices with their start and end apart: 7 -> 7, of which waited for: 4 -> 4; matrix products, arithmetic and copies ran while one was open for 0% -> 0% of each run, Pallas kernels for 1% -> 4%
where the time goes in v4:
time: 100 us; the launch traced here: 99.5 us
  blocking collectives  41.3 us (41%)
  Pallas kernels  22.4 us (22%)
  starting transfers between devices  20.7 us (21%)
  waiting for transfers between devices  9.48 us (9%)
  local copies, waits for them, and re-layouts  3.58 us (4%)
  other arithmetic  1.08 us (1%)
    all_to_all x1, blocking collectives, shards(): joined = lax.all_to_all(joined, 'depth', 0, 0, axis_index_groups=alike)  22.8 us
    pallas_call x3, Pallas kernels, sweep(): pl.pallas_call(kernel, out_shape=outs, in_specs=on_chip(len(args)), out_s...  18.2 us
    all_to_all x1, blocking collectives, shards(): errors = lax.all_to_all(errors, 'depth', 0, 0, axis_index_groups=alike)  13.9 us
    ppermute x4, starting transfers between devices, neighbour(): return lax.ppermute(block, 'space', route)  12.2 us
    ppermute x3, starting transfers between devices, from_previous(): return lax.ppermute(block, ('depth', 'space'), route)  8.55 us
    ppermute x4, waiting for transfers between devices, neighbour(): return lax.ppermute(block, 'space', route)  4.79 us
    ppermute x3, waiting for transfers between devices, from_previous(): return lax.ppermute(block, ('depth', 'space'), route)  4.69 us
    unnamed x8, local copies, waits for them, and re-layouts  3.58 us
  transfers between devices with their start and end apart: 7, of which 4 were waited for; matrix products, arithmetic and copies ran while one was open for 0% of the time, Pallas kernels for 4%

profile of v4, /device:TPU:2, one launch (start us, length us, event | category | flops | bytes accessed | tf_op | source)
XLA Modules:
  0.0 99.5 jit_solution(15710096238487211540)
XLA Ops:
  0.6 1.1 %bitcast_convert_fusion = bf16[8,128,128]{2,1,0:T(8,128)(2,1)S(1)} fusion(f32[1,8,128,128]{3,2,1,0:T(8,128)} %param.4), kind=kLoop, calls=%fused_computation | loop fusion | flops 131072 | bytes 786432 | tf_op jit(solution)/shard_map/convert_element_type | solution.py:347
  1.7 4.2 %collective-permute-start.1 = (bf16[8,128,128]{2,1,0:T(8,128)(2,1)S(1)}, bf16[8,128,128]{2,1,0:T(8,128)(2,1)S(1)}, u32[]{:S(2)}, u32[]{:S(2)}) collective-permute-start(bf16[8,128,128]{2,1,0:T(8,128)(2,1)S(1)} %bitcast_convert_fusion), channel_id=1, source_target_pairs={{1,0},{2,1},{3,2},{5,4},{6,5},{7,6},{9,8},{10,9},{11,10},{13,12},{... | collective-permute-start | bytes 786440 | tf_op jit(solution)/shard_map/ppermute | solution.py:323
  5.9 1.9 %collective-permute-start = (bf16[8,128,128]{2,1,0:T(8,128)(2,1)S(1)}, bf16[8,128,128]{2,1,0:T(8,128)(2,1)S(1)}, u32[]{:S(2)}, u32[]{:S(2)}) collective-permute-start(bf16[8,128,128]{2,1,0:T(8,128)(2,1)S(1)} %bitcast_convert_fusion), channel_id=1, source_target_pairs={{0,1},{1,2},{2,3},{4,5},{5,6},{6,7},{8,9},{9,10},{10,11},{12,13},{... | collective-permute-start | bytes 786440 | tf_op jit(solution)/shard_map/ppermute | solution.py:323
  7.8 0.0 copy-start
  7.8 1.0 %copy-done = f32[1,8,128,128]{3,2,1,0:T(8,128)S(1)} copy-done((f32[1,8,128,128]{3,2,1,0:T(8,128)S(1)}, f32[1,8,128,128]{3,2,1,0:T(8,128)}, u32[]{:S(2)}) %copy-start) | copy-done | bytes 524312
  8.9 0.0 copy-start.1
  8.9 1.3 %copy-done.1 = bf16[4,9,128,128]{3,2,1,0:T(8,128)(2,1)S(1)} copy-done((bf16[4,9,128,128]{3,2,1,0:T(8,128)(2,1)S(1)}, bf16[4,9,128,128]{3,2,1,0:T(8,128)(2,1)}, u32[]{:S(2)}) %copy-start.1) | copy-done | bytes 1179672
  10.1 0.0 copy-start.2
  10.2 1.3 %copy-done.2 = bf16[4,9,128,128]{3,2,1,0:T(8,128)(2,1)S(1)} copy-done((bf16[4,9,128,128]{3,2,1,0:T(8,128)(2,1)S(1)}, bf16[4,9,128,128]{3,2,1,0:T(8,128)(2,1)}, u32[]{:S(2)}) %copy-start.2) | copy-done | bytes 1179672
  11.4 1.2 %shard_map.59 = (f32[8,128,128]{2,1,0:T(8,128)S(1)}, bf16[8,1536,256]{2,1,0:T(8,128)(2,1)S(1)}) custom-call(f32[8,128,128]{2,1,0:T(8,128)S(1)} %bitcast.11, bf16[4,1152,128]{2,1,0:T(8,128)(2,1)S(1)} %bitcast.12, bf16[4,1152,128]{2,1,0:T(8,128)(2,1)S(1)} %bitcast.13), custom_call_target="tpu_custom_call" | custom-call | bytes 16777216 | tf_op jit(solution)/shard_map/pallas_call | solution.py:350
  12.7 1.3 %shard_map.60 = (f32[4,128,128]{2,1,0:T(8,128)S(1)}, bf16[4,128,768]{2,1,0:T(8,128)(2,1)S(1)}, bf16[3,128,768]{2,1,0:T(8,128)(2,1)S(1)}, bf16[2,128,768]{2,1,0:T(8,128)(2,1)S(1)}, bf16[1,128,768]{2,1,0:T(8,128)(2,1)S(1)}) custom-call(f32[8,128,128]{2,1,0:T(8,128)S(1)} %get-tuple-element.22.own_ref, bf16[8,1536,256]{2,1,0:T(8,128)(2,1)S(1)} %get-tuple-element.23.wide), custom_call_target="tpu_custom_call" | custom-call | flops 452984832 | bytes 524288 | tf_op jit(solution)/shard_map/pallas_call | solution.py:281
  14.0 0.0 collective-permute-done.1.bottom_ref
  14.0 0.2 collective-permute-done.top_ref
  14.2 6.3 %shard_map.61.y_ref = bf16[8,128,128]{2,1,0:T(8,128)(2,1)S(1)} custom-call(f32[8,128,128]{2,1,0:T(8,128)S(1)} %get-tuple-element.22.own_ref, bf16[8,1536,256]{2,1,0:T(8,128)(2,1)S(1)} %get-tuple-element.23.wide, bf16[8,128,128]{2,1,0:T(8,128)(2,1)S(1)} %collective-permute-done.top_ref, bf16[8,128,128]{2,1,0:T(8,128)(2,1)S(1)} %collective-permute-done.1.bottom_ref, ...), custom_call_target="tpu_custom_call" | custom-call | flops 4529848320 | bytes 4194304 | tf_op jit(solution)/shard_map/pallas_call | solution.py:309
  20.5 0.0 copy-start.3
  20.5 1.3 %collective-permute-start.4 = (bf16[8,128,128]{2,1,0:T(8,128)(2,1)S(1)}, bf16[8,128,128]{2,1,0:T(8,128)(2,1)S(1)}, u32[]{:S(2)}, u32[]{:S(2)}) collective-permute-start(bf16[8,128,128]{2,1,0:T(8,128)(2,1)S(1)} %shard_map.61.y_ref), channel_id=1, source_target_pairs={{1,4},{2,5},{3,6},{5,8},{6,9},{7,10},{9,12},{10,13},{11,14},{13,16... | collective-permute-start | bytes 786440 | tf_op jit(solution)/shard_map/ppermute | solution.py:334
  21.8 5.3 %collective-permute-start.3 = (bf16[8,128,128]{2,1,0:T(8,128)(2,1)S(1)}, bf16[8,128,128]{2,1,0:T(8,128)(2,1)S(1)}, u32[]{:S(2)}, u32[]{:S(2)}) collective-permute-start(bf16[8,128,128]{2,1,0:T(8,128)(2,1)S(1)} %shard_map.61.y_ref), channel_id=1, source_target_pairs={{0,5},{1,6},{2,7},{4,9},{5,10},{6,11},{8,13},{9,14},{10,15},{12,17... | collective-permute-start | bytes 786440 | tf_op jit(solution)/shard_map/ppermute | solution.py:334
  27.1 2.0 %collective-permute-start.2 = (bf16[8,128,128]{2,1,0:T(8,128)(2,1)S(1)}, bf16[8,128,128]{2,1,0:T(8,128)(2,1)S(1)}, u32[]{:S(2)}, u32[]{:S(2)}) collective-permute-start(bf16[8,128,128]{2,1,0:T(8,128)(2,1)S(1)} %shard_map.61.y_ref), channel_id=1, source_target_pairs={{0,4},{1,5},{2,6},{3,7},{4,8},{5,9},{6,10},{7,11},{8,12},{9,13},{1... | collective-permute-start | bytes 786440 | tf_op jit(solution)/shard_map/ppermute | solution.py:334
  29.0 0.0 collective-permute-done.4.got_bottom_ref
  29.0 4.7 %collective-permute-done.3.got_top_ref = bf16[8,128,128]{2,1,0:T(8,128)(2,1)S(1)} collective-permute-done((bf16[8,128,128]{2,1,0:T(8,128)(2,1)S(1)}, bf16[8,128,128]{2,1,0:T(8,128)(2,1)S(1)}, u32[]{:S(2)}, u32[]{:S(2)}) %collective-permute-start.3) | collective-permute-done | bytes 262176 | tf_op jit(solution)/shard_map/ppermute | solution.py:334
  33.7 0.0 collective-permute-done.2.got_ref
  33.7 6.9 %shard_map.62 = (f32[8,128,128]{2,1,0:T(8,128)S(1)}, bf16[8,128,128]{2,1,0:T(8,128)(2,1)S(1)}) custom-call(f32[8,128,128]{2,1,0:T(8,128)S(1)} %get-tuple-element.22.own_ref, bf16[8,1536,256]{2,1,0:T(8,128)(2,1)S(1)} %get-tuple-element.23.wide, bf16[8,128,128]{2,1,0:T(8,128)(2,1)S(1)} %collective-permute-done.top_ref, ...), custom_call_target="tpu_custom_call" | custom-call | flops 4529848320 | bytes 4194304 | tf_op jit(solution)/shard_map/pallas_call | solution.py:309
  40.7 2.5 %all-gather = bf16[16,128,128]{2,1,0:T(8,128)(2,1)S(1)} all-gather(bf16[8,128,128]{2,1,0:T(8,128)(2,1)S(1)} %get-tuple-element.29), channel_id=2, replica_groups={{0,4},{8,12},{16,20},{24,28},{32,36},{40,44},{48,52},{56,60},{64,68},{7..., dimensions={0}, use_global_device_ids=true | all-gather | bytes 786432 | tf_op jit(solution)/shard_map/all_gather | solution.py:379
  43.2 0.0 copy-done.3
  43.2 0.1 shard_map.63
  43.4 22.8 %all_to_all.10.joined_ref = bf16[32,16,128]{2,1,0:T(8,128)(2,1)S(1)} all-to-all(bf16[32,16,128]{2,1,0:T(8,128)(2,1)S(1)} %bitcast.15), channel_id=1, replica_groups={{0,8,16,24,32,40,48,56,64,72,80,88,96,104,112,120,128,136,144,152,160,1..., dimensions={0} | all-to-all | bytes 262144 | tf_op jit(solution)/shard_map/all_to_all | solution.py:383
  66.2 0.1 shard_map.64
  66.3 13.9 %all_to_all.11 = bf16[32,16,128]{2,1,0:T(8,128)(2,1)S(1)} all-to-all(bf16[32,16,128]{2,1,0:T(8,128)(2,1)S(1)} %shard_map.64), channel_id=1, replica_groups={{0,8,16,24,32,40,48,56,64,72,80,88,96,104,112,120,128,136,144,152,160,1..., dimensions={0} | all-to-all | bytes 262144 | tf_op jit(solution)/shard_map/all_to_all | solution.py:387
  80.2 2.0 %all_gather.11 = bf16[2,4,128,128]{3,2,1,0:T(8,128)(2,1)S(1)} all-gather(bf16[1,4,128,128]{3,2,1,0:T(8,128)(2,1)S(1)} %bitcast.16), channel_id=1, replica_groups={{0,4},{8,12},{16,20},{24,28},{32,36},{40,44},{48,52},{56,60},{64,68},{7..., dimensions={0}, use_global_device_ids=true | all-gather | bytes 393216 | tf_op jit(solution)/shard_map/all_gather | solution.py:388
  82.2 0.2 shard_map.65
  82.4 3.4 %collective-permute-start.5 = (bf16[6,128,128]{2,1,0:T(8,128)(2,1)S(1)}, bf16[6,128,128]{2,1,0:T(8,128)(2,1)S(1)}, u32[]{:S(2)}, u32[]{:S(2)}) collective-permute-start(bf16[6,128,128]{2,1,0:T(8,128)(2,1)S(1)} %get-tuple-element.32), channel_id=1, source_target_pairs={{0,1},{1,2},{2,3},{4,5},{5,6},{6,7},{8,9},{9,10},{10,11},{12,13},{... | collective-permute-start | bytes 589832 | tf_op jit(solution)/shard_map/ppermute | solution.py:323
  85.8 2.7 %collective-permute-start.6 = (bf16[6,128,128]{2,1,0:T(8,128)(2,1)S(1)}, bf16[6,128,128]{2,1,0:T(8,128)(2,1)S(1)}, u32[]{:S(2)}, u32[]{:S(2)}) collective-permute-start(bf16[6,128,128]{2,1,0:T(8,128)(2,1)S(1)} %get-tuple-element.33), channel_id=1, source_target_pairs={{1,0},{2,1},{3,2},{5,4},{6,5},{7,6},{9,8},{10,9},{11,10},{13,12},{... | collective-permute-start | bytes 589832 | tf_op jit(solution)/shard_map/ppermute | solution.py:323
  88.5 1.3 %shard_map.66 = (f32[8,128,128]{2,1,0:T(8,128)S(1)}, f32[4,128,128]{2,1,0:T(8,128)S(1)}, bf16[4,128,768]{2,1,0:T(8,128)(2,1)S(1)}, bf16[3,128,768]{2,1,0:T(8,128...) custom-call(f32[8,128,128]{2,1,0:T(8,128)S(1)} %get-tuple-element.22.own_ref, ...), custom_call_target="tpu_custom_call" | custom-call | flops 452984832 | bytes 524288 | tf_op jit(solution)/shard_map/pallas_call | solution.py:281
  89.8 1.4 %collective-permute-done.5.error_top_ref = bf16[6,128,128]{2,1,0:T(8,128)(2,1)S(1)} collective-permute-done((bf16[6,128,128]{2,1,0:T(8,128)(2,1)S(1)}, bf16[6,128,128]{2,1,0:T(8,128)(2,1)S(1)}, u32[]{:S(2)}, u32[]{:S(2)}) %collective-permute-start.5) | collective-permute-done | bytes 196640 | tf_op jit(solution)/shard_map/ppermute | solution.py:323
  91.2 3.1 %collective-permute-done.6.error_bottom_ref = bf16[6,128,128]{2,1,0:T(8,128)(2,1)S(1)} collective-permute-done((bf16[6,128,128]{2,1,0:T(8,128)(2,1)S(1)}, bf16[6,128,128]{2,1,0:T(8,128)(2,1)S(1)}, u32[]{:S(2)}, u32[]{:S(2)}) %collective-permute-start.6) | collective-permute-done | bytes 196640 | tf_op jit(solution)/shard_map/ppermute | solution.py:323
  94.4 4.9 %shard_map.67 = (f32[4,8,128,128]{3,2,1,0:T(8,128)}, f32[8,128,128]{2,1,0:T(8,128)}) custom-call(f32[8,128,128]{2,1,0:T(8,128)S(1)} %get-tuple-element.31.own_ref, bf16[8,1536,256]{2,1,0:T(8,128)(2,1)S(1)} %get-tuple-element.23.wide, bf16[8,128,128]{2,1,0:T(8,128)(2,1)S(1)} %collective-permute-done.top_ref, ...), custom_call_target="tpu_custom_call" | custom-call | flops 2944401408 | bytes 4194304 | tf_op jit(solution)/shard_map/pallas_call | solution.py:309
Async XLA Ops:
  1.7 12.3 %collective-permute-start.1 = (bf16[8,128,128]{2,1,0:T(8,128)(2,1)S(1)}, bf16[8,128,128]{2,1,0:T(8,128)(2,1)S(1)}, u32[]{:S(2)}, u32[]{:S(2)}) collective-permute-start(bf16[8,128,128]{2,1,0:T(8,128)(2,1)S(1)} %bitcast_convert_fusion), channel_id=1, source_target_pairs={{1,0},{2,1},{3,2},{5,4},{6,5},{7,6},{9,8},{10,9},{11,10},{13,12},{... | collective-permute-start | bytes 786440 | tf_op jit(solution)/shard_map/ppermute | solution.py:323
  5.9 8.3 %collective-permute-start = (bf16[8,128,128]{2,1,0:T(8,128)(2,1)S(1)}, bf16[8,128,128]{2,1,0:T(8,128)(2,1)S(1)}, u32[]{:S(2)}, u32[]{:S(2)}) collective-permute-start(bf16[8,128,128]{2,1,0:T(8,128)(2,1)S(1)} %bitcast_convert_fusion), channel_id=1, source_target_pairs={{0,1},{1,2},{2,3},{4,5},{5,6},{6,7},{8,9},{9,10},{10,11},{12,13},{... | collective-permute-start | bytes 786440 | tf_op jit(solution)/shard_map/ppermute | solution.py:323
  7.8 1.0 %copy-start = (f32[1,8,128,128]{3,2,1,0:T(8,128)S(1)}, f32[1,8,128,128]{3,2,1,0:T(8,128)}, u32[]{:S(2)}) copy-start(f32[1,8,128,128]{3,2,1,0:T(8,128)} %param.4) | copy-start | bytes 1572868
  8.9 1.3 %copy-start.1 = (bf16[4,9,128,128]{3,2,1,0:T(8,128)(2,1)S(1)}, bf16[4,9,128,128]{3,2,1,0:T(8,128)(2,1)}, u32[]{:S(2)}) copy-start(bf16[4,9,128,128]{3,2,1,0:T(8,128)(2,1)} %param.5) | copy-start | bytes 3538948
  10.1 1.3 %copy-start.2 = (bf16[4,9,128,128]{3,2,1,0:T(8,128)(2,1)S(1)}, bf16[4,9,128,128]{3,2,1,0:T(8,128)(2,1)}, u32[]{:S(2)}) copy-start(bf16[4,9,128,128]{3,2,1,0:T(8,128)(2,1)} %param.6) | copy-start | bytes 3538948
  20.5 22.8 %copy-start.3 = (f32[64,128]{1,0:T(8,128)S(1)}, f32[64,128]{1,0:T(8,128)}, u32[]{:S(2)}) copy-start(f32[64,128]{1,0:T(8,128)} %gain_ref.5) | copy-start | bytes 98308
  20.5 8.6 %collective-permute-start.4 = (bf16[8,128,128]{2,1,0:T(8,128)(2,1)S(1)}, bf16[8,128,128]{2,1,0:T(8,128)(2,1)S(1)}, u32[]{:S(2)}, u32[]{:S(2)}) collective-permute-start(bf16[8,128,128]{2,1,0:T(8,128)(2,1)S(1)} %shard_map.61.y_ref), channel_id=1, source_target_pairs={{1,4},{2,5},{3,6},{5,8},{6,9},{7,10},{9,12},{10,13},{11,14},{13,16... | collective-permute-start | bytes 786440 | tf_op jit(solution)/shard_map/ppermute | solution.py:334
  21.8 12.0 %collective-permute-start.3 = (bf16[8,128,128]{2,1,0:T(8,128)(2,1)S(1)}, bf16[8,128,128]{2,1,0:T(8,128)(2,1)S(1)}, u32[]{:S(2)}, u32[]{:S(2)}) collective-permute-start(bf16[8,128,128]{2,1,0:T(8,128)(2,1)S(1)} %shard_map.61.y_ref), channel_id=1, source_target_pairs={{0,5},{1,6},{2,7},{4,9},{5,10},{6,11},{8,13},{9,14},{10,15},{12,17... | collective-permute-start | bytes 786440 | tf_op jit(solution)/shard_map/ppermute | solution.py:334
  27.1 6.7 %collective-permute-start.2 = (bf16[8,128,128]{2,1,0:T(8,128)(2,1)S(1)}, bf16[8,128,128]{2,1,0:T(8,128)(2,1)S(1)}, u32[]{:S(2)}, u32[]{:S(2)}) collective-permute-start(bf16[8,128,128]{2,1,0:T(8,128)(2,1)S(1)} %shard_map.61.y_ref), channel_id=1, source_target_pairs={{0,4},{1,5},{2,6},{3,7},{4,8},{5,9},{6,10},{7,11},{8,12},{9,13},{1... | collective-permute-start | bytes 786440 | tf_op jit(solution)/shard_map/ppermute | solution.py:334
  82.4 8.8 %collective-permute-start.5 = (bf16[6,128,128]{2,1,0:T(8,128)(2,1)S(1)}, bf16[6,128,128]{2,1,0:T(8,128)(2,1)S(1)}, u32[]{:S(2)}, u32[]{:S(2)}) collective-permute-start(bf16[6,128,128]{2,1,0:T(8,128)(2,1)S(1)} %get-tuple-element.32), channel_id=1, source_target_pairs={{0,1},{1,2},{2,3},{4,5},{5,6},{6,7},{8,9},{9,10},{10,11},{12,13},{... | collective-permute-start | bytes 589832 | tf_op jit(solution)/shard_map/ppermute | solution.py:323
  85.8 8.6 %collective-permute-start.6 = (bf16[6,128,128]{2,1,0:T(8,128)(2,1)S(1)}, bf16[6,128,128]{2,1,0:T(8,128)(2,1)S(1)}, u32[]{:S(2)}, u32[]{:S(2)}) collective-permute-start(bf16[6,128,128]{2,1,0:T(8,128)(2,1)S(1)} %get-tuple-element.33), channel_id=1, source_target_pairs={{1,0},{2,1},{3,2},{5,4},{6,5},{7,6},{9,8},{10,9},{11,10},{13,12},{... | collective-permute-start | bytes 589832 | tf_op jit(solution)/shard_map/ppermute | solution.py:323

commit v5 on v4

--- a/solution.py
+++ b/solution.py
@@ -83,11 +83,16 @@
     inner_steps(own_ref.shape[0], lambda row: own_ref[row], wide, mid, parts)
 
 
-def third_inner(own_ref, wide, got_ref, error_ref, begin_ref, mid, *parts):
+def second_inner(own_ref, wide, got_ref, begin_ref, mid, *parts):
     begin = lax.axis_index("depth") == 0
     for row in range(own_ref.shape[0]):
-        value = jnp.where(begin, own_ref[row], got_ref[row].astype(jnp.float32))
-        begin_ref[row] = value + error_ref[row].astype(jnp.float32)
+        begin_ref[row] = jnp.where(begin, own_ref[row], got_ref[row].astype(jnp.float32))
+    inner_steps(own_ref.shape[0], lambda row: begin_ref[row], wide, mid, parts)
+
+
+def third_inner(own_ref, wide, error_ref, begin_ref, mid, *parts):
+    for row in range(own_ref.shape[0]):
+        begin_ref[row] = own_ref[row] + error_ref[row].astype(jnp.float32)
     inner_steps(own_ref.shape[0], lambda row: begin_ref[row], wide, mid, parts)
 
 
@@ -106,7 +111,7 @@
     rows = own + 2 * halo
     for step in range(1, 2 * count + 1):
         src, dst = fields[(step - 1) % 2], fields[step % 2]
-        inside = range(halo // 2, halo // 2 + inner_pairs(own, step)) if parts else ()
+        inside = range(halo // 2, halo // 2 + inner_pairs(own, step))
 
         def hidden(pair, half, value, step=step, dst=dst):
             row = step + 2 * pair + half
@@ -142,11 +147,10 @@
     for row in range(own + 2 * halo):
         value = value_of(row)
         state[row] = value
-        if part is None or not halo <= row < halo + own:
+        if not halo <= row < halo + own:
             spread(field, row // 2, row % 2, value)
-    if part is not None:
-        for pair in range(own // 2):
-            field[halo // 2 + pair] = part[pair]
+    for pair in range(own // 2):
+        field[halo // 2 + pair] = part[pair]
 
 
 def first_kernel(own_ref, wide, top_ref, bottom_ref, mid, *refs):
@@ -170,8 +174,8 @@
     layers(halo // 2, halo, own, state, (fa, fb), wide, after_layer, mid, parts)
 
 
-def second_kernel(own_ref, wide, top_ref, bottom_ref, got_ref, got_top_ref, got_bottom_ref, y_ref,
-                  relaxed_ref, code_ref, state, fa, fb):
+def second_kernel(own_ref, wide, top_ref, bottom_ref, got_top_ref, got_bottom_ref, y_ref, mid, *refs):
+    parts, (relaxed_ref, code_ref, state, fa, fb) = refs[:-5], refs[-5:]
     own = own_ref.shape[0]
     halo = top_ref.shape[0]
     begin = lax.axis_index("depth") == 0
@@ -182,9 +186,9 @@
         if row >= halo + own:
             at = row - halo - own
             return jnp.where(begin, bottom_ref[at], got_bottom_ref[at]).astype(jnp.float32)
-        return jnp.where(begin, own_ref[row - halo], got_ref[row - halo].astype(jnp.float32))
-
-    load_rows(halo, own, value_of, state, fa, None)
+        return own_ref[row - halo]
+
+    load_rows(halo, own, value_of, state, fa, parts[0])
 
     def after_layer(done, row, new):
         if 2 * done == halo:
@@ -192,7 +196,7 @@
             resid = new - y_ref[row].astype(jnp.float32)
             code_ref[row] = encode(resid, RESID_SCALE)
 
-    layers(halo // 2, halo, own, state, (fa, fb), wide, after_layer, None, ())
+    layers(halo // 2, halo, own, state, (fa, fb), wide, after_layer, mid, parts)
 
 
 def third_kernel(own_ref, wide, top_ref, bottom_ref, got_top_ref, got_bottom_ref,
@@ -367,12 +371,13 @@
     pairs_inside = sum(inner_pairs(own, step) for step in range(1, own // 2))
     known = small(first_inner, inner, start, wide, flops=pairs_inside)
     (y_first,) = sweep(first_kernel, halo, own, (field,), (start, wide, top, bottom, *known))
+    got = from_previous(y_first, 0)
     got_top = from_previous(y_first[own - halo :], -1)
-    got = from_previous(y_first, 0)
     got_bottom = from_previous(y_first[:halo], 1)
-    before = (start, wide, top, bottom, got, got_top, got_bottom)
+    begin, *known = small(second_inner, [wide_field] + inner, start, wide, got, flops=pairs_inside)
     y_second, code = sweep(
-        second_kernel, halo, own, (wide_field, field), before + (y_first,)
+        second_kernel, halo, own, (wide_field, field),
+        (begin, wide, top, bottom, got_top, got_bottom, y_first, *known),
     )
     pairs = [[at, at + 1] for at in range(0, depth, 2)]
     alike = [list(range(core, depth, 2)) for core in range(2)]
@@ -394,7 +399,7 @@
     error_top = neighbour(lower, True)
     error_bottom = neighbour(upper, False)
     begin, *known = small(
-        third_inner, [wide_field] + inner, start, wide, got, error, flops=pairs_inside
+        third_inner, [wide_field] + inner, begin, wide, error, flops=pairs_inside
     )
     states, relaxed = sweep(
         third_kernel, near, own,

time: 100 us -> 99.8 us (level)
  waiting for transfers between devices: 9.48 us -> 7.14 us
  blocking collectives: 41.3 us -> 42.5 us
    ppermute x3, waiting for transfers between devices: 4.69 us -> 2.36 us  [from_previous(): return lax.ppermute(block, ('depth', 'space'), route)]
    pallas_call x5 -> x6, Pallas kernels: 2.97 us -> 4.25 us  [small(): pl.pallas_call(kernel, out_shape=outs, in_specs=on_chip(len(args)), out_s...]
  transfers between devices with their start and end apart: 7 -> 7, of which waited for: 4 -> 4; matrix products, arithmetic and copies ran while one was open for 0% -> 0% of each run, Pallas kernels for 4% -> 5%
where the time goes in v5:
time: 99.8 us; the launch traced here: 99.2 us
  blocking collectives  42.5 us (43%)
  Pallas kernels  23 us (23%)
  starting transfers between devices  20.9 us (21%)
  waiting for transfers between devices  7.14 us (7%)
  local copies, waits for them, and re-layouts  3.58 us (4%)
  other arithmetic  1.08 us (1%)
    all_to_all x1, blocking collectives, shards(): joined = lax.all_to_all(joined, 'depth', 0, 0, axis_index_groups=alike)  23.1 us
    pallas_call x3, Pallas kernels, sweep(): pl.pallas_call(kernel, out_shape=outs, in_specs=on_chip(len(args)), out_s...  17.6 us
    all_to_all x1, blocking collectives, shards(): errors = lax.all_to_all(errors, 'depth', 0, 0, axis_index_groups=alike)  13.9 us
    ppermute x4, starting transfers between devices, neighbour(): return lax.ppermute(block, 'space', route)  12.2 us
    ppermute x3, starting transfers between devices, from_previous(): return lax.ppermute(block, ('depth', 'space'), route)  8.72 us
    ppermute x4, waiting for transfers between devices, neighbour(): return lax.ppermute(block, 'space', route)  4.78 us
    pallas_call x6, Pallas kernels, small(): pl.pallas_call(kernel, out_shape=outs, in_specs=on_chip(len(args)), out_s...  4.25 us
    unnamed x8, local copies, waits for them, and re-layouts  3.58 us
  transfers between devices with their start and end apart: 7, of which 4 were waited for; matrix products, arithmetic and copies ran while one was open for 0% of the time, Pallas kernels for 5%

profile of v5, /device:TPU:2, one launch (start us, length us, event | category | flops | bytes accessed | tf_op | source)
XLA Modules:
  0.0 99.2 jit_solution(17776228926466324244)
XLA Ops:
  0.6 1.1 %bitcast_convert_fusion = bf16[8,128,128]{2,1,0:T(8,128)(2,1)S(1)} fusion(f32[1,8,128,128]{3,2,1,0:T(8,128)} %param.4), kind=kLoop, calls=%fused_computation | loop fusion | flops 131072 | bytes 786432 | tf_op jit(solution)/shard_map/convert_element_type | solution.py:351
  1.7 4.2 %collective-permute-start.1 = (bf16[8,128,128]{2,1,0:T(8,128)(2,1)S(1)}, bf16[8,128,128]{2,1,0:T(8,128)(2,1)S(1)}, u32[]{:S(2)}, u32[]{:S(2)}) collective-permute-start(bf16[8,128,128]{2,1,0:T(8,128)(2,1)S(1)} %bitcast_convert_fusion), channel_id=1, source_target_pairs={{1,0},{2,1},{3,2},{5,4},{6,5},{7,6},{9,8},{10,9},{11,10},{13,12},{... | collective-permute-start | bytes 786440 | tf_op jit(solution)/shard_map/ppermute | solution.py:327
  5.9 1.9 %collective-permute-start = (bf16[8,128,128]{2,1,0:T(8,128)(2,1)S(1)}, bf16[8,128,128]{2,1,0:T(8,128)(2,1)S(1)}, u32[]{:S(2)}, u32[]{:S(2)}) collective-permute-start(bf16[8,128,128]{2,1,0:T(8,128)(2,1)S(1)} %bitcast_convert_fusion), channel_id=1, source_target_pairs={{0,1},{1,2},{2,3},{4,5},{5,6},{6,7},{8,9},{9,10},{10,11},{12,13},{... | collective-permute-start | bytes 786440 | tf_op jit(solution)/shard_map/ppermute | solution.py:327
  7.8 0.0 copy-start
  7.8 1.0 %copy-done = f32[1,8,128,128]{3,2,1,0:T(8,128)S(1)} copy-done((f32[1,8,128,128]{3,2,1,0:T(8,128)S(1)}, f32[1,8,128,128]{3,2,1,0:T(8,128)}, u32[]{:S(2)}) %copy-start) | copy-done | bytes 524312
  8.9 0.0 copy-start.1
  8.9 1.3 %copy-done.1 = bf16[4,9,128,128]{3,2,1,0:T(8,128)(2,1)S(1)} copy-done((bf16[4,9,128,128]{3,2,1,0:T(8,128)(2,1)S(1)}, bf16[4,9,128,128]{3,2,1,0:T(8,128)(2,1)}, u32[]{:S(2)}) %copy-start.1) | copy-done | bytes 1179672
  10.1 0.0 copy-start.2
  10.2 1.3 %copy-done.2 = bf16[4,9,128,128]{3,2,1,0:T(8,128)(2,1)S(1)} copy-done((bf16[4,9,128,128]{3,2,1,0:T(8,128)(2,1)S(1)}, bf16[4,9,128,128]{3,2,1,0:T(8,128)(2,1)}, u32[]{:S(2)}) %copy-start.2) | copy-done | bytes 1179672
  11.4 1.2 %shard_map.59 = (f32[8,128,128]{2,1,0:T(8,128)S(1)}, bf16[8,1536,256]{2,1,0:T(8,128)(2,1)S(1)}) custom-call(f32[8,128,128]{2,1,0:T(8,128)S(1)} %bitcast.11, bf16[4,1152,128]{2,1,0:T(8,128)(2,1)S(1)} %bitcast.12, bf16[4,1152,128]{2,1,0:T(8,128)(2,1)S(1)} %bitcast.13), custom_call_target="tpu_custom_call" | custom-call | bytes 16777216 | tf_op jit(solution)/shard_map/pallas_call | solution.py:354
  12.7 1.3 %shard_map.60 = (f32[4,128,128]{2,1,0:T(8,128)S(1)}, bf16[4,128,768]{2,1,0:T(8,128)(2,1)S(1)}, bf16[3,128,768]{2,1,0:T(8,128)(2,1)S(1)}, bf16[2,128,768]{2,1,0:T(8,128)(2,1)S(1)}, bf16[1,128,768]{2,1,0:T(8,128)(2,1)S(1)}) custom-call(f32[8,128,128]{2,1,0:T(8,128)S(1)} %get-tuple-element.28.own_ref, bf16[8,1536,256]{2,1,0:T(8,128)(2,1)S(1)} %get-tuple-element.29.wide), custom_call_target="tpu_custom_call" | custom-call | flops 452984832 | bytes 524288 | tf_op jit(solution)/shard_map/pallas_call | solution.py:285
  14.0 0.0 collective-permute-done.1.bottom_ref
  14.0 0.2 collective-permute-done.top_ref
  14.2 6.3 %shard_map.61.y_ref = bf16[8,128,128]{2,1,0:T(8,128)(2,1)S(1)} custom-call(f32[8,128,128]{2,1,0:T(8,128)S(1)} %get-tuple-element.28.own_ref, bf16[8,1536,256]{2,1,0:T(8,128)(2,1)S(1)} %get-tuple-element.29.wide, bf16[8,128,128]{2,1,0:T(8,128)(2,1)S(1)} %collective-permute-done.top_ref, bf16[8,128,128]{2,1,0:T(8,128)(2,1)S(1)} %collective-permute-done.1.bottom_ref, ...), custom_call_target="tpu_custom_call" | custom-call | flops 4529848320 | bytes 4194304 | tf_op jit(solution)/shard_map/pallas_call | solution.py:313
  20.5 1.3 %collective-permute-start.2 = (bf16[8,128,128]{2,1,0:T(8,128)(2,1)S(1)}, bf16[8,128,128]{2,1,0:T(8,128)(2,1)S(1)}, u32[]{:S(2)}, u32[]{:S(2)}) collective-permute-start(bf16[8,128,128]{2,1,0:T(8,128)(2,1)S(1)} %shard_map.61.y_ref), channel_id=1, source_target_pairs={{0,4},{1,5},{2,6},{3,7},{4,8},{5,9},{6,10},{7,11},{8,12},{9,13},{1... | collective-permute-start | bytes 786440 | tf_op jit(solution)/shard_map/ppermute | solution.py:338
  21.8 4.3 %collective-permute-start.4 = (bf16[8,128,128]{2,1,0:T(8,128)(2,1)S(1)}, bf16[8,128,128]{2,1,0:T(8,128)(2,1)S(1)}, u32[]{:S(2)}, u32[]{:S(2)}) collective-permute-start(bf16[8,128,128]{2,1,0:T(8,128)(2,1)S(1)} %shard_map.61.y_ref), channel_id=1, source_target_pairs={{1,4},{2,5},{3,6},{5,8},{6,9},{7,10},{9,12},{10,13},{11,14},{13,16... | collective-permute-start | bytes 786440 | tf_op jit(solution)/shard_map/ppermute | solution.py:338
  26.0 3.1 %collective-permute-start.3 = (bf16[8,128,128]{2,1,0:T(8,128)(2,1)S(1)}, bf16[8,128,128]{2,1,0:T(8,128)(2,1)S(1)}, u32[]{:S(2)}, u32[]{:S(2)}) collective-permute-start(bf16[8,128,128]{2,1,0:T(8,128)(2,1)S(1)} %shard_map.61.y_ref), channel_id=1, source_target_pairs={{0,5},{1,6},{2,7},{4,9},{5,10},{6,11},{8,13},{9,14},{10,15},{12,17... | collective-permute-start | bytes 786440 | tf_op jit(solution)/shard_map/ppermute | solution.py:338
  29.2 0.0 collective-permute-done.2.got_ref
  29.2 1.3 %shard_map.62 = (f32[8,128,128]{2,1,0:T(8,128)S(1)}, f32[4,128,128]{2,1,0:T(8,128)S(1)}, bf16[4,128,768]{2,1,0:T(8,128)(2,1)S(1)}, bf16[3,128,768]{2,1,0:T(8,128...) custom-call(f32[8,128,128]{2,1,0:T(8,128)S(1)} %get-tuple-element.28.own_ref, ...), custom_call_target="tpu_custom_call" | custom-call | flops 452984832 | bytes 524288 | tf_op jit(solution)/shard_map/pallas_call | solution.py:285
  30.5 0.0 collective-permute-done.4.got_bottom_ref
  30.5 2.4 %collective-permute-done.3.got_top_ref = bf16[8,128,128]{2,1,0:T(8,128)(2,1)S(1)} collective-permute-done((bf16[8,128,128]{2,1,0:T(8,128)(2,1)S(1)}, bf16[8,128,128]{2,1,0:T(8,128)(2,1)S(1)}, u32[]{:S(2)}, u32[]{:S(2)}) %collective-permute-start.3) | collective-permute-done | bytes 262176 | tf_op jit(solution)/shard_map/ppermute | solution.py:338
  32.9 0.0 copy-start.3
  32.9 6.3 %shard_map.63 = (f32[8,128,128]{2,1,0:T(8,128)S(1)}, bf16[8,128,128]{2,1,0:T(8,128)(2,1)S(1)}) custom-call(f32[8,128,128]{2,1,0:T(8,128)S(1)} %get-tuple-element.35.own_ref, bf16[8,1536,256]{2,1,0:T(8,128)(2,1)S(1)} %get-tuple-element.29.wide, bf16[8,128,128]{2,1,0:T(8,128)(2,1)S(1)} %collective-permute-done.top_ref, ...), custom_call_target="tpu_custom_call" | custom-call | flops 4529848320 | bytes 4194304 | tf_op jit(solution)/shard_map/pallas_call | solution.py:313
  39.2 3.5 %all-gather = bf16[16,128,128]{2,1,0:T(8,128)(2,1)S(1)} all-gather(bf16[8,128,128]{2,1,0:T(8,128)(2,1)S(1)} %get-tuple-element.41), channel_id=2, replica_groups={{0,4},{8,12},{16,20},{24,28},{32,36},{40,44},{48,52},{56,60},{64,68},{7..., dimensions={0}, use_global_device_ids=true | all-gather | bytes 786432 | tf_op jit(solution)/shard_map/all_gather | solution.py:384
  42.7 0.0 copy-done.3
  42.7 0.1 shard_map.64
  42.9 23.1 %all_to_all.10.joined_ref = bf16[32,16,128]{2,1,0:T(8,128)(2,1)S(1)} all-to-all(bf16[32,16,128]{2,1,0:T(8,128)(2,1)S(1)} %bitcast.15), channel_id=1, replica_groups={{0,8,16,24,32,40,48,56,64,72,80,88,96,104,112,120,128,136,144,152,160,1..., dimensions={0} | all-to-all | bytes 262144 | tf_op jit(solution)/shard_map/all_to_all | solution.py:388
  66.0 0.1 shard_map.65
  66.1 13.9 %all_to_all.11 = bf16[32,16,128]{2,1,0:T(8,128)(2,1)S(1)} all-to-all(bf16[32,16,128]{2,1,0:T(8,128)(2,1)S(1)} %shard_map.65), channel_id=1, replica_groups={{0,8,16,24,32,40,48,56,64,72,80,88,96,104,112,120,128,136,144,152,160,1..., dimensions={0} | all-to-all | bytes 262144 | tf_op jit(solution)/shard_map/all_to_all | solution.py:392
  80.0 2.0 %all_gather.11 = bf16[2,4,128,128]{3,2,1,0:T(8,128)(2,1)S(1)} all-gather(bf16[1,4,128,128]{3,2,1,0:T(8,128)(2,1)S(1)} %bitcast.16), channel_id=1, replica_groups={{0,4},{8,12},{16,20},{24,28},{32,36},{40,44},{48,52},{56,60},{64,68},{7..., dimensions={0}, use_global_device_ids=true | all-gather | bytes 393216 | tf_op jit(solution)/shard_map/all_gather | solution.py:393
  82.0 0.2 shard_map.66
  82.1 3.4 %collective-permute-start.5 = (bf16[6,128,128]{2,1,0:T(8,128)(2,1)S(1)}, bf16[6,128,128]{2,1,0:T(8,128)(2,1)S(1)}, u32[]{:S(2)}, u32[]{:S(2)}) collective-permute-start(bf16[6,128,128]{2,1,0:T(8,128)(2,1)S(1)} %get-tuple-element.44), channel_id=1, source_target_pairs={{0,1},{1,2},{2,3},{4,5},{5,6},{6,7},{8,9},{9,10},{10,11},{12,13},{... | collective-permute-start | bytes 589832 | tf_op jit(solution)/shard_map/ppermute | solution.py:327
  85.5 2.7 %collective-permute-start.6 = (bf16[6,128,128]{2,1,0:T(8,128)(2,1)S(1)}, bf16[6,128,128]{2,1,0:T(8,128)(2,1)S(1)}, u32[]{:S(2)}, u32[]{:S(2)}) collective-permute-start(bf16[6,128,128]{2,1,0:T(8,128)(2,1)S(1)} %get-tuple-element.45), channel_id=1, source_target_pairs={{1,0},{2,1},{3,2},{5,4},{6,5},{7,6},{9,8},{10,9},{11,10},{13,12},{... | collective-permute-start | bytes 589832 | tf_op jit(solution)/shard_map/ppermute | solution.py:327
  88.2 1.3 %shard_map.67 = (f32[8,128,128]{2,1,0:T(8,128)S(1)}, f32[4,128,128]{2,1,0:T(8,128)S(1)}, bf16[4,128,768]{2,1,0:T(8,128)(2,1)S(1)}, bf16[3,128,768]{2,1,0:T(8,128...) custom-call(f32[8,128,128]{2,1,0:T(8,128)S(1)} %get-tuple-element.35.own_ref, ...), custom_call_target="tpu_custom_call" | custom-call | flops 452984832 | bytes 524288 | tf_op jit(solution)/shard_map/pallas_call | solution.py:285
  89.5 1.5 %collective-permute-done.5.error_top_ref = bf16[6,128,128]{2,1,0:T(8,128)(2,1)S(1)} collective-permute-done((bf16[6,128,128]{2,1,0:T(8,128)(2,1)S(1)}, bf16[6,128,128]{2,1,0:T(8,128)(2,1)S(1)}, u32[]{:S(2)}, u32[]{:S(2)}) %collective-permute-start.5) | collective-permute-done | bytes 196640 | tf_op jit(solution)/shard_map/ppermute | solution.py:327
  91.0 3.1 %collective-permute-done.6.error_bottom_ref = bf16[6,128,128]{2,1,0:T(8,128)(2,1)S(1)} collective-permute-done((bf16[6,128,128]{2,1,0:T(8,128)(2,1)S(1)}, bf16[6,128,128]{2,1,0:T(8,128)(2,1)S(1)}, u32[]{:S(2)}, u32[]{:S(2)}) %collective-permute-start.6) | collective-permute-done | bytes 196640 | tf_op jit(solution)/shard_map/ppermute | solution.py:327
  94.1 4.9 %shard_map.68 = (f32[4,8,128,128]{3,2,1,0:T(8,128)}, f32[8,128,128]{2,1,0:T(8,128)}) custom-call(f32[8,128,128]{2,1,0:T(8,128)S(1)} %get-tuple-element.43.own_ref, bf16[8,1536,256]{2,1,0:T(8,128)(2,1)S(1)} %get-tuple-element.29.wide, bf16[8,128,128]{2,1,0:T(8,128)(2,1)S(1)} %collective-permute-done.top_ref, ...), custom_call_target="tpu_custom_call" | custom-call | flops 2944401408 | bytes 4194304 | tf_op jit(solution)/shard_map/pallas_call | solution.py:313
Async XLA Ops:
  1.7 12.3 %collective-permute-start.1 = (bf16[8,128,128]{2,1,0:T(8,128)(2,1)S(1)}, bf16[8,128,128]{2,1,0:T(8,128)(2,1)S(1)}, u32[]{:S(2)}, u32[]{:S(2)}) collective-permute-start(bf16[8,128,128]{2,1,0:T(8,128)(2,1)S(1)} %bitcast_convert_fusion), channel_id=1, source_target_pairs={{1,0},{2,1},{3,2},{5,4},{6,5},{7,6},{9,8},{10,9},{11,10},{13,12},{... | collective-permute-start | bytes 786440 | tf_op jit(solution)/shard_map/ppermute | solution.py:327
  5.9 8.3 %collective-permute-start = (bf16[8,128,128]{2,1,0:T(8,128)(2,1)S(1)}, bf16[8,128,128]{2,1,0:T(8,128)(2,1)S(1)}, u32[]{:S(2)}, u32[]{:S(2)}) collective-permute-start(bf16[8,128,128]{2,1,0:T(8,128)(2,1)S(1)} %bitcast_convert_fusion), channel_id=1, source_target_pairs={{0,1},{1,2},{2,3},{4,5},{5,6},{6,7},{8,9},{9,10},{10,11},{12,13},{... | collective-permute-start | bytes 786440 | tf_op jit(solution)/shard_map/ppermute | solution.py:327
  7.8 1.0 %copy-start = (f32[1,8,128,128]{3,2,1,0:T(8,128)S(1)}, f32[1,8,128,128]{3,2,1,0:T(8,128)}, u32[]{:S(2)}) copy-start(f32[1,8,128,128]{3,2,1,0:T(8,128)} %param.4) | copy-start | bytes 1572868
  8.9 1.3 %copy-start.1 = (bf16[4,9,128,128]{3,2,1,0:T(8,128)(2,1)S(1)}, bf16[4,9,128,128]{3,2,1,0:T(8,128)(2,1)}, u32[]{:S(2)}) copy-start(bf16[4,9,128,128]{3,2,1,0:T(8,128)(2,1)} %param.5) | copy-start | bytes 3538948
  10.1 1.3 %copy-start.2 = (bf16[4,9,128,128]{3,2,1,0:T(8,128)(2,1)S(1)}, bf16[4,9,128,128]{3,2,1,0:T(8,128)(2,1)}, u32[]{:S(2)}) copy-start(bf16[4,9,128,128]{3,2,1,0:T(8,128)(2,1)} %param.6) | copy-start | bytes 3538948
  20.5 8.7 %collective-permute-start.2 = (bf16[8,128,128]{2,1,0:T(8,128)(2,1)S(1)}, bf16[8,128,128]{2,1,0:T(8,128)(2,1)S(1)}, u32[]{:S(2)}, u32[]{:S(2)}) collective-permute-start(bf16[8,128,128]{2,1,0:T(8,128)(2,1)S(1)} %shard_map.61.y_ref), channel_id=1, source_target_pairs={{0,4},{1,5},{2,6},{3,7},{4,8},{5,9},{6,10},{7,11},{8,12},{9,13},{1... | collective-permute-start | bytes 786440 | tf_op jit(solution)/shard_map/ppermute | solution.py:338
  21.8 8.7 %collective-permute-start.4 = (bf16[8,128,128]{2,1,0:T(8,128)(2,1)S(1)}, bf16[8,128,128]{2,1,0:T(8,128)(2,1)S(1)}, u32[]{:S(2)}, u32[]{:S(2)}) collective-permute-start(bf16[8,128,128]{2,1,0:T(8,128)(2,1)S(1)} %shard_map.61.y_ref), channel_id=1, source_target_pairs={{1,4},{2,5},{3,6},{5,8},{6,9},{7,10},{9,12},{10,13},{11,14},{13,16... | collective-permute-start | bytes 786440 | tf_op jit(solution)/shard_map/ppermute | solution.py:338
  26.0 6.8 %collective-permute-start.3 = (bf16[8,128,128]{2,1,0:T(8,128)(2,1)S(1)}, bf16[8,128,128]{2,1,0:T(8,128)(2,1)S(1)}, u32[]{:S(2)}, u32[]{:S(2)}) collective-permute-start(bf16[8,128,128]{2,1,0:T(8,128)(2,1)S(1)} %shard_map.61.y_ref), channel_id=1, source_target_pairs={{0,5},{1,6},{2,7},{4,9},{5,10},{6,11},{8,13},{9,14},{10,15},{12,17... | collective-permute-start | bytes 786440 | tf_op jit(solution)/shard_map/ppermute | solution.py:338
  32.9 9.8 %copy-start.3 = (f32[64,128]{1,0:T(8,128)S(1)}, f32[64,128]{1,0:T(8,128)}, u32[]{:S(2)}) copy-start(f32[64,128]{1,0:T(8,128)} %gain_ref.5) | copy-start | bytes 98308
  82.1 8.8 %collective-permute-start.5 = (bf16[6,128,128]{2,1,0:T(8,128)(2,1)S(1)}, bf16[6,128,128]{2,1,0:T(8,128)(2,1)S(1)}, u32[]{:S(2)}, u32[]{:S(2)}) collective-permute-start(bf16[6,128,128]{2,1,0:T(8,128)(2,1)S(1)} %get-tuple-element.44), channel_id=1, source_target_pairs={{0,1},{1,2},{2,3},{4,5},{5,6},{6,7},{8,9},{9,10},{10,11},{12,13},{... | collective-permute-start | bytes 589832 | tf_op jit(solution)/shard_map/ppermute | solution.py:327
  85.5 8.6 %collective-permute-start.6 = (bf16[6,128,128]{2,1,0:T(8,128)(2,1)S(1)}, bf16[6,128,128]{2,1,0:T(8,128)(2,1)S(1)}, u32[]{:S(2)}, u32[]{:S(2)}) collective-permute-start(bf16[6,128,128]{2,1,0:T(8,128)(2,1)S(1)} %get-tuple-element.45), channel_id=1, source_target_pairs={{1,0},{2,1},{3,2},{5,4},{6,5},{7,6},{9,8},{10,9},{11,10},{13,12},{... | collective-permute-start | bytes 589832 | tf_op jit(solution)/shard_map/ppermute | solution.py:327
